TPU v7x, 32 devices: a whole 2x2x4 slice. The times are simulated.
32 devices in a mesh: dp: 4 (over y, x), expert: 8 (over z, core).
Axes of the slice: x: 2, y: 2, z: 4, core: 2. Of those that a mesh axis runs over, the one named last changes fastest.
Arguments:
- tokens: bfloat16 [4096, 2048], P(('dp', 'expert')), may hold values from -6 to 6
- cotangent: bfloat16 [4096, 2048], P(('dp', 'expert')), may hold values from -3 to 3
- routes: int32 [4096, 1], P(('dp', 'expert')), may hold values from 0 to 7, as said below
- gate_fixed: int32 [4096, 1], P(('dp', 'expert')), may hold values from 8192 to 65535
- w_gate: bfloat16 [8, 2048, 768], P('expert', 'dp'), may hold values from -0.125 to 0.125
- w_up: bfloat16 [8, 2048, 768], P('expert', 'dp'), may hold values from -0.125 to 0.125
- w_down: bfloat16 [8, 768, 2048], P('expert', None, 'dp'), may hold values from -0.21875 to 0.21875
Outputs:
- mixed: bfloat16 [4096, 2048], P(('dp', 'expert'))
- grad_tokens: bfloat16 [4096, 2048], P(('dp', 'expert'))
- grad_w_gate: bfloat16 [8, 2048, 768], P('expert', 'dp')
- grad_w_up: bfloat16 [8, 2048, 768], P('expert', 'dp')
- grad_w_down: bfloat16 [8, 768, 2048], P('expert', None, 'dp')
Inputs may be any that keep to these rules, and one draw needn't show every extreme that they name: `routes`: each token names one expert. Among the tokens of one device no expert is named more than 24 times, and some experts are named exactly 24 times by the tokens of every device.
All inputs are finite; a program needn't handle non-finite values.
Results may differ from a plain program's by a relative error of at most 0.0058.
Values may be sent and summed in bfloat16 or wider, within the bound.
No kernel may reach another device: no remote copies, remote signals or barrier semaphores. Data moves between devices by JAX's collectives and lax.ppermute only.
A program may use at most 64 MiB of HBM per device.

v0:
```python
import jax
import jax.numpy as jnp
from jax import lax
from jax.sharding import PartitionSpec as P


def swap_experts(buffer):
    return lax.all_to_all(buffer, "expert", split_axis=1, concat_axis=1, tiled=True)


def contract_last(left_side, right_side):
    return lax.dot_general(
        left_side, right_side, (((1,), (1,)), ((), ())), preferred_element_type=jnp.float32
    )


def contract_first(left_side, right_side):
    return lax.dot_general(
        left_side, right_side, (((0,), (0,)), ((), ())), preferred_element_type=jnp.float32
    )


def gate_gradients(grad_hidden, gate_pre, up_pre):
    sigmoid_gate = jax.nn.sigmoid(gate_pre)
    grad_gate = grad_hidden * up_pre * sigmoid_gate * (1.0 + gate_pre * (1.0 - sigmoid_gate))
    grad_up = grad_hidden * gate_pre * sigmoid_gate
    return jnp.concatenate([grad_gate, grad_up], axis=1).astype(jnp.bfloat16)


def full_width_pass(outgoing, grad_outgoing, gate_up_w, down_all, shape_out):
    expert_count, capacity, model_width = shape_out
    own_rows = expert_count * capacity
    hidden_width = down_all.shape[0]
    received = swap_experts(outgoing)
    flat_received = received.reshape(own_rows, model_width)
    gate_up = jnp.dot(flat_received, gate_up_w, preferred_element_type=jnp.float32)
    gate_pre = gate_up[:, :hidden_width]
    up_pre = gate_up[:, hidden_width:]
    hidden = (gate_pre * jax.nn.sigmoid(gate_pre) * up_pre).astype(jnp.bfloat16)
    slot_out = jnp.dot(hidden, down_all, preferred_element_type=jnp.float32).astype(jnp.bfloat16)
    returned = swap_experts(slot_out.reshape(1, expert_count, capacity, model_width)).reshape(
        own_rows, model_width
    )
    grad_received = swap_experts(grad_outgoing)
    grad_hidden = contract_last(grad_received.reshape(own_rows, model_width), down_all)
    grad_gate_up = gate_gradients(grad_hidden, gate_pre, up_pre)
    slot_grad_in = contract_last(grad_gate_up, gate_up_w).astype(jnp.bfloat16)
    grad_returned = swap_experts(
        slot_grad_in.reshape(1, expert_count, capacity, model_width)
    ).reshape(own_rows, model_width)
    return (received, grad_received, hidden, grad_gate_up, returned, grad_returned)


def body(tokens, cotangent, routes, gate_fixed, w_gate, w_up, w_down):
    tok_count = tokens.shape[0]
    model_width = tokens.shape[1]
    route_count = routes.shape[1]
    hidden_width = w_gate.shape[2]
    expert_count = lax.axis_size("expert")
    capacity = 3 * tok_count * route_count // (2 * expert_count)
    own_rows = expert_count * capacity
    flat_total = tok_count * route_count
    route_weight = gate_fixed.astype(jnp.float32) / 65536.0
    flat_routes = routes.reshape(flat_total)
    one_hot = (flat_routes[:, None] == jnp.arange(expert_count, dtype=jnp.int32)[None, :]).astype(
        jnp.int32
    )
    position = jnp.sum((jnp.cumsum(one_hot, axis=0) - one_hot) * one_hot, axis=1)
    slot_index = flat_routes * capacity + position
    matches = slot_index[None, :] == jnp.arange(own_rows, dtype=jnp.int32)[:, None]
    occupied = jnp.any(matches, axis=1)
    source_row = jnp.sum(
        jnp.where(matches, jnp.arange(flat_total, dtype=jnp.int32)[None, :], 0), axis=1
    )
    slot_weight = jnp.sum(
        jnp.where(matches, route_weight.reshape(flat_total)[None, :], 0.0), axis=1
    )
    token_row = source_row // route_count
    outgoing = jnp.where(
        occupied[:, None], jnp.take(tokens, token_row, axis=0), jnp.zeros((), tokens.dtype)
    )
    outgoing = outgoing.reshape(1, expert_count, capacity, model_width)
    scaled = (
        slot_weight[:, None] * jnp.take(cotangent, token_row, axis=0).astype(jnp.float32)
    ).astype(jnp.bfloat16)
    grad_outgoing = jnp.where(occupied[:, None], scaled, jnp.zeros((), scaled.dtype))
    grad_outgoing = grad_outgoing.reshape(1, expert_count, capacity, model_width)
    shape_out = (expert_count, capacity, model_width)
    replicas = lax.axis_size("dp")
    part_width = model_width // replicas
    gate_all, up_all, down_all = (
        lax.all_gather(w_gate[0], "dp", axis=0, tiled=True),
        lax.all_gather(w_up[0], "dp", axis=0, tiled=True),
        lax.all_gather(w_down[0], "dp", axis=1, tiled=True),
    )
    gate_up_w = jnp.concatenate([gate_all, up_all], axis=1)
    received, grad_received, hidden, grad_gate_up, returned, grad_returned = full_width_pass(
        outgoing, grad_outgoing, gate_up_w, down_all, shape_out
    )
    slot_cols, grad_cols = (
        lax.all_to_all(received, "dp", split_axis=3, concat_axis=0, tiled=True),
        lax.all_to_all(grad_received, "dp", split_axis=3, concat_axis=0, tiled=True),
    )
    hidden_all, grad_gate_up_all = (
        lax.all_gather(hidden, "dp", axis=0, tiled=True),
        lax.all_gather(grad_gate_up, "dp", axis=0, tiled=True),
    )
    slot_cols = slot_cols.reshape(replicas * own_rows, part_width)
    grad_cols = grad_cols.reshape(replicas * own_rows, part_width)
    gate_up_grad = contract_first(slot_cols, grad_gate_up_all)
    down_grad = contract_first(hidden_all, grad_cols)
    picked = (
        jnp.take(returned, slot_index, axis=0)
        .reshape(tok_count, route_count, model_width)
        .astype(jnp.float32)
    )
    mixed = jnp.sum(route_weight[:, :, None] * picked, axis=1).astype(jnp.bfloat16)
    grad_picked = (
        jnp.take(grad_returned, slot_index, axis=0)
        .reshape(tok_count, route_count, model_width)
        .astype(jnp.float32)
    )
    grad_tokens = jnp.sum(grad_picked, axis=1).astype(jnp.bfloat16)
    grad_w_gate = gate_up_grad[:, :hidden_width].astype(jnp.bfloat16)[None]
    grad_w_up = gate_up_grad[:, hidden_width:].astype(jnp.bfloat16)[None]
    grad_w_down = down_grad.astype(jnp.bfloat16)[None]
    return (mixed, grad_tokens, grad_w_gate, grad_w_up, grad_w_down)


def solution(mesh):
    return jax.shard_map(
        body,
        mesh=mesh,
        in_specs=(
            P(("dp", "expert"), None),
            P(("dp", "expert"), None),
            P(("dp", "expert"), None),
            P(("dp", "expert"), None),
            P("expert", "dp", None),
            P("expert", "dp", None),
            P("expert", None, "dp"),
        ),
        out_specs=(
            P(("dp", "expert"), None),
            P(("dp", "expert"), None),
            P("expert", "dp", None),
            P("expert", "dp", None),
            P("expert", None, "dp"),
        ),
        check_vma=False,
    )
```

profile of v0, /device:TPU:19, one launch (start us, length us, event | category | flops | bytes accessed | tf_op | source)
XLA Modules:
  0.0 270.6 jit_solution(8451315099808107304)
XLA Ops:
  7.2 0.7 all-gather.15.cloned.1.call-update
  8.0 0.7 all-gather.13.cloned.1.call-update
  8.7 0.7 all-gather.17.cloned.1.call-update
  9.4 0.7 fusion.13
  10.1 0.2 reduce_window_sum.11
  10.3 0.8 select_reduce_fusion.2
  11.1 0.7 compare_and_fusion
  11.8 0.1 select_reduce_fusion.1
  12.0 1.1 gather_fusion.2
  13.2 1.1 gather_fusion
  14.3 0.1 fusion.12
  14.4 0.1 select_reduce_fusion
  14.6 1.3 fusion.11
  15.8 22.4 %all_to_all.50 = bf16[1,8,24,2048]{3,2,0,1:T(8,128)(2,1)S(1)} all-to-all(bf16[1,8,24,2048]{3,2,0,1:T(8,128)(2,1)S(1)} %bitcast.66), channel_id=1, replica_groups=mesh['dp'=4,'expert'=8] {'expert'}, dimensions={1} | all-to-all | bytes 1572864 | tf_op jit(solution)/shard_map/all_to_all | solution.py:8
  38.2 7.4 %all-to-all-start.2 = ((bf16[1,8,24,2048]{3,2,0,1:T(8,128)(2,1)}), bf16[1,8,24,2048]{3,2,0,1:T(8,128)(2,1)S(1)}, u32[]{:S(2)}, u32[]{:S(2)}) async-start(bf16[1,8,24,2048]{3,2,0,1:T(8,128)(2,1)} %bitcast.12), calls=%async_computation.2 | async-start | bytes 1572864 | tf_op jit(solution)/shard_map/all_to_all | solution.py:8
  45.6 9.3 %all-gather.15.cloned.1.call-done = bf16[1,2048,768]{2,1,0:T(8,128)(2,1)} async-done(((bf16[1,512,768]{2,1,0:T(8,128)(2,1)}), bf16[1,2048,768]{2,1,0:T(8,128)(2,1)}) %all-gather.15.cloned.1.call-update) | async-done | bytes 3145744 | tf_op jit(solution)/shard_map/all_gather | solution.py:93
  54.9 45.8 %all-gather.13.cloned.1.call-done = bf16[1,2048,768]{2,1,0:T(8,128)(2,1)} async-done(((bf16[1,512,768]{2,1,0:T(8,128)(2,1)}), bf16[1,2048,768]{2,1,0:T(8,128)(2,1)}) %all-gather.13.cloned.1.call-update) | async-done | bytes 3145744 | tf_op jit(solution)/shard_map/all_gather | solution.py:92
  100.8 5.3 %fusion.1 = f32[192,1536]{1,0:T(8,128)} fusion(bf16[192,2048]{1,0:T(8,128)(2,1)S(1)} %bitcast.62, bf16[2048,768]{1,0:T(8,128)(2,1)} %bitcast.71, bf16[2048,768]{1,0:T(8,128)(2,1)} %bitcast.73), kind=kOutput, calls=%fused_computation.6 | convolution fusion | flops 1220542464 | bytes 8257536 | tf_op jit(solution)/shard_map/dot_general | solution.py:36
  106.0 40.4 %all-gather.17.cloned.1.call-done = bf16[1,768,2048]{2,1,0:T(8,128)(2,1)} async-done(((bf16[1,768,512]{2,1,0:T(8,128)(2,1)}), bf16[1,768,2048]{2,1,0:T(8,128)(2,1)}) %all-gather.17.cloned.1.call-update) | async-done | bytes 3145744 | tf_op jit(solution)/shard_map/all_gather | solution.py:94
  146.4 4.4 %multiply_convert_fusion.3 = (bf16[192,768]{1,0:T(8,128)(2,1)}, bf16[192,768]{1,0:T(8,128)(2,1)}, bf16[192,768]{1,0:T(8,128)(2,1)}) fusion(f32[192,1536]{1,0:T(8,128)} %fusion.1, bf16[192,2048]{1,0:T(8,128)(2,1)S(1)} %bitcast.61, bf16[1,768,2048]{2,1,0:T(8,128)(2,1)} %all-gather.17.cloned.1.call-done), kind=kOutput, calls=%fused_computation.24 | convolution fusion | flops 606339072 | bytes 5996544 | tf_op jit(solution)/shard_map/dot_general | solution.py:12
  150.9 4.2 %copy.28 = bf16[1,8,24,2048]{2,1,0,3:T(8,128)(2,1)} copy(bf16[1,8,24,2048]{3,2,0,1:T(8,128)(2,1)S(1)} %all_to_all.50) | data formatting | bytes 1572864 | tf_op jit(solution)/shard_map/all_to_all | solution.py:8
  155.1 7.3 %reshape.136 = bf16[4,2,49152]{2,1,0:T(2,128)(2,1)} reshape(bf16[2048,1,8,24]{3,2,1,0:T(8,128)(2,1)} %bitcast.57) | data formatting | bytes 1572864
  162.3 3.8 %all-to-all-start.4 = ((bf16[4,2,49152]{2,1,0:T(2,128)(2,1)}), bf16[4,2,49152]{2,1,0:T(2,128)(2,1)S(1)}, u32[]{:S(2)}, u32[]{:S(2)}) async-start(bf16[4,2,49152]{2,1,0:T(2,128)(2,1)} %reshape.136), calls=%async_computation.4 | async-start | bytes 1572864 | tf_op jit(solution)/shard_map/all_to_all | solution.py:101
  166.1 4.2 %copy.31 = bf16[1,8,24,2048]{2,1,0,3:T(8,128)(2,1)} copy(bf16[1,8,24,2048]{3,2,0,1:T(8,128)(2,1)S(1)} %all-to-all-done.2) | data formatting | bytes 1572864 | tf_op jit(solution)/shard_map/all_to_all | solution.py:8
  170.3 7.4 %reshape.138 = bf16[4,2,49152]{2,1,0:T(2,128)(2,1)} reshape(bf16[2048,1,8,24]{3,2,1,0:T(8,128)(2,1)} %bitcast.58) | data formatting | bytes 1572864
  177.7 1.8 all-to-all-done.4
  179.5 4.0 %all-to-all-start.5 = ((bf16[4,2,49152]{2,1,0:T(2,128)(2,1)}), bf16[4,2,49152]{2,1,0:T(2,128)(2,1)S(1)}, u32[]{:S(2)}, u32[]{:S(2)}) async-start(bf16[4,2,49152]{2,1,0:T(2,128)(2,1)} %reshape.138), calls=%async_computation.5 | async-start | bytes 1572864 | tf_op jit(solution)/shard_map/all_to_all | solution.py:102
  183.5 3.6 %fusion.6 = bf16[192,2048]{1,0:T(8,128)(2,1)} fusion(bf16[192,768]{1,0:T(8,128)(2,1)S(1)} %copy-done.5, bf16[1,768,2048]{2,1,0:T(8,128)(2,1)} %all-gather.17.cloned.1.call-done), kind=kOutput, calls=%fused_computation.12 | convolution fusion | flops 604372992 | bytes 4227072 | tf_op jit(solution)/shard_map/dot_general | solution.py:40
  187.2 3.0 %all-to-all-done.5 = bf16[4,2,49152]{2,1,0:T(2,128)(2,1)S(1)} async-done(((bf16[4,2,49152]{2,1,0:T(2,128)(2,1)}), bf16[4,2,49152]{2,1,0:T(2,128)(2,1)S(1)}, u32[]{:S(2)}, u32[]{:S(2)}) %all-to-all-start.5) | async-done | bytes 786464 | tf_op jit(solution)/shard_map/all_to_all | solution.py:102
  190.2 0.9 copy-done.2
  191.0 9.6 %all-to-all-start.1 = ((bf16[1,8,24,2048]{3,2,0,1:T(8,128)(2,1)}), bf16[1,8,24,2048]{3,2,0,1:T(8,128)(2,1)S(1)}, u32[]{:S(2)}, u32[]{:S(2)}) async-start(bf16[1,8,24,2048]{3,2,0,1:T(8,128)(2,1)} %bitcast.9), calls=%async_computation.1 | async-start | bytes 1572864 | tf_op jit(solution)/shard_map/all_to_all | solution.py:8
  200.7 0.9 pad_maximum_fusion.5
  201.6 5.9 %fusion.9 = bf16[192,2048]{1,0:T(8,128)(2,1)} fusion(bf16[2048,768]{1,0:T(8,128)(2,1)} %bitcast.72, bf16[2048,768]{1,0:T(8,128)(2,1)} %bitcast.74, bf16[192,768]{1,0:T(8,128)(2,1)S(1)} %copy-done.7, bf16[192,768]{1,0:T(8,128)(2,1)S(1)} %copy-done.6), kind=kOutput, calls=%fused_computation.13 | convolution fusion | flops 1222115328 | bytes 7667712 | tf_op jit(solution)/shard_map/dot_general | solution.py:12
  207.5 10.4 %all-to-all-done.1 = bf16[1,8,24,2048]{3,2,0,1:T(8,128)(2,1)S(1)} async-done(((bf16[1,8,24,2048]{3,2,0,1:T(8,128)(2,1)}), bf16[1,8,24,2048]{3,2,0,1:T(8,128)(2,1)S(1)}, u32[]{:S(2)}, u32[]{:S(2)}) %all-to-all-start.1) | async-done | bytes 786464 | tf_op jit(solution)/shard_map/all_to_all | solution.py:8
  217.8 7.3 %all-to-all-start.3 = ((bf16[1,8,24,2048]{3,2,0,1:T(8,128)(2,1)}), bf16[1,8,24,2048]{3,2,0,1:T(8,128)(2,1)S(1)}, u32[]{:S(2)}, u32[]{:S(2)}) async-start(bf16[1,8,24,2048]{3,2,0,1:T(8,128)(2,1)} %bitcast.67), calls=%async_computation.3 | async-start | bytes 1572864 | tf_op jit(solution)/shard_map/all_to_all | solution.py:8
  225.1 6.9 %reshape.137 = bf16[2048,1,8,24]{3,2,1,0:T(8,128)(2,1)} reshape(bf16[4,2,49152]{2,1,0:T(2,128)(2,1)S(1)} %all-to-all-done.4) | data formatting | bytes 1572864
  232.0 5.6 %copy.34 = bf16[1,8,24,4,512]{4,3,2,1,0:T(4,128)(2,1)} copy(bf16[1,8,24,4,512]{2,1,4,3,0:T(8,128)(2,1)} %bitcast.59) | data formatting | bytes 1572864 | tf_op jit(solution)/shard_map/all_to_all | solution.py:101
  237.6 2.2 copy.30
  239.8 6.9 %reshape.139 = bf16[2048,1,8,24]{3,2,1,0:T(8,128)(2,1)} reshape(bf16[4,2,49152]{2,1,0:T(2,128)(2,1)S(1)} %copy-done.3) | data formatting | bytes 1572864
  246.7 4.9 %copy.35 = bf16[1,8,24,4,512]{4,3,2,1,0:T(4,128)(2,1)S(1)} copy(bf16[1,8,24,4,512]{2,1,4,3,0:T(8,128)(2,1)} %bitcast.60) | data formatting | bytes 1572864 | tf_op jit(solution)/shard_map/all_to_all | solution.py:102
  251.6 1.0 copy.33
  252.7 0.9 gather_fusion.1
  253.6 0.9 gather_fusion.3
  254.6 0.9 broadcast_select_fusion
  255.5 1.1 multiply_convert_fusion.1
  256.6 3.2 %fusion.10 = bf16[1,768,512]{2,1,0:T(8,128)(2,1)} fusion(bf16[768,768]{1,0:T(8,128)(2,1)} %all-gather.11.cloned.1.call-done, bf16[768,512]{1,0:T(8,128)(2,1)} %bitcast.68), kind=kOutput, calls=%fused_computation.16 | convolution fusion | flops 604372992 | bytes 2752512 | tf_op jit(solution)/shard_map/dot_general | solution.py:18
  259.7 3.1 %convolution_convert_fusion = bf16[512,1536]{1,0:T(8,128)(2,1)S(1)} fusion(bf16[768,512]{1,0:T(8,128)(2,1)S(1)} %bitcast.63, bf16[768,1536]{1,0:T(8,128)(2,1)} %all-gather.9.cloned.1.call-done), kind=kOutput, calls=%fused_computation.11 | convolution fusion | flops 1208745984 | bytes 4718592 | tf_op jit(solution)/shard_map/dot_general | solution.py:18
  262.8 1.2 slice_bitcast_fusion
  (34 shorter events, 0.2 us)
Async XLA Ops:
  7.2 4.8 %copy-start = (bf16[128,2048]{1,0:T(8,128)(2,1)S(1)}, bf16[128,2048]{1,0:T(8,128)(2,1)}, u32[]{:S(2)}) copy-start(bf16[128,2048]{1,0:T(8,128)(2,1)} %param.12) | copy-start | bytes 1572868
  7.2 47.7 %all-gather.15.cloned.1.call-start = ((), (), s32[]{:S(2)}) async-start(), calls=%async_computation.9 | async-start | bytes 3932160 | tf_op jit(solution)/shard_map/all_gather | solution.py:93
  7.9 92.8 %all-gather.13.cloned.1.call-start = ((), (), s32[]{:S(2)}) async-start(), calls=%async_computation.8 | async-start | bytes 3932160 | tf_op jit(solution)/shard_map/all_gather | solution.py:92
  8.7 137.8 %all-gather.17.cloned.1.call-start = ((), (), s32[]{:S(2)}) async-start(), calls=%async_computation.10 | async-start | bytes 3932160 | tf_op jit(solution)/shard_map/all_gather | solution.py:94
  12.0 1.2 copy-start.1
  13.1 1.3 copy-start.8
  38.2 67.8 %all-to-all-start.2 = ((bf16[1,8,24,2048]{3,2,0,1:T(8,128)(2,1)}), bf16[1,8,24,2048]{3,2,0,1:T(8,128)(2,1)S(1)}, u32[]{:S(2)}, u32[]{:S(2)}) async-start(bf16[1,8,24,2048]{3,2,0,1:T(8,128)(2,1)} %bitcast.12), calls=%async_computation.2 | async-start | bytes 1572864 | tf_op jit(solution)/shard_map/all_to_all | solution.py:8
  45.6 211.0 %all-gather.11.cloned.1.call-start = ((), (), s32[]{:S(2)}) async-start(), calls=%async_computation.7 | async-start | bytes 1474560 | tf_op jit(solution)/shard_map/all_gather | solution.py:105
  162.3 17.1 %all-to-all-start.4 = ((bf16[4,2,49152]{2,1,0:T(2,128)(2,1)}), bf16[4,2,49152]{2,1,0:T(2,128)(2,1)S(1)}, u32[]{:S(2)}, u32[]{:S(2)}) async-start(bf16[4,2,49152]{2,1,0:T(2,128)(2,1)} %reshape.136), calls=%async_computation.4 | async-start | bytes 1572864 | tf_op jit(solution)/shard_map/all_to_all | solution.py:101
  170.3 13.2 %copy-start.5 = (bf16[192,768]{1,0:T(8,128)(2,1)S(1)}, bf16[192,768]{1,0:T(8,128)(2,1)}, u32[]{:S(2)}) copy-start(bf16[192,768]{1,0:T(8,128)(2,1)} %get-tuple-element.13) | copy-start | bytes 884740
  179.5 10.7 %all-to-all-start.5 = ((bf16[4,2,49152]{2,1,0:T(2,128)(2,1)}), bf16[4,2,49152]{2,1,0:T(2,128)(2,1)S(1)}, u32[]{:S(2)}, u32[]{:S(2)}) async-start(bf16[4,2,49152]{2,1,0:T(2,128)(2,1)} %reshape.138), calls=%async_computation.5 | async-start | bytes 1572864 | tf_op jit(solution)/shard_map/all_to_all | solution.py:102
  183.5 17.1 %copy-start.6 = (bf16[192,768]{1,0:T(8,128)(2,1)S(1)}, bf16[192,768]{1,0:T(8,128)(2,1)}, u32[]{:S(2)}) copy-start(bf16[192,768]{1,0:T(8,128)(2,1)} %get-tuple-element.9) | copy-start | bytes 884740
  183.5 17.1 %copy-start.7 = (bf16[192,768]{1,0:T(8,128)(2,1)S(1)}, bf16[192,768]{1,0:T(8,128)(2,1)}, u32[]{:S(2)}) copy-start(bf16[192,768]{1,0:T(8,128)(2,1)} %get-tuple-element.10) | copy-start | bytes 884740
  190.2 0.9 copy-start.2
  191.0 26.8 %all-to-all-start.1 = ((bf16[1,8,24,2048]{3,2,0,1:T(8,128)(2,1)}), bf16[1,8,24,2048]{3,2,0,1:T(8,128)(2,1)S(1)}, u32[]{:S(2)}, u32[]{:S(2)}) async-start(bf16[1,8,24,2048]{3,2,0,1:T(8,128)(2,1)} %bitcast.9), calls=%async_computation.1 | async-start | bytes 1572864 | tf_op jit(solution)/shard_map/all_to_all | solution.py:8
  200.6 59.1 %all-gather.9.cloned.1.call-start = ((), (), s32[]{:S(2)}) async-start(), calls=%async_computation.6 | async-start | bytes 2949120 | tf_op jit(solution)/shard_map/all_gather | solution.py:106
  217.8 35.7 %all-to-all-start.3 = ((bf16[1,8,24,2048]{3,2,0,1:T(8,128)(2,1)}), bf16[1,8,24,2048]{3,2,0,1:T(8,128)(2,1)S(1)}, u32[]{:S(2)}, u32[]{:S(2)}) async-start(bf16[1,8,24,2048]{3,2,0,1:T(8,128)(2,1)} %bitcast.67), calls=%async_computation.3 | async-start | bytes 1572864 | tf_op jit(solution)/shard_map/all_to_all | solution.py:8
  232.0 7.7 %copy-start.3 = (bf16[4,2,49152]{2,1,0:T(2,128)(2,1)S(1)}, bf16[4,2,49152]{2,1,0:T(2,128)(2,1)}, u32[]{:S(2)}) copy-start(bf16[4,2,49152]{2,1,0:T(2,128)(2,1)} %copy-done.2) | copy-start | bytes 2359300
  254.5 5.2 %copy-start.4 = (bf16[4,1,8,24,512]{4,3,2,0,1:T(8,128)(2,1)S(1)}, bf16[4,1,8,24,512]{4,3,2,0,1:T(8,128)(2,1)}, u32[]{:S(2)}) copy-start(bf16[4,1,8,24,512]{4,3,2,0,1:T(8,128)(2,1)} %copy.30) | copy-start | bytes 2359300
Sparse Core Ops, SparseCore 0:
  9.9 45.0 all-gather.14
  56.8 43.9 all-gather.12
  102.6 43.7 all-gather.16
  151.0 32.7 all-gather.10
  203.0 37.2 all-gather.8
where the time goes:
time: 273 us; the launch traced here: 271 us
  waiting for transfers between devices  113 us (41%)
  local copies, waits for them, and re-layouts  56.8 us (21%)
  starting transfers between devices  32.2 us (12%)
  matrix products  25.5 us (9%)
  blocking collectives  22.4 us (8%)
  between operations  13.9 us (5%)
  other arithmetic  6.93 us (3%)
    all_gather x1, waiting for transfers between devices, body(): lax.all_gather(w_gate[0], 'dp', axis=0, tiled=True)  45.8 us
    all_gather x1, waiting for transfers between devices, body(): lax.all_gather(w_down[0], 'dp', axis=1, tiled=True)  40.4 us
    unnamed x22, local copies, waits for them, and re-layouts  29.4 us
    all_to_all x3, starting transfers between devices, swap_experts(): lax.all_to_all(buffer, 'expert', split_axis=1, concat_axis=1, tiled=True)  24.2 us
    all_to_all x1, blocking collectives, swap_experts(): lax.all_to_all(buffer, 'expert', split_axis=1, concat_axis=1, tiled=True)  22.4 us
    all_to_all x3, waiting for transfers between devices, swap_experts(): lax.all_to_all(buffer, 'expert', split_axis=1, concat_axis=1, tiled=True)  10.4 us
    dot_general x2, matrix products, contract_last(): lax.dot_general(left_side, right_side, (((1,), (1,)), ((), ())), preferre...  10.3 us
    all_gather x1, waiting for transfers between devices, body(): lax.all_gather(w_up[0], 'dp', axis=0, tiled=True)  9.32 us
  transfers between devices with their start and end apart: 10, of which 6 were waited for; matrix products, arithmetic and copies ran while one was open for 29% of the time, Pallas kernels for 0%

commit v1 on v0

v1 whole, which is shorter than its diff:
```python
import jax
import jax.numpy as jnp
from jax import lax
from jax.sharding import PartitionSpec as P

BOTH = ("dp", "expert")


def contract_last(left_side, right_side):
    return lax.dot_general(
        left_side, right_side, (((1,), (1,)), ((), ())), preferred_element_type=jnp.float32
    )


def contract_first(left_side, right_side):
    return lax.dot_general(
        left_side, right_side, (((0,), (0,)), ((), ())), preferred_element_type=jnp.float32
    )


def pair_list(experts, masks):
    return [
        (replica * experts + expert, (replica ^ masks[expert % 2]) * experts + expert)
        for replica in range(4)
        for expert in range(experts)
    ]


def swap_weight(value):
    experts = lax.axis_size("expert")
    return lax.ppermute(value, BOTH, pair_list(experts, (1, 2)))


def swap_rows(value):
    experts = lax.axis_size("expert")
    return lax.ppermute(value, BOTH, pair_list(experts, (2, 1)))


def swap_expert(value, mask):
    experts = lax.axis_size("expert")
    return lax.ppermute(value, "expert", [(i, i ^ mask) for i in range(experts)])


def turn(value):
    first, second, third, last = jnp.split(value, 4, axis=-1)
    return jnp.concatenate([first, third, second, last], axis=-1)


def send_slots(slots, chips, capacity):
    width = slots.shape[-1]
    half = width // 2
    other = swap_expert(turn(slots[1]), 1)
    rows = jnp.stack([slots[0], other], axis=1).reshape(chips, 2 * capacity, width)
    far = swap_rows(rows[:, :, half:])
    near = rows[:, :, :half]
    pieces = jnp.stack([near, far], axis=1)
    got = [pieces[0]] + [swap_expert(pieces[k], 2 * k) for k in range(1, chips)]
    return jnp.stack(got, axis=0).reshape(chips * 4 * capacity, half)


def return_slots(rows, chips, capacity):
    half = rows.shape[1]
    pieces = rows.reshape(chips, 2, 2 * capacity, half)
    got = [pieces[0]] + [swap_expert(pieces[k], 2 * k) for k in range(1, chips)]
    back = jnp.stack(got, axis=0)
    far = swap_rows(back[:, 1])
    full = jnp.concatenate([back[:, 0], far], axis=2).reshape(chips, 2, capacity, 2 * half)
    other = swap_expert(turn(full[:, 1]), 1)
    return jnp.concatenate([full[:, 0], other], axis=0).reshape(
        2 * chips * capacity, 2 * half
    )


def exchange_sum(part, chips, capacity):
    width = part.shape[1]
    turned = part.astype(jnp.bfloat16).reshape(chips, 2, 2 * capacity, width)[:, ::-1]
    return part + swap_rows(turned.reshape(part.shape)).astype(jnp.float32)


def reorder(value, order):
    rows, width = value.shape
    return jnp.take(value.reshape(rows, 4, width // 4), order, axis=1).reshape(rows, width)


def body(tokens, cotangent, routes, gate_fixed, w_gate, w_up, w_down):
    tok_count, model_width = tokens.shape
    hidden_width = w_gate.shape[2]
    experts = lax.axis_size("expert")
    chips = experts // 2
    capacity = 3 * tok_count // (2 * experts)
    replica = lax.axis_index("dp")
    expert = lax.axis_index("expert")
    side = jnp.where(expert % 2 == 0, 1, 2)
    order = replica ^ jnp.stack([0 * side, side, 3 - side, 0 * side + 3])
    inverse = jnp.argsort(order)

    w_gate, w_up, w_down = w_gate[0], w_up[0], w_down[0]
    gate_w = jnp.concatenate([w_gate, swap_weight(w_gate)], axis=0)
    up_w = jnp.concatenate([w_up, swap_weight(w_up)], axis=0)
    down_w = jnp.concatenate([w_down, swap_weight(w_down)], axis=1)

    route_weight = gate_fixed.astype(jnp.float32) / 65536.0
    one_hot = (routes == jnp.arange(experts, dtype=jnp.int32)[None, :]).astype(jnp.int32)
    position = jnp.sum((jnp.cumsum(one_hot, axis=0) - one_hot) * one_hot, axis=1)
    relative = routes[:, 0] ^ expert
    slot = ((relative % 2) * chips + relative // 2) * capacity + position
    pick = (slot[:, None] == jnp.arange(experts * capacity, dtype=jnp.int32)[None, :]).astype(
        jnp.bfloat16
    )

    scaled = (route_weight * cotangent.astype(jnp.float32)).astype(jnp.bfloat16)
    shape = (2, chips, capacity, model_width)
    slots = contract_first(pick, reorder(tokens, order)).astype(jnp.bfloat16).reshape(shape)
    grad_slots = contract_first(pick, reorder(scaled, order)).astype(jnp.bfloat16).reshape(shape)
    rows = send_slots(slots, chips, capacity)
    grad_rows = send_slots(grad_slots, chips, capacity)

    gate_part = jnp.dot(rows, gate_w, preferred_element_type=jnp.float32)
    up_part = jnp.dot(rows, up_w, preferred_element_type=jnp.float32)
    gate_pre = exchange_sum(gate_part, chips, capacity)
    up_pre = exchange_sum(up_part, chips, capacity)
    grad_hidden = exchange_sum(contract_last(grad_rows, down_w), chips, capacity)
    sigmoid_gate = jax.nn.sigmoid(gate_pre)
    hidden = (gate_pre * sigmoid_gate * up_pre).astype(jnp.bfloat16)
    slot_out = jnp.dot(hidden, down_w, preferred_element_type=jnp.float32).astype(jnp.bfloat16)
    returned = return_slots(slot_out, chips, capacity)
    grad_gate = (
        grad_hidden * up_pre * sigmoid_gate * (1.0 + gate_pre * (1.0 - sigmoid_gate))
    ).astype(jnp.bfloat16)
    grad_up = (grad_hidden * gate_pre * sigmoid_gate).astype(jnp.bfloat16)
    slot_grad_in = (contract_last(grad_gate, gate_w) + contract_last(grad_up, up_w)).astype(
        jnp.bfloat16
    )
    grad_returned = return_slots(slot_grad_in, chips, capacity)

    part = model_width // 4

    def share(pair_sum, axis):
        own, far = jnp.split(pair_sum, 2, axis=axis)
        got = swap_weight(far.astype(jnp.bfloat16)).astype(jnp.float32)
        return (own + got).astype(jnp.bfloat16)[None]

    grad_w_gate = share(contract_first(rows, grad_gate), 0)
    grad_w_up = share(contract_first(rows, grad_up), 0)
    grad_w_down = share(contract_first(hidden, grad_rows), 1)

    picked = jnp.dot(pick, returned, preferred_element_type=jnp.float32)
    mixed = reorder((route_weight * picked).astype(jnp.bfloat16), inverse)
    grad_picked = jnp.dot(pick, grad_returned, preferred_element_type=jnp.float32)
    grad_tokens = reorder(grad_picked.astype(jnp.bfloat16), inverse)
    return (mixed, grad_tokens, grad_w_gate, grad_w_up, grad_w_down)


def solution(mesh):
    return jax.shard_map(
        body,
        mesh=mesh,
        in_specs=(
            P(("dp", "expert"), None),
            P(("dp", "expert"), None),
            P(("dp", "expert"), None),
            P(("dp", "expert"), None),
            P("expert", "dp", None),
            P("expert", "dp", None),
            P("expert", None, "dp"),
        ),
        out_specs=(
            P(("dp", "expert"), None),
            P(("dp", "expert"), None),
            P("expert", "dp", None),
            P("expert", "dp", None),
            P("expert", None, "dp"),
        ),
        check_vma=False,
    )
```

time: 273 us -> 162 us (0.59)
  local copies, waits for them, and re-layouts: 56.8 us -> 12.5 us
  waiting for transfers between devices: 113 us -> 84.8 us
  blocking collectives: 22.4 us -> 0 us
  between operations: 13.9 us -> 1.19 us
  matrix products: 25.5 us -> 20.3 us
  other arithmetic: 6.93 us -> 11.7 us
    all_gather x5 -> x0, waiting for transfers between devices: 95.6 us -> none  [the longest x1 45.8 us: body(): lax.all_gather(w_gate[0], 'dp', axis=0, tiled=True)]
    ppermute x0 -> x29, waiting for transfers between devices: none -> 84.8 us  [the longest x16 43.1 us: swap_expert(): lax.ppermute(value, 'expert', [(i, i ^ mask) for i in range(experts)])]
    all_to_all x5 -> x0, starting transfers between devices: 32 us -> none  [the longest x3 24.2 us: swap_experts(): lax.all_to_all(buffer, 'expert', split_axis=1, concat_axis=1, tiled=True)]
    ppermute x0 -> x29, starting transfers between devices: none -> 30.2 us  [the longest x16 18.8 us: swap_expert(): lax.ppermute(value, 'expert', [(i, i ^ mask) for i in range(experts)])]
    unnamed x22 -> x9, local copies, waits for them, and re-layouts: 29.4 us -> 3.19 us
    all_to_all x1 -> x0, blocking collectives: 22.4 us -> none  [swap_experts(): lax.all_to_all(buffer, 'expert', split_axis=1, concat_axis=1, tiled=True)]
    all_to_all x6 -> x0, local copies, waits for them, and re-layouts: 22 us -> none  [the longest x2 8.37 us: swap_experts(): lax.all_to_all(buffer, 'expert', split_axis=1, concat_axis=1, tiled=True)]
    all_to_all x5 -> x0, waiting for transfers between devices: 15.2 us -> none  [the longest x3 10.4 us: swap_experts(): lax.all_to_all(buffer, 'expert', split_axis=1, concat_axis=1, tiled=True)]
  transfers between devices with their start and end apart: 10 -> 29, of which waited for: 6 -> 14; matrix products, arithmetic and copies ran while one was open for 29% -> 17% of each run, Pallas kernels for 0% -> 0%
where the time goes in v1:
time: 162 us; the launch traced here: 161 us
  waiting for transfers between devices  84.8 us (52%)
  starting transfers between devices  30.2 us (19%)
  matrix products  20.3 us (13%)
  local copies, waits for them, and re-layouts  12.5 us (8%)
  other arithmetic  11.7 us (7%)
    ppermute x16, waiting for transfers between devices, swap_expert(): lax.ppermute(value, 'expert', [(i, i ^ mask) for i in range(experts)])  43.1 us
    ppermute x7, waiting for transfers between devices, swap_rows(): return lax.ppermute(value, BOTH, pair_list(experts, (2, 1)))  28.3 us
    ppermute x16, starting transfers between devices, swap_expert(): lax.ppermute(value, 'expert', [(i, i ^ mask) for i in range(experts)])  18.8 us
    ppermute x6, waiting for transfers between devices, swap_weight(): return lax.ppermute(value, BOTH, pair_list(experts, (1, 2)))  13.5 us
    dot_general x3, matrix products, contract_last(): lax.dot_general(left_side, right_side, (((1,), (1,)), ((), ())), preferre...  6.55 us
    ppermute x6, starting transfers between devices, swap_weight(): return lax.ppermute(value, BOTH, pair_list(experts, (1, 2)))  6.13 us
    ppermute x7, starting transfers between devices, swap_rows(): return lax.ppermute(value, BOTH, pair_list(experts, (2, 1)))  5.27 us
    rev x3, local copies, waits for them, and re-layouts, exchange_sum(): part.astype(jnp.bfloat16).reshape(chips, 2, 2 * capacity, width)[:, ::-1]  4.68 us
  transfers between devices with their start and end apart: 29, of which 14 were waited for; matrix products, arithmetic and copies ran while one was open for 17% of the time, Pallas kernels for 0%

profile of v1, /device:TPU:19, one launch (start us, length us, event | category | flops | bytes accessed | tf_op | source)
XLA Modules:
  0.0 160.7 jit_solution(6915199748854357232)
XLA Ops:
  1.5 1.2 multiply_convert_fusion.3
  6.9 1.2 collective-permute-start.9
  9.9 0.9 collective-permute-done
  11.3 1.2 collective-permute-start.5
  12.5 8.2 %collective-permute-done.16 = bf16[4,48,1024]{2,1,0:T(8,128)(2,1)S(1)} collective-permute-done((bf16[4,48,1024]{2,1,0:T(8,128)(2,1)S(1)}, bf16[4,48,1024]{2,1,0:T(8,128)(2,1)S(1)}, u32[]{:S(2)}, u32[]{:S(2)}) %collective-permute-start.16) | collective-permute-done | bytes 393248 | tf_op jit(solution)/shard_map/ppermute | solution.py:36
  20.7 1.4 collective-permute-start.17
  22.1 6.9 %collective-permute-done.1 = bf16[4,48,1024]{2,1,0:T(8,128)(2,1)S(1)} collective-permute-done((bf16[4,48,1024]{2,1,0:T(8,128)(2,1)S(1)}, bf16[4,48,1024]{2,1,0:T(8,128)(2,1)S(1)}, u32[]{:S(2)}, u32[]{:S(2)}) %collective-permute-start.1) | collective-permute-done | bytes 393248 | tf_op jit(solution)/shard_map/ppermute | solution.py:36
  30.0 1.3 collective-permute-start.2
  31.4 9.1 %collective-permute-done.19 = bf16[2,48,1024]{2,1,0:T(8,128)(2,1)S(1)} collective-permute-done((bf16[2,48,1024]{2,1,0:T(8,128)(2,1)S(1)}, bf16[2,48,1024]{2,1,0:T(8,128)(2,1)S(1)}, u32[]{:S(2)}, u32[]{:S(2)}) %collective-permute-start.19) | collective-permute-done | bytes 196640 | tf_op jit(solution)/shard_map/ppermute | solution.py:41
  40.6 1.4 collective-permute-start.4
  42.0 2.2 %fusion.59 = (bf16[384,768]{1,0:T(8,128)(2,1)S(1)}, f32[384,768]{1,0:T(8,128)S(1)}) fusion(bf16[384,1024]{1,0:T(8,128)(2,1)S(1)} %bitcast.161, bf16[768,512]{1,0:T(8,128)(2,1)} %collective-permute-done.9, bf16[768,512]{1,0:T(8,128)(2,1)} %bitcast.29), kind=kOutput, calls=%fused_computation.144 | convolution fusion | flops 607420416 | bytes 4128768 | tf_op jit(solution)/shard_map/dot_general | solution.py:10
  44.2 0.9 rev.11
  45.6 0.9 collective-permute-done.3
  46.5 12.3 %collective-permute-done.4 = bf16[2,48,1024]{2,1,0:T(8,128)(2,1)S(1)} collective-permute-done((bf16[2,48,1024]{2,1,0:T(8,128)(2,1)S(1)}, bf16[2,48,1024]{2,1,0:T(8,128)(2,1)S(1)}, u32[]{:S(2)}, u32[]{:S(2)}) %collective-permute-start.4) | collective-permute-done | bytes 196640 | tf_op jit(solution)/shard_map/ppermute | solution.py:41
  59.5 1.2 pad_maximum_fusion.10
  60.7 3.3 %fusion.60 = (bf16[384,768]{1,0:T(8,128)(2,1)}, f32[384,768]{1,0:T(8,128)}) fusion(bf16[384,1024]{1,0:T(8,128)(2,1)S(1)} %bitcast.153, bf16[512,768]{1,0:T(8,128)(2,1)} %collective-permute-done.5, bf16[512,768]{1,0:T(8,128)(2,1)} %bitcast.23), kind=kOutput, calls=%fused_computation.145 | convolution fusion | flops 607420416 | bytes 4128768 | tf_op jit(solution)/shard_map/dot_general | solution.py:118
  64.0 1.9 %rev.9 = bf16[4,2,48,768]{3,2,1,0:T(8,128)(2,1)} reverse(bf16[4,2,48,768]{3,2,1,0:T(8,128)(2,1)} %bitcast.185), dimensions={1} | reverse | bytes 1179648 | tf_op jit(solution)/shard_map/rev | solution.py:76
  66.0 1.0 collective-permute-start.6
  66.9 3.3 %fusion.58 = (bf16[384,768]{1,0:T(8,128)(2,1)}, f32[384,768]{1,0:T(8,128)}) fusion(bf16[384,1024]{1,0:T(8,128)(2,1)S(1)} %bitcast.154, bf16[512,768]{1,0:T(8,128)(2,1)} %collective-permute-done.7, bf16[512,768]{1,0:T(8,128)(2,1)} %bitcast.26), kind=kOutput, calls=%fused_computation.143 | convolution fusion | flops 607420416 | bytes 4128768 | tf_op jit(solution)/shard_map/dot_general | solution.py:119
  70.3 1.9 %rev.10 = bf16[4,2,48,768]{3,2,1,0:T(8,128)(2,1)} reverse(bf16[4,2,48,768]{3,2,1,0:T(8,128)(2,1)} %bitcast.186), dimensions={1} | reverse | bytes 1179648 | tf_op jit(solution)/shard_map/rev | solution.py:76
  73.5 1.8 %collective-permute-done.6 = bf16[384,768]{1,0:T(8,128)(2,1)} collective-permute-done((bf16[384,768]{1,0:T(8,128)(2,1)}, bf16[384,768]{1,0:T(8,128)(2,1)}, u32[]{:S(2)}, u32[]{:S(2)}) %collective-permute-start.6) | collective-permute-done | bytes 589856 | tf_op jit(solution)/shard_map/ppermute | solution.py:36
  75.3 6.3 %collective-permute-done.8 = bf16[384,768]{1,0:T(8,128)(2,1)} collective-permute-done((bf16[384,768]{1,0:T(8,128)(2,1)}, bf16[384,768]{1,0:T(8,128)(2,1)}, u32[]{:S(2)}, u32[]{:S(2)}) %collective-permute-start.8) | collective-permute-done | bytes 589856 | tf_op jit(solution)/shard_map/ppermute | solution.py:36
  81.6 2.8 %multiply_convert_fusion.1 = (bf16[384,768]{1,0:T(8,128)(2,1)S(1)}, bf16[384,768]{1,0:T(8,128)(2,1)S(1)}, bf16[384,768]{1,0:T(8,128)(2,1)S(1)}) fusion(f32[384,768]{1,0:T(8,128)} %get-tuple-element.71, bf16[384,768]{1,0:T(8,128)(2,1)} %collective-permute-done.8, f32[384,768]{1,0:T(8,128)S(1)} %get-tuple-element.73, ...), kind=kLoop, calls=%fused_computation.24 | loop fusion | flops 6488064 | bytes 7077888 | tf_op jit(solution)/shard_map/convert_element_type | solution.py:129
  84.4 1.0 fusion.63
  85.4 2.1 %convolution_convert_fusion.3 = bf16[384,1024]{1,0:T(8,128)(2,1)S(1)} fusion(bf16[384,768]{1,0:T(8,128)(2,1)S(1)} %get-tuple-element.17, bf16[768,512]{1,0:T(8,128)(2,1)} %collective-permute-done.9, bf16[768,512]{1,0:T(8,128)(2,1)} %bitcast.29), kind=kOutput, calls=%fused_computation.22 | convolution fusion | flops 607518720 | bytes 2949120 | tf_op jit(solution)/shard_map/dot_general | solution.py:125
  88.4 1.9 %collective-permute-start.12 = (bf16[2,48,1024]{2,1,0:T(8,128)(2,1)S(1)}, bf16[2,48,1024]{2,1,0:T(8,128)(2,1)S(1)}, u32[]{:S(2)}, u32[]{:S(2)}) collective-permute-start(bf16[2,48,1024]{2,1,0:T(8,128)(2,1)S(1)} %bitcast.199), channel_id=1, source_target_pairs={{0,6},{1,7},{2,4},{3,5},{4,2},{5,3},{6,0},{7,1},{8,14},{9,15},{10,... | collective-permute-start | bytes 589832 | tf_op jit(solution)/shard_map/ppermute | solution.py:41
  90.3 2.2 %fusion.5 = f32[384,1024]{1,0:T(8,128)S(1)} fusion(bf16[384,768]{1,0:T(8,128)(2,1)S(1)} %get-tuple-element.16, bf16[512,768]{1,0:T(8,128)(2,1)} %collective-permute-done.7, bf16[512,768]{1,0:T(8,128)(2,1)} %bitcast.26), kind=kOutput, calls=%fused_computation.32 | convolution fusion | flops 607125504 | bytes 3735552 | tf_op jit(solution)/shard_map/dot_general | solution.py:10
  92.5 2.2 %add_convert_fusion = bf16[384,1024]{1,0:T(8,128)(2,1)S(1)} fusion(f32[384,1024]{1,0:T(8,128)S(1)} %fusion.5, bf16[384,768]{1,0:T(8,128)(2,1)S(1)} %get-tuple-element.15, bf16[512,768]{1,0:T(8,128)(2,1)} %collective-permute-done.5, bf16[512,768]{1,0:T(8,128)(2,1)} %bitcast.23), kind=kOutput, calls=%fused_computation.21 | convolution fusion | flops 607911936 | bytes 4521984 | tf_op jit(solution)/shard_map/dot_general | solution.py:10
  94.8 1.0 collective-permute-start.21
  96.0 1.0 fusion.62
  97.1 1.5 collective-permute-start.23
  98.6 17.2 %collective-permute-done.12 = bf16[2,48,1024]{2,1,0:T(8,128)(2,1)S(1)} collective-permute-done((bf16[2,48,1024]{2,1,0:T(8,128)(2,1)S(1)}, bf16[2,48,1024]{2,1,0:T(8,128)(2,1)S(1)}, u32[]{:S(2)}, u32[]{:S(2)}) %collective-permute-start.12) | collective-permute-done | bytes 196640 | tf_op jit(solution)/shard_map/ppermute | solution.py:41
  116.0 1.2 collective-permute-start.13
  117.1 1.2 fusion.61
  118.5 1.6 collective-permute-start.28
  120.3 1.4 collective-permute-start.26
  121.8 2.5 %collective-permute-done.23 = bf16[2,48,1024]{2,1,0:T(8,128)(2,1)S(1)} collective-permute-done((bf16[2,48,1024]{2,1,0:T(8,128)(2,1)S(1)}, bf16[2,48,1024]{2,1,0:T(8,128)(2,1)S(1)}, u32[]{:S(2)}, u32[]{:S(2)}) %collective-permute-start.23) | collective-permute-done | bytes 196640 | tf_op jit(solution)/shard_map/ppermute | solution.py:41
  124.4 1.2 collective-permute-start.24
  125.7 4.9 %collective-permute-start.14 = (bf16[4,24,2048]{2,1,0:T(8,128)(2,1)S(1)}, bf16[4,24,2048]{2,1,0:T(8,128)(2,1)S(1)}, u32[]{:S(2)}, u32[]{:S(2)}) collective-permute-start(bf16[4,24,2048]{2,1,0:T(8,128)(2,1)S(1)} %pad_maximum_fusion.20), channel_id=1, source_target_pairs={{0,1},{1,0},{2,3},{3,2},{4,5},{5,4},{6,7},{7,6},{8,9},{9,8},{10,11... | collective-permute-start | bytes 1179656 | tf_op jit(solution)/shard_map/ppermute | solution.py:41
  130.6 5.0 %collective-permute-done.24 = bf16[4,48,1024]{2,1,0:T(8,128)(2,1)S(1)} collective-permute-done((bf16[4,48,1024]{2,1,0:T(8,128)(2,1)S(1)}, bf16[4,48,1024]{2,1,0:T(8,128)(2,1)S(1)}, u32[]{:S(2)}, u32[]{:S(2)}) %collective-permute-start.24) | collective-permute-done | bytes 393248 | tf_op jit(solution)/shard_map/ppermute | solution.py:36
  135.8 3.3 %collective-permute-start.25 = (bf16[4,24,2048]{2,1,0:T(8,128)(2,1)S(1)}, bf16[4,24,2048]{2,1,0:T(8,128)(2,1)S(1)}, u32[]{:S(2)}, u32[]{:S(2)}) collective-permute-start(bf16[4,24,2048]{2,1,0:T(8,128)(2,1)S(1)} %pad_maximum_fusion.22), channel_id=1, source_target_pairs={{0,1},{1,0},{2,3},{3,2},{4,5},{5,4},{6,7},{7,6},{8,9},{9,8},{10,11... | collective-permute-start | bytes 1179656 | tf_op jit(solution)/shard_map/ppermute | solution.py:41
  139.1 1.1 fusion.10
  140.2 6.4 %collective-permute-done.27 = bf16[512,768]{1,0:T(8,128)(2,1)S(1)} collective-permute-done((bf16[512,768]{1,0:T(8,128)(2,1)S(1)}, bf16[512,768]{1,0:T(8,128)(2,1)S(1)}, u32[]{:S(2)}, u32[]{:S(2)}) %collective-permute-start.27) | collective-permute-done | bytes 786464 | tf_op jit(solution)/shard_map/ppermute | solution.py:31
  146.6 1.1 fusion.9
  147.7 7.1 %collective-permute-done.26 = bf16[512,768]{1,0:T(8,128)(2,1)S(1)} collective-permute-done((bf16[512,768]{1,0:T(8,128)(2,1)S(1)}, bf16[512,768]{1,0:T(8,128)(2,1)S(1)}, u32[]{:S(2)}, u32[]{:S(2)}) %collective-permute-start.26) | collective-permute-done | bytes 786464 | tf_op jit(solution)/shard_map/ppermute | solution.py:31
  154.7 1.0 fusion.8
  158.4 1.0 copy.52
  159.7 1.0 copy.53
  (98 shorter events, 15.5 us)
Async XLA Ops:
  0.6 2.1 %copy-start = (bf16[128,2048]{1,0:T(8,128)(2,1)S(1)}, bf16[128,2048]{1,0:T(8,128)(2,1)}, u32[]{:S(2)}) copy-start(bf16[128,2048]{1,0:T(8,128)(2,1)} %param.9) | copy-start | bytes 1572868
  4.4 0.7 copy-start.2
  6.1 3.0 %collective-permute-start.15 = (bf16[4,24,2048]{2,1,0:T(8,128)(2,1)S(1)}, bf16[4,24,2048]{2,1,0:T(8,128)(2,1)S(1)}, u32[]{:S(2)}, u32[]{:S(2)}) collective-permute-start(bf16[4,24,2048]{2,1,0:T(8,128)(2,1)S(1)} %pad_maximum_fusion.21), channel_id=1, source_target_pairs={{0,1},{1,0},{2,3},{3,2},{4,5},{5,4},{6,7},{7,6},{8,9},{9,8},{10,11... | collective-permute-start | bytes 1179656 | tf_op jit(solution)/shard_map/ppermute | solution.py:41
  6.9 33.7 %collective-permute-start.9 = (bf16[768,512]{1,0:T(8,128)(2,1)}, bf16[768,512]{1,0:T(8,128)(2,1)}, u32[]{:S(2)}, u32[]{:S(2)}) collective-permute-start(bf16[768,512]{1,0:T(8,128)(2,1)} %bitcast.29), channel_id=1, source_target_pairs={{0,8},{1,17},{2,10},{3,19},{4,12},{5,21},{6,14},{7,23},{8,0},{9,25... | collective-permute-start | bytes 2359304 | tf_op jit(solution)/shard_map/ppermute | solution.py:31
  9.0 1.8 %collective-permute-start = (bf16[4,24,2048]{2,1,0:T(8,128)(2,1)S(1)}, bf16[4,24,2048]{2,1,0:T(8,128)(2,1)S(1)}, u32[]{:S(2)}, u32[]{:S(2)}) collective-permute-start(bf16[4,24,2048]{2,1,0:T(8,128)(2,1)S(1)} %pad_maximum_fusion.19), channel_id=1, source_target_pairs={{0,1},{1,0},{2,3},{3,2},{4,5},{5,4},{6,7},{7,6},{8,9},{9,8},{10,11... | collective-permute-start | bytes 1179656 | tf_op jit(solution)/shard_map/ppermute | solution.py:41
  9.3 11.4 %collective-permute-start.16 = (bf16[4,48,1024]{2,1,0:T(8,128)(2,1)S(1)}, bf16[4,48,1024]{2,1,0:T(8,128)(2,1)S(1)}, u32[]{:S(2)}, u32[]{:S(2)}) collective-permute-start(bf16[4,48,1024]{2,1,0:T(8,128)(2,1)S(1)} %get-tuple-element.31), channel_id=1, source_target_pairs={{0,16},{1,9},{2,18},{3,11},{4,20},{5,13},{6,22},{7,15},{8,24},{9,1... | collective-permute-start | bytes 1179656 | tf_op jit(solution)/shard_map/ppermute | solution.py:36
  11.0 18.1 %collective-permute-start.1 = (bf16[4,48,1024]{2,1,0:T(8,128)(2,1)S(1)}, bf16[4,48,1024]{2,1,0:T(8,128)(2,1)S(1)}, u32[]{:S(2)}, u32[]{:S(2)}) collective-permute-start(bf16[4,48,1024]{2,1,0:T(8,128)(2,1)S(1)} %get-tuple-element.47), channel_id=1, source_target_pairs={{0,16},{1,9},{2,18},{3,11},{4,20},{5,13},{6,22},{7,15},{8,24},{9,1... | collective-permute-start | bytes 1179656 | tf_op jit(solution)/shard_map/ppermute | solution.py:36
  11.3 49.4 %collective-permute-start.5 = (bf16[512,768]{1,0:T(8,128)(2,1)}, bf16[512,768]{1,0:T(8,128)(2,1)}, u32[]{:S(2)}, u32[]{:S(2)}) collective-permute-start(bf16[512,768]{1,0:T(8,128)(2,1)} %bitcast.23), channel_id=1, source_target_pairs={{0,8},{1,17},{2,10},{3,19},{4,12},{5,21},{6,14},{7,23},{8,0},{9,25... | collective-permute-start | bytes 2359304 | tf_op jit(solution)/shard_map/ppermute | solution.py:31
  20.7 8.6 %collective-permute-start.17 = (bf16[2,48,1024]{2,1,0:T(8,128)(2,1)S(1)}, bf16[2,48,1024]{2,1,0:T(8,128)(2,1)S(1)}, u32[]{:S(2)}, u32[]{:S(2)}) collective-permute-start(bf16[2,48,1024]{2,1,0:T(8,128)(2,1)S(1)} %get-tuple-element.27), channel_id=1, source_target_pairs={{0,2},{1,3},{2,0},{3,1},{4,6},{5,7},{6,4},{7,5},{8,10},{9,11},{10,... | collective-permute-start | bytes 589832 | tf_op jit(solution)/shard_map/ppermute | solution.py:41
  22.1 8.0 %collective-permute-start.18 = (bf16[2,48,1024]{2,1,0:T(8,128)(2,1)S(1)}, bf16[2,48,1024]{2,1,0:T(8,128)(2,1)S(1)}, u32[]{:S(2)}, u32[]{:S(2)}) collective-permute-start(bf16[2,48,1024]{2,1,0:T(8,128)(2,1)S(1)} %get-tuple-element.29), channel_id=1, source_target_pairs={{0,4},{1,5},{2,6},{3,7},{4,0},{5,1},{6,2},{7,3},{8,12},{9,13},{10,... | collective-permute-start | bytes 589832 | tf_op jit(solution)/shard_map/ppermute | solution.py:41
  29.1 11.4 %collective-permute-start.19 = (bf16[2,48,1024]{2,1,0:T(8,128)(2,1)S(1)}, bf16[2,48,1024]{2,1,0:T(8,128)(2,1)S(1)}, u32[]{:S(2)}, u32[]{:S(2)}) collective-permute-start(bf16[2,48,1024]{2,1,0:T(8,128)(2,1)S(1)} %get-tuple-element.28), channel_id=1, source_target_pairs={{0,6},{1,7},{2,4},{3,5},{4,2},{5,3},{6,0},{7,1},{8,14},{9,15},{10,... | collective-permute-start | bytes 589832 | tf_op jit(solution)/shard_map/ppermute | solution.py:41
  29.3 37.6 %collective-permute-start.7 = (bf16[512,768]{1,0:T(8,128)(2,1)}, bf16[512,768]{1,0:T(8,128)(2,1)}, u32[]{:S(2)}, u32[]{:S(2)}) collective-permute-start(bf16[512,768]{1,0:T(8,128)(2,1)} %bitcast.26), channel_id=1, source_target_pairs={{0,8},{1,17},{2,10},{3,19},{4,12},{5,21},{6,14},{7,23},{8,0},{9,25... | collective-permute-start | bytes 2359304 | tf_op jit(solution)/shard_map/ppermute | solution.py:31
  30.0 15.0 %collective-permute-start.2 = (bf16[2,48,1024]{2,1,0:T(8,128)(2,1)S(1)}, bf16[2,48,1024]{2,1,0:T(8,128)(2,1)}, u32[]{:S(2)}, u32[]{:S(2)}) collective-permute-start(bf16[2,48,1024]{2,1,0:T(8,128)(2,1)S(1)} %get-tuple-element.43), channel_id=1, source_target_pairs={{0,2},{1,3},{2,0},{3,1},{4,6},{5,7},{6,4},{7,5},{8,10},{9,11},{10,... | collective-permute-start | bytes 589832 | tf_op jit(solution)/shard_map/ppermute | solution.py:41
  40.5 6.0 %collective-permute-start.3 = (bf16[2,48,1024]{2,1,0:T(8,128)(2,1)S(1)}, bf16[2,48,1024]{2,1,0:T(8,128)(2,1)}, u32[]{:S(2)}, u32[]{:S(2)}) collective-permute-start(bf16[2,48,1024]{2,1,0:T(8,128)(2,1)S(1)} %get-tuple-element.45), channel_id=1, source_target_pairs={{0,4},{1,5},{2,6},{3,7},{4,0},{5,1},{6,2},{7,3},{8,12},{9,13},{10,... | collective-permute-start | bytes 589832 | tf_op jit(solution)/shard_map/ppermute | solution.py:41
  40.6 18.2 %collective-permute-start.4 = (bf16[2,48,1024]{2,1,0:T(8,128)(2,1)S(1)}, bf16[2,48,1024]{2,1,0:T(8,128)(2,1)S(1)}, u32[]{:S(2)}, u32[]{:S(2)}) collective-permute-start(bf16[2,48,1024]{2,1,0:T(8,128)(2,1)S(1)} %get-tuple-element.44), channel_id=1, source_target_pairs={{0,6},{1,7},{2,4},{3,5},{4,2},{5,3},{6,0},{7,1},{8,14},{9,15},{10,... | collective-permute-start | bytes 589832 | tf_op jit(solution)/shard_map/ppermute | solution.py:41
  45.0 28.5 %collective-permute-start.20 = (bf16[384,768]{1,0:T(8,128)(2,1)}, bf16[384,768]{1,0:T(8,128)(2,1)S(1)}, u32[]{:S(2)}, u32[]{:S(2)}) collective-permute-start(bf16[384,768]{1,0:T(8,128)(2,1)} %bitcast.62), channel_id=1, source_target_pairs={{0,16},{1,9},{2,18},{3,11},{4,20},{5,13},{6,22},{7,15},{8,24},{9,1... | collective-permute-start | bytes 1769480 | tf_op jit(solution)/shard_map/ppermute | solution.py:36
  58.8 0.7 copy-start.1
  66.0 9.3 %collective-permute-start.6 = (bf16[384,768]{1,0:T(8,128)(2,1)}, bf16[384,768]{1,0:T(8,128)(2,1)}, u32[]{:S(2)}, u32[]{:S(2)}) collective-permute-start(bf16[384,768]{1,0:T(8,128)(2,1)} %bitcast.182), channel_id=1, source_target_pairs={{0,16},{1,9},{2,18},{3,11},{4,20},{5,13},{6,22},{7,15},{8,24},{9,1... | collective-permute-start | bytes 1769480 | tf_op jit(solution)/shard_map/ppermute | solution.py:36
  72.2 9.4 %collective-permute-start.8 = (bf16[384,768]{1,0:T(8,128)(2,1)}, bf16[384,768]{1,0:T(8,128)(2,1)}, u32[]{:S(2)}, u32[]{:S(2)}) collective-permute-start(bf16[384,768]{1,0:T(8,128)(2,1)} %bitcast.183), channel_id=1, source_target_pairs={{0,16},{1,9},{2,18},{3,11},{4,20},{5,13},{6,22},{7,15},{8,24},{9,1... | collective-permute-start | bytes 1769480 | tf_op jit(solution)/shard_map/ppermute | solution.py:36
  87.6 9.4 %collective-permute-start.10 = (bf16[2,48,1024]{2,1,0:T(8,128)(2,1)S(1)}, bf16[2,48,1024]{2,1,0:T(8,128)(2,1)S(1)}, u32[]{:S(2)}, u32[]{:S(2)}) collective-permute-start(bf16[2,48,1024]{2,1,0:T(8,128)(2,1)S(1)} %bitcast.206), channel_id=1, source_target_pairs={{0,2},{1,3},{2,0},{3,1},{4,6},{5,7},{6,4},{7,5},{8,10},{9,11},{10,... | collective-permute-start | bytes 589832 | tf_op jit(solution)/shard_map/ppermute | solution.py:41
  87.7 10.9 %collective-permute-start.11 = (bf16[2,48,1024]{2,1,0:T(8,128)(2,1)S(1)}, bf16[2,48,1024]{2,1,0:T(8,128)(2,1)S(1)}, u32[]{:S(2)}, u32[]{:S(2)}) collective-permute-start(bf16[2,48,1024]{2,1,0:T(8,128)(2,1)S(1)} %bitcast.202), channel_id=1, source_target_pairs={{0,4},{1,5},{2,6},{3,7},{4,0},{5,1},{6,2},{7,3},{8,12},{9,13},{10,... | collective-permute-start | bytes 589832 | tf_op jit(solution)/shard_map/ppermute | solution.py:41
  88.4 27.4 %collective-permute-start.12 = (bf16[2,48,1024]{2,1,0:T(8,128)(2,1)S(1)}, bf16[2,48,1024]{2,1,0:T(8,128)(2,1)S(1)}, u32[]{:S(2)}, u32[]{:S(2)}) collective-permute-start(bf16[2,48,1024]{2,1,0:T(8,128)(2,1)S(1)} %bitcast.199), channel_id=1, source_target_pairs={{0,6},{1,7},{2,4},{3,5},{4,2},{5,3},{6,0},{7,1},{8,14},{9,15},{10,... | collective-permute-start | bytes 589832 | tf_op jit(solution)/shard_map/ppermute | solution.py:41
  94.8 25.5 %collective-permute-start.21 = (bf16[2,48,1024]{2,1,0:T(8,128)(2,1)S(1)}, bf16[2,48,1024]{2,1,0:T(8,128)(2,1)S(1)}, u32[]{:S(2)}, u32[]{:S(2)}) collective-permute-start(bf16[2,48,1024]{2,1,0:T(8,128)(2,1)S(1)} %bitcast.198), channel_id=1, source_target_pairs={{0,2},{1,3},{2,0},{3,1},{4,6},{5,7},{6,4},{7,5},{8,10},{9,11},{10,... | collective-permute-start | bytes 589832 | tf_op jit(solution)/shard_map/ppermute | solution.py:41
  95.8 24.5 %collective-permute-start.22 = (bf16[2,48,1024]{2,1,0:T(8,128)(2,1)S(1)}, bf16[2,48,1024]{2,1,0:T(8,128)(2,1)S(1)}, u32[]{:S(2)}, u32[]{:S(2)}) collective-permute-start(bf16[2,48,1024]{2,1,0:T(8,128)(2,1)S(1)} %bitcast.196), channel_id=1, source_target_pairs={{0,4},{1,5},{2,6},{3,7},{4,0},{5,1},{6,2},{7,3},{8,12},{9,13},{10,... | collective-permute-start | bytes 589832 | tf_op jit(solution)/shard_map/ppermute | solution.py:41
  97.1 27.2 %collective-permute-start.23 = (bf16[2,48,1024]{2,1,0:T(8,128)(2,1)S(1)}, bf16[2,48,1024]{2,1,0:T(8,128)(2,1)S(1)}, u32[]{:S(2)}, u32[]{:S(2)}) collective-permute-start(bf16[2,48,1024]{2,1,0:T(8,128)(2,1)S(1)} %bitcast.193), channel_id=1, source_target_pairs={{0,6},{1,7},{2,4},{3,5},{4,2},{5,3},{6,0},{7,1},{8,14},{9,15},{10,... | collective-permute-start | bytes 589832 | tf_op jit(solution)/shard_map/ppermute | solution.py:41
  116.0 9.6 %collective-permute-start.13 = (bf16[4,48,1024]{2,1,0:T(8,128)(2,1)S(1)}, bf16[4,48,1024]{2,1,0:T(8,128)(2,1)S(1)}, u32[]{:S(2)}, u32[]{:S(2)}) collective-permute-start(bf16[4,48,1024]{2,1,0:T(8,128)(2,1)S(1)} %get-tuple-element.37), channel_id=1, source_target_pairs={{0,16},{1,9},{2,18},{3,11},{4,20},{5,13},{6,22},{7,15},{8,24},{9,1... | collective-permute-start | bytes 1179656 | tf_op jit(solution)/shard_map/ppermute | solution.py:36
  118.5 20.6 %collective-permute-start.28 = (bf16[768,512]{1,0:T(8,128)(2,1)S(1)}, bf16[768,512]{1,0:T(8,128)(2,1)S(1)}, u32[]{:S(2)}, u32[]{:S(2)}) collective-permute-start(bf16[768,512]{1,0:T(8,128)(2,1)S(1)} %split.131), channel_id=1, source_target_pairs={{0,8},{1,17},{2,10},{3,19},{4,12},{5,21},{6,14},{7,23},{8,0},{9,25... | collective-permute-start | bytes 2359304 | tf_op jit(solution)/shard_map/ppermute | solution.py:31
  120.2 26.3 %collective-permute-start.27 = (bf16[512,768]{1,0:T(8,128)(2,1)S(1)}, bf16[512,768]{1,0:T(8,128)(2,1)S(1)}, u32[]{:S(2)}, u32[]{:S(2)}) collective-permute-start(bf16[512,768]{1,0:T(8,128)(2,1)S(1)} %split.132), channel_id=1, source_target_pairs={{0,8},{1,17},{2,10},{3,19},{4,12},{5,21},{6,14},{7,23},{8,0},{9,25... | collective-permute-start | bytes 2359304 | tf_op jit(solution)/shard_map/ppermute | solution.py:31
  120.3 34.4 %collective-permute-start.26 = (bf16[512,768]{1,0:T(8,128)(2,1)S(1)}, bf16[512,768]{1,0:T(8,128)(2,1)S(1)}, u32[]{:S(2)}, u32[]{:S(2)}) collective-permute-start(bf16[512,768]{1,0:T(8,128)(2,1)S(1)} %split.133), channel_id=1, source_target_pairs={{0,8},{1,17},{2,10},{3,19},{4,12},{5,21},{6,14},{7,23},{8,0},{9,25... | collective-permute-start | bytes 2359304 | tf_op jit(solution)/shard_map/ppermute | solution.py:31
  124.4 11.3 %collective-permute-start.24 = (bf16[4,48,1024]{2,1,0:T(8,128)(2,1)S(1)}, bf16[4,48,1024]{2,1,0:T(8,128)(2,1)S(1)}, u32[]{:S(2)}, u32[]{:S(2)}) collective-permute-start(bf16[4,48,1024]{2,1,0:T(8,128)(2,1)S(1)} %get-tuple-element.21), channel_id=1, source_target_pairs={{0,16},{1,9},{2,18},{3,11},{4,20},{5,13},{6,22},{7,15},{8,24},{9,1... | collective-permute-start | bytes 1179656 | tf_op jit(solution)/shard_map/ppermute | solution.py:36
  125.7 30.1 %collective-permute-start.14 = (bf16[4,24,2048]{2,1,0:T(8,128)(2,1)S(1)}, bf16[4,24,2048]{2,1,0:T(8,128)(2,1)S(1)}, u32[]{:S(2)}, u32[]{:S(2)}) collective-permute-start(bf16[4,24,2048]{2,1,0:T(8,128)(2,1)S(1)} %pad_maximum_fusion.20), channel_id=1, source_target_pairs={{0,1},{1,0},{2,3},{3,2},{4,5},{5,4},{6,7},{7,6},{8,9},{9,8},{10,11... | collective-permute-start | bytes 1179656 | tf_op jit(solution)/shard_map/ppermute | solution.py:41
  135.8 20.5 %collective-permute-start.25 = (bf16[4,24,2048]{2,1,0:T(8,128)(2,1)S(1)}, bf16[4,24,2048]{2,1,0:T(8,128)(2,1)S(1)}, u32[]{:S(2)}, u32[]{:S(2)}) collective-permute-start(bf16[4,24,2048]{2,1,0:T(8,128)(2,1)S(1)} %pad_maximum_fusion.22), channel_id=1, source_target_pairs={{0,1},{1,0},{2,3},{3,2},{4,5},{5,4},{6,7},{7,6},{8,9},{9,8},{10,11... | collective-permute-start | bytes 1179656 | tf_op jit(solution)/shard_map/ppermute | solution.py:41

commit v2 on v1

v2 whole, which is shorter than its diff:
```python
import functools

import jax
import jax.numpy as jnp
from jax import lax
from jax.experimental import pallas as pl
from jax.experimental.pallas import tpu as pltpu
from jax.sharding import PartitionSpec as P

BOTH = ("dp", "expert")
VMEM_BYTES = 40 * 2**20
F32 = jnp.float32
BF16 = jnp.bfloat16


def contract_last(left_side, right_side):
    return lax.dot_general(
        left_side, right_side, (((1,), (1,)), ((), ())), preferred_element_type=F32
    )


def contract_first(left_side, right_side):
    return lax.dot_general(
        left_side, right_side, (((0,), (0,)), ((), ())), preferred_element_type=F32
    )


def plain_dot(left_side, right_side):
    return jnp.dot(left_side, right_side, preferred_element_type=F32)


def pair_list(experts, masks):
    return [
        (replica * experts + expert, (replica ^ masks[expert % 2]) * experts + expert)
        for replica in range(4)
        for expert in range(experts)
    ]


def swap_weight(value):
    return lax.ppermute(value, BOTH, pair_list(lax.axis_size("expert"), (1, 2)))


def swap_rows(value):
    return lax.ppermute(value, BOTH, pair_list(lax.axis_size("expert"), (2, 1)))


def swap_expert(value, mask):
    experts = lax.axis_size("expert")
    return lax.ppermute(value, "expert", [(i, i ^ mask) for i in range(experts)])


def offset(expert, j):
    side = 1 + (expert & 1)
    return (0, side, 3 - side, 3)[j]


def after(value, *earlier):
    return lax.optimization_barrier((value,) + earlier)[0]


def params(limit=VMEM_BYTES):
    return pltpu.CompilerParams(vmem_limit_bytes=limit)


def cost(microseconds):
    return pl.CostEstimate(
        flops=int(microseconds * 1e9), bytes_accessed=int(microseconds * 3e6), transcendentals=0
    )


def whole(shape):
    return pl.BlockSpec(shape, lambda *_: (0,) * len(shape))


def slot_kernel(
    experts, capacity, tok, cot, route, fixed, gate, up, down,
    slots, grads, pick, weight, packed,
):
    strip = packed.shape[1]
    first = 0
    for source in (gate, up, down):
        count = source.shape[1]
        for j in range(source.shape[2] // strip):
            packed[pl.ds(first, count), :] = source[0, :, j * strip : (j + 1) * strip]
            first += count
    replica, expert = lax.axis_index("dp"), lax.axis_index("expert")
    chips = experts // 2
    tokens, width = tok.shape
    block = width // 4
    half_rows = chips * capacity
    routes = route[...]
    expert_row = lax.broadcasted_iota(jnp.int32, (experts, tokens), 0)
    one_hot = jnp.where(expert_row == routes, 1.0, 0.0)
    earlier = jnp.where(
        lax.broadcasted_iota(jnp.int32, (tokens, tokens), 0)
        < lax.broadcasted_iota(jnp.int32, (tokens, tokens), 1),
        1.0,
        0.0,
    )
    before = plain_dot(one_hot.astype(BF16), earlier.astype(BF16))
    position = jnp.sum(before * one_hot, axis=0, keepdims=True).astype(jnp.int32)
    relative = routes ^ expert
    slot = ((relative & 1) * chips + (relative >> 1)) * capacity + position
    rows = experts * capacity
    chosen = jnp.where(lax.broadcasted_iota(jnp.int32, (rows, tokens), 0) == slot, 1.0, 0.0)
    route_weight = fixed[...].astype(F32) / 65536.0
    slot_weight = jnp.sum(chosen * route_weight, axis=1, keepdims=True)
    pick[...] = jnp.transpose(chosen).astype(BF16)
    weight[...] = jnp.transpose(jnp.broadcast_to(route_weight, (tokens, tokens)))
    chosen = chosen.astype(BF16)
    for core in range(2):
        part = chosen[core * half_rows : (core + 1) * half_rows]
        scale = slot_weight[core * half_rows : (core + 1) * half_rows]
        for j in range(4):
            start = pl.multiple_of((replica ^ offset(expert + core, j)) * block, block)
            out = pl.ds((j % 2) * block, block)
            source = tok[:, pl.ds(start, block)]
            slots[core, j // 2, :, out] = plain_dot(part, source).astype(BF16)
            source = cot[:, pl.ds(start, block)]
            grads[core, j // 2, :, out] = (scale * plain_dot(part, source)).astype(BF16)


def make_slots(tokens, cotangent, routes, gate_fixed, weights, experts, capacity, strip):
    count, width = tokens.shape
    half_rows = experts * capacity // 2
    slot_shape = jax.ShapeDtypeStruct((2, 2, half_rows, width // 2), BF16)
    strips = [(value.shape[1], value.shape[2] // strip) for value in weights]
    packed_rows = sum(rows * n for rows, n in strips)
    return pl.pallas_call(
        functools.partial(slot_kernel, experts, capacity),
        out_shape=[
            slot_shape,
            slot_shape,
            jax.ShapeDtypeStruct((count, experts * capacity), BF16),
            jax.ShapeDtypeStruct((count, count), F32),
            jax.ShapeDtypeStruct((packed_rows, strip), BF16),
        ],
        compiler_params=params(60 * 2**20),
        cost_estimate=cost(2),
        name="make_slots",
    )(tokens, cotangent, routes.reshape(1, count), gate_fixed.reshape(1, count), *weights)


def gather_rows(pieces, out):
    rows = out.shape[0] // 2
    step = pieces[0].shape[1]
    for k, piece in enumerate(pieces):
        out[pl.ds(k * step, step), :] = piece[0]
        out[pl.ds(rows + k * step, step), :] = piece[1]


def spread_rows(value, pieces):
    rows = value.shape[0] // 2
    count, _, step, _ = pieces.shape
    for k in range(count):
        pieces[k, 0] = value[k * step : (k + 1) * step].astype(BF16)
        pieces[k, 1] = value[rows + k * step : rows + (k + 1) * step].astype(BF16)


def add_swapped(own, got):
    rows = own.shape[0] // 2
    return own + jnp.concatenate([got[rows:], got[:rows]], axis=0).astype(F32)


def gate_up_kernel(count, *refs):
    pieces, (gate, up, far_gate, far_up, rows, own, send) = refs[:count], refs[count:]

    @pl.when(pl.program_id(0) == 0)
    def _():
        gather_rows(pieces, rows)

    block = gate.shape[1]
    near_x, far_x = rows[:, :block], rows[:, block:]
    for k, (near_w, far_w) in enumerate(((gate, far_gate), (up, far_up))):
        part = plain_dot(near_x, near_w[0]) + plain_dot(far_x, far_w[...])
        own[k] = part
        send[k] = part.astype(BF16)


def gate_up_parts(pieces, w_gate, w_up, far_w, tile):
    _, step, half = pieces[0].shape
    rows = 2 * step * len(pieces)
    _, block, hidden = w_gate.shape
    near = pl.BlockSpec((1, block, tile), lambda j: (0, 0, j))
    part = pl.BlockSpec((2, rows, tile), lambda j: (0, 0, j))
    return pl.pallas_call(
        functools.partial(gate_up_kernel, len(pieces)),
        grid=(hidden // tile,),
        in_specs=[whole(pieces[0].shape)] * len(pieces)
        + [
            near,
            near,
            pl.BlockSpec((block, tile), lambda j: (j, 0)),
            pl.BlockSpec((block, tile), lambda j: (hidden // tile + j, 0)),
        ],
        out_specs=[whole((rows, half)), part, part],
        out_shape=[
            jax.ShapeDtypeStruct((rows, half), BF16),
            jax.ShapeDtypeStruct((2, rows, hidden), F32),
            jax.ShapeDtypeStruct((2, rows, hidden), BF16),
        ],
        compiler_params=params(),
        cost_estimate=cost(3),
        name="gate_up_parts",
    )(*pieces, w_gate, w_up, far_w, far_w)


def grad_hidden_kernel(count, *refs):
    pieces, (down, *far_down, rows, own, send) = refs[:count], refs[count:]

    @pl.when(pl.program_id(0) == 0)
    def _():
        gather_rows(pieces, rows)

    block = down.shape[2]
    part = contract_last(rows[:, :block], down[0])
    for k, strip in enumerate(far_down):
        width = strip.shape[1]
        part += contract_last(rows[:, block + k * width : block + (k + 1) * width], strip[...])
    own[...] = part
    send[...] = part.astype(BF16)


def down_strips(hidden, block, tile):
    first = 2 * block * hidden // tile
    return [
        pl.BlockSpec((tile, tile), lambda j, k=k: ((first + k * hidden) // tile + j, 0))
        for k in range(block // tile)
    ]


def grad_hidden_parts(pieces, w_down, far_w, tile):
    _, step, half = pieces[0].shape
    rows = 2 * step * len(pieces)
    _, hidden, block = w_down.shape
    part = pl.BlockSpec((rows, tile), lambda j: (0, j))
    strips = down_strips(hidden, block, tile)
    return pl.pallas_call(
        functools.partial(grad_hidden_kernel, len(pieces)),
        grid=(hidden // tile,),
        in_specs=[whole(pieces[0].shape)] * len(pieces)
        + [
            pl.BlockSpec((1, tile, block), lambda j: (0, j, 0)),
        ]
        + strips,
        out_specs=[whole((rows, half)), part, part],
        out_shape=[
            jax.ShapeDtypeStruct((rows, half), BF16),
            jax.ShapeDtypeStruct((rows, hidden), F32),
            jax.ShapeDtypeStruct((rows, hidden), BF16),
        ],
        compiler_params=params(),
        cost_estimate=cost(100),
        name="grad_hidden_parts",
    )(*pieces, w_down, *[far_w] * len(strips))


def slot_out_kernel(own, got, down, *refs):
    *far_down, hidden, out, total = refs
    step = pl.program_id(0)
    block = down.shape[2]
    gate_pre = add_swapped(own[0], got[0])
    up_pre = add_swapped(own[1], got[1])
    value = (gate_pre * jax.nn.sigmoid(gate_pre) * up_pre).astype(BF16)
    hidden[...] = value

    @pl.when(step == 0)
    def _():
        total[...] = jnp.zeros_like(total)

    total[:, :block] += plain_dot(value, down[0])
    for k, strip in enumerate(far_down):
        width = strip.shape[1]
        total[:, block + k * width : block + (k + 1) * width] += plain_dot(value, strip[...])

    @pl.when(step == pl.num_programs(0) - 1)
    def _():
        spread_rows(total[...], out)


def slot_out_parts(own, got, w_down, far_w, tile, count):
    _, rows, hidden = own.shape
    block = w_down.shape[2]
    part = pl.BlockSpec((2, rows, tile), lambda j: (0, 0, j))
    out_shape = (count, 2, rows // (2 * count), 2 * block)
    strips = down_strips(hidden, block, tile)
    return pl.pallas_call(
        slot_out_kernel,
        grid=(hidden // tile,),
        in_specs=[
            part,
            part,
            pl.BlockSpec((1, tile, block), lambda j: (0, j, 0)),
        ]
        + strips,
        out_specs=[pl.BlockSpec((rows, tile), lambda j: (0, j)), whole(out_shape)],
        out_shape=[
            jax.ShapeDtypeStruct((rows, hidden), BF16),
            jax.ShapeDtypeStruct(out_shape, BF16),
        ],
        scratch_shapes=[pltpu.VMEM((rows, 2 * block), F32)],
        compiler_params=params(),
        cost_estimate=cost(3),
        name="slot_out",
    )(own, got, w_down, *[far_w] * len(strips))


def slot_grad_kernel(
    own, got, own_grad, got_grad, gate, up, far_gate, far_up, rows, grad_rows, hidden,
    grads, out, far_grads, far_down, total,
):
    step = pl.program_id(0)
    block = gate.shape[1]
    gate_pre = add_swapped(own[0], got[0])
    up_pre = add_swapped(own[1], got[1])
    grad_hidden = add_swapped(own_grad[...], got_grad[...])
    sigmoid_gate = jax.nn.sigmoid(gate_pre)
    grad_gate = (
        grad_hidden * up_pre * sigmoid_gate * (1.0 + gate_pre * (1.0 - sigmoid_gate))
    ).astype(BF16)
    grad_up = (grad_hidden * gate_pre * sigmoid_gate).astype(BF16)
    grads[0] = grad_gate
    grads[1] = grad_up
    far_grads[0] = contract_first(rows[:, block:], grad_gate).astype(BF16)
    far_grads[1] = contract_first(rows[:, block:], grad_up).astype(BF16)
    far_down[...] = contract_first(hidden[...], grad_rows[:, block:]).astype(BF16)

    @pl.when(step == 0)
    def _():
        total[...] = jnp.zeros_like(total)

    total[:, :block] += contract_last(grad_gate, gate[0]) + contract_last(grad_up, up[0])
    total[:, block:] += contract_last(grad_gate, far_gate[...]) + contract_last(
        grad_up, far_up[...]
    )

    @pl.when(step == pl.num_programs(0) - 1)
    def _():
        spread_rows(total[...], out)


def slot_grad_parts(own, got, own_grad, got_grad, w_gate, w_up, far_w, x, y, h, tile, count):
    _, rows, hidden = own.shape
    block = w_gate.shape[1]
    part = pl.BlockSpec((2, rows, tile), lambda j: (0, 0, j))
    near = pl.BlockSpec((1, block, tile), lambda j: (0, 0, j))
    grad_part = pl.BlockSpec((rows, tile), lambda j: (0, j))
    out_shape = (count, 2, rows // (2 * count), 2 * block)
    return pl.pallas_call(
        slot_grad_kernel,
        grid=(hidden // tile,),
        in_specs=[
            part,
            part,
            grad_part,
            grad_part,
            near,
            near,
            pl.BlockSpec((block, tile), lambda j: (j, 0)),
            pl.BlockSpec((block, tile), lambda j: (hidden // tile + j, 0)),
            whole(x.shape),
            whole(y.shape),
            grad_part,
        ],
        out_specs=[
            part,
            whole(out_shape),
            pl.BlockSpec((2, block, tile), lambda j: (0, 0, j)),
            pl.BlockSpec((tile, block), lambda j: (j, 0)),
        ],
        out_shape=[
            jax.ShapeDtypeStruct((2, rows, hidden), BF16),
            jax.ShapeDtypeStruct(out_shape, BF16),
            jax.ShapeDtypeStruct((2, block, hidden), BF16),
            jax.ShapeDtypeStruct((hidden, block), BF16),
        ],
        scratch_shapes=[pltpu.VMEM((rows, 2 * block), F32)],
        compiler_params=params(),
        cost_estimate=cost(100),
        name="slot_grad",
    )(own, got, own_grad, got_grad, w_gate, w_up, far_w, far_w, x, y, h)


def unslot_kernel(weighted, pick, weight, near, far, other, out):
    half_rows, half = near.shape
    block = half // 2
    replica, expert = lax.axis_index("dp"), lax.axis_index("expert")
    for j in range(4):
        start = pl.multiple_of((replica ^ offset(expert, j)) * block, block)
        own = (near if j < 2 else far)[:, pl.ds((j % 2) * block, block)]
        k = (0, 2, 1, 3)[j]
        rest = other[k // 2, :, pl.ds((k % 2) * block, block)]
        value = plain_dot(pick[:, :half_rows], own) + plain_dot(pick[:, half_rows:], rest)
        if weighted:
            value = weight[:, :1] * value
        out[:, pl.ds(start, block)] = value.astype(BF16)


def unslot(pick, weight, near, far, other, weighted):
    count = pick.shape[0]
    half_rows, half = near.shape
    return pl.pallas_call(
        functools.partial(unslot_kernel, weighted),
        out_shape=jax.ShapeDtypeStruct((count, 2 * half), BF16),
        compiler_params=params(),
        cost_estimate=cost(2),
        name="unslot",
    )(pick, weight, near, far, other)


def swap_chips(pieces, earlier):
    got = [pieces[0]]
    for k in range(1, len(pieces)):
        value = pieces[k] if earlier is None else after(pieces[k], earlier[k])
        got.append(swap_expert(value, 2 * k))
    return got


def send_slots(slots, chips, capacity, earlier_far, earlier):
    half = slots.shape[-1]
    other = swap_expert(slots[1], 1)
    far = jnp.stack([slots[0, 1], other[1]], axis=0)
    far = swap_rows(far if earlier_far is None else after(far, earlier_far))
    shape = (chips, 1, capacity, half)
    near = jnp.concatenate([slots[0, 0].reshape(shape), other[0].reshape(shape)], axis=1)
    both = jnp.concatenate([far[0].reshape(shape), far[1].reshape(shape)], axis=1)
    shape = (2 * capacity, half)
    pieces = [
        jnp.stack([near[k].reshape(shape), both[k].reshape(shape)], axis=0) for k in range(chips)
    ]
    return far, swap_chips(pieces, earlier)


def return_slots(got, chips, capacity, before_rows, before_core):
    half = got[0].shape[-1]
    far = swap_rows(after(jnp.stack([piece[1] for piece in got], axis=0), *before_rows))
    near = jnp.stack([piece[0] for piece in got], axis=0)
    shape = (chips, 2, capacity, half)
    near, far = near.reshape(shape), far.reshape(shape)
    rows = chips * capacity
    other = jnp.stack([near[:, 1].reshape(rows, half), far[:, 1].reshape(rows, half)], axis=0)
    other = swap_expert(after(other, *before_core), 1)
    return near[:, 0].reshape(rows, half), far[:, 0].reshape(rows, half), other


def body(tokens, cotangent, routes, gate_fixed, w_gate, w_up, w_down):
    tok_count, model_width = tokens.shape
    hidden_width = w_gate.shape[2]
    experts = lax.axis_size("expert")
    chips = experts // 2
    capacity = 3 * tok_count // (2 * experts)
    block = model_width // 4
    tile = 256 if hidden_width % 256 == 0 else hidden_width
    slots, grad_slots, pick, weight, packed = make_slots(
        tokens, cotangent, routes, gate_fixed, (w_gate, w_up, w_down), experts, capacity, tile
    )
    far_w = swap_weight(packed)
    far, got_pieces = send_slots(slots, chips, capacity, None, None)
    _, got_grad_pieces = send_slots(grad_slots, chips, capacity, far, got_pieces)
    aligned = (2 * capacity) % 16 == 0

    def merged(pieces):
        return pieces if aligned else [jnp.concatenate(pieces, axis=1)]

    def split(value):
        if aligned:
            return [value[k] for k in range(chips)]
        value = value.reshape(2, chips, 2 * capacity, 2 * block)
        return [value[:, k] for k in range(chips)]

    pieces, grad_pieces = merged(got_pieces), merged(got_grad_pieces)
    rows, own, send = gate_up_parts(pieces, w_gate, w_up, far_w, tile)
    got = swap_rows(send)
    grad_rows, own_grad, send_grad = grad_hidden_parts(grad_pieces, w_down, far_w, tile)
    got_grad = swap_rows(send_grad)

    hidden, slot_out = slot_out_parts(own, got, w_down, far_w, tile, len(pieces))
    out_pieces = swap_chips(split(slot_out), None)
    grads, slot_grad, far_grads, far_down = slot_grad_parts(
        own, got, own_grad, got_grad, w_gate, w_up, far_w, rows, grad_rows, hidden, tile, len(pieces)
    )
    grad_out_pieces = swap_chips(split(slot_grad), out_pieces)

    got_far = swap_weight(far_grads)
    got_down = swap_weight(far_down)
    grad_w_gate = contract_first(rows[:, :block], grads[0]) + got_far[0].astype(F32)
    grad_w_up = contract_first(rows[:, :block], grads[1]) + got_far[1].astype(F32)
    grad_w_down = contract_first(hidden, grad_rows[:, :block]) + got_down.astype(F32)
    grad_w_gate, grad_w_up, grad_w_down = (
        value.astype(BF16)[None] for value in (grad_w_gate, grad_w_up, grad_w_down)
    )

    back = return_slots(out_pieces, chips, capacity, (), ())
    mixed = unslot(pick, weight, *back, True)
    grad_back = return_slots(
        grad_out_pieces, chips, capacity, (got_down,), (mixed, grad_w_gate, grad_w_up, grad_w_down)
    )
    grad_tokens = unslot(pick, weight, *grad_back, False)
    return (
        mixed,
        grad_tokens,
        grad_w_gate,
        grad_w_up,
        grad_w_down,
    )


def solution(mesh):
    return jax.shard_map(
        body,
        mesh=mesh,
        in_specs=(
            P(("dp", "expert"), None),
            P(("dp", "expert"), None),
            P(("dp", "expert"), None),
            P(("dp", "expert"), None),
            P("expert", "dp", None),
            P("expert", "dp", None),
            P("expert", None, "dp"),
        ),
        out_specs=(
            P(("dp", "expert"), None),
            P(("dp", "expert"), None),
            P("expert", "dp", None),
            P("expert", "dp", None),
            P("expert", None, "dp"),
        ),
        check_vma=False,
    )
```

time: 162 us -> 131 us (0.81)
  Pallas kernels: 0 us -> 18.6 us
  matrix products: 20.3 us -> 4.46 us
  waiting for transfers between devices: 84.8 us -> 69.7 us
  other arithmetic: 11.7 us -> 0.69 us
  local copies, waits for them, and re-layouts: 12.5 us -> 2.69 us
    pallas_call x0 -> x7, Pallas kernels: none -> 18.6 us  [the longest x1 5.83 us: slot_grad_parts(): pl.pallas_call(slot_grad_kernel, grid=(hidden // tile,), in_specs=[part,...]
    dot_general x8 -> x0, matrix products: 16.1 us -> none  [the longest x3 6.55 us: contract_last(): lax.dot_general(left_side, right_side, (((1,), (1,)), ((), ())), preferre...]
    ppermute x13 -> x9, waiting for transfers between devices: 41.7 us -> 28.3 us  [the longest x6 27.4 us: swap_rows(): return lax.ppermute(value, BOTH, pair_list(lax.axis_size('expert'), (2, 1)))]
    ppermute x16, starting transfers between devices: 18.8 us -> 24.1 us  [swap_expert(): lax.ppermute(value, 'expert', [(i, i ^ mask) for i in range(experts)])]
    rev x3 -> x0, local copies, waits for them, and re-layouts: 4.68 us -> none  [exchange_sum(): part.astype(jnp.bfloat16).reshape(chips, 2, 2 * capacity, width)[:, ::-1]]
    convert_element_type x3 -> x0, other arithmetic: 4.05 us -> none  [the longest x1 2.77 us: body(): grad_gate = (grad_hidden * up_pre * sigmoid_gate * (1.0 + gate_pre * (1.0...]
    ppermute x13 -> x9, starting transfers between devices: 11.4 us -> 7.45 us  [the longest x6 4.68 us: swap_rows(): return lax.ppermute(value, BOTH, pair_list(lax.axis_size('expert'), (2, 1)))]
    broadcast_in_dim x3 -> x0, other arithmetic: 3.27 us -> none  [share(): return (own + got).astype(jnp.bfloat16)[None]]
  transfers between devices with their start and end apart: 29 -> 25, of which waited for: 14 -> 14; matrix products, arithmetic and copies ran while one was open for 17% -> 3% of each run, Pallas kernels for 0% -> 5%
where the time goes in v2:
time: 131 us; the launch traced here: 129 us
  waiting for transfers between devices  69.7 us (53%)
  starting transfers between devices  31.6 us (24%)
  Pallas kernels  18.6 us (14%)
  matrix products  4.46 us (3%)
  local copies, waits for them, and re-layouts  2.69 us (2%)
    ppermute x16, waiting for transfers between devices, swap_expert(): lax.ppermute(value, 'expert', [(i, i ^ mask) for i in range(experts)])  41.4 us
    ppermute x6, waiting for transfers between devices, swap_rows(): return lax.ppermute(value, BOTH, pair_list(lax.axis_size('expert'), (2, 1)))  27.4 us
    ppermute x16, starting transfers between devices, swap_expert(): lax.ppermute(value, 'expert', [(i, i ^ mask) for i in range(experts)])  24.1 us
    pallas_call x1, Pallas kernels, slot_grad_parts(): pl.pallas_call(slot_grad_kernel, grid=(hidden // tile,), in_specs=[part,...  5.83 us
    ppermute x6, starting transfers between devices, swap_rows(): return lax.ppermute(value, BOTH, pair_list(lax.axis_size('expert'), (2, 1)))  4.68 us
    pallas_call x1, Pallas kernels, make_slots(): pl.pallas_call(functools.partial(slot_kernel, experts, capacity), out_sha...  4.61 us
    dot_general x3, matrix products, contract_first(): lax.dot_general(left_side, right_side, (((0,), (0,)), ((), ())), preferre...  4.46 us
    ppermute x3, starting transfers between devices, swap_weight(): return lax.ppermute(value, BOTH, pair_list(lax.axis_size('expert'), (1, 2)))  2.77 us
  transfers between devices with their start and end apart: 25, of which 14 were waited for; matrix products, arithmetic and copies ran while one was open for 3% of the time, Pallas kernels for 5%

profile of v2, /device:TPU:19, one launch (start us, length us, event | category | flops | bytes accessed | tf_op | source)
XLA Modules:
  0.0 128.7 jit_solution(2250871973661099644)
XLA Ops:
  0.6 4.6 %make_slots.1 = (bf16[2,2,96,1024]{3,2,1,0:T(8,128)(2,1)}, bf16[2,2,96,1024]{3,2,1,0:T(8,128)(2,1)}, bf16[128,192]{1,0:T(8,128)(2,1)}, f32[128,128]{1,0:T(8,128)}, bf16[4608,256]{1,0:T(8,128)(2,1)}) custom-call(bf16[128,2048]{1,0:T(8,128)(2,1)} %tok.1, bf16[128,2048]{1,0:T(8,128)(2,1)} %cot.1, s32[1,128]{1,0:T(1,128)} %bitcast.173, s32[1,128]{1,0:T(1,128)} %bitcast.174, ...), custom_call_target="tpu_custom_call" | custom-call | flops 2000000000 | bytes 6000000 | tf_op jit(solution)/shard_map/make_slots/pallas_call | solution.py:130
  5.2 1.1 slice_bitcast_fusion.3
  6.4 0.7 collective-permute-start
  7.1 1.0 slice_bitcast_fusion.2
  8.2 1.3 %collective-permute-start.5 = (bf16[4608,256]{1,0:T(8,128)(2,1)}, bf16[4608,256]{1,0:T(8,128)(2,1)S(1)}, u32[]{:S(2)}, u32[]{:S(2)}) collective-permute-start(bf16[4608,256]{1,0:T(8,128)(2,1)} %get-tuple-element.34), channel_id=1, source_target_pairs={{0,8},{1,17},{2,10},{3,19},{4,12},{5,21},{6,14},{7,23},{8,0},{9,25... | collective-permute-start | bytes 7077896 | tf_op jit(solution)/shard_map/ppermute | solution.py:41
  9.7 0.3 collective-permute-start.1
  10.2 10.6 %collective-permute-done.1 = bf16[2,96,1024]{2,1,0:T(8,128)(2,1)S(1)} collective-permute-done((bf16[2,96,1024]{2,1,0:T(8,128)(2,1)S(1)}, bf16[2,96,1024]{2,1,0:T(8,128)(2,1)S(1)}, u32[]{:S(2)}, u32[]{:S(2)}) %collective-permute-start.1) | collective-permute-done | bytes 393248 | tf_op jit(solution)/shard_map/ppermute | solution.py:45
  20.8 0.3 collective-permute-start.13
  21.2 0.2 collective-permute-start.3
  21.4 1.3 collective-permute-start.2
  22.7 1.4 %collective-permute-start.4 = (bf16[2,48,1024]{2,1,0:T(8,128)(2,1)S(1)}, bf16[2,48,1024]{2,1,0:T(8,128)(2,1)S(1)}, u32[]{:S(2)}, u32[]{:S(2)}) collective-permute-start(bf16[2,48,1024]{2,1,0:T(8,128)(2,1)S(1)} %pad_maximum_fusion.11), channel_id=1, source_target_pairs={{0,6},{1,7},{2,4},{3,5},{4,2},{5,3},{6,0},{7,1},{8,14},{9,15},{10,... | collective-permute-start | bytes 589832 | tf_op jit(solution)/shard_map/ppermute | solution.py:50
  24.1 7.9 %collective-permute-done.13 = bf16[2,96,1024]{2,1,0:T(8,128)(2,1)S(1)} collective-permute-done((bf16[2,96,1024]{2,1,0:T(8,128)(2,1)S(1)}, bf16[2,96,1024]{2,1,0:T(8,128)(2,1)S(1)}, u32[]{:S(2)}, u32[]{:S(2)}) %collective-permute-start.13) | collective-permute-done | bytes 393248 | tf_op jit(solution)/shard_map/ppermute | solution.py:45
  32.1 9.1 %collective-permute-done.4.refs_3_ = bf16[2,48,1024]{2,1,0:T(8,128)(2,1)S(1)} collective-permute-done((bf16[2,48,1024]{2,1,0:T(8,128)(2,1)S(1)}, bf16[2,48,1024]{2,1,0:T(8,128)(2,1)S(1)}, u32[]{:S(2)}, u32[]{:S(2)}) %collective-permute-start.4) | collective-permute-done | bytes 196640 | tf_op jit(solution)/shard_map/ppermute | solution.py:50
  41.3 0.4 collective-permute-start.14
  41.8 2.2 %collective-permute-start.16 = (bf16[2,48,1024]{2,1,0:T(8,128)(2,1)S(1)}, bf16[2,48,1024]{2,1,0:T(8,128)(2,1)S(1)}, u32[]{:S(2)}, u32[]{:S(2)}) collective-permute-start(bf16[2,48,1024]{2,1,0:T(8,128)(2,1)S(1)} %pad_maximum_fusion.15), channel_id=1, source_target_pairs={{0,6},{1,7},{2,4},{3,5},{4,2},{5,3},{6,0},{7,1},{8,14},{9,15},{10,... | collective-permute-start | bytes 589832 | tf_op jit(solution)/shard_map/ppermute | solution.py:50
  44.0 0.9 collective-permute-done.5.refs_6_.refs_7_.refs_0_.refs_1_.refs_5_.far_gate.far_up
  44.9 2.2 %gate_up_parts.1 = (bf16[384,1024]{1,0:T(8,128)(2,1)S(1)}, f32[2,384,768]{2,1,0:T(8,128)S(1)}, bf16[2,384,768]{2,1,0:T(8,128)(2,1)S(1)}) custom-call(bf16[2,48,1024]{2,1,0:T(8,128)(2,1)S(1)} %pad_maximum_fusion.8.refs_0_, bf16[2,48,1024]{2,1,0:T(8,128)(2,1)S(1)} %collective-permute-done.2.refs_1_, bf16[2,48,1024]{2,1,0:T(8,128)(2,1)S(1)} %collective-permute-done.3.refs_2_, ...), custom_call_target="tpu_custom_call" | custom-call | flops 3000000000 | bytes 9000000 | tf_op jit(solution)/shard_map/gate_up_parts/pallas_call | solution.py:187
  47.1 0.4 collective-permute-start.6
  47.5 3.0 %collective-permute-done.15.refs_2_ = bf16[2,48,1024]{2,1,0:T(8,128)(2,1)S(1)} collective-permute-done((bf16[2,48,1024]{2,1,0:T(8,128)(2,1)S(1)}, bf16[2,48,1024]{2,1,0:T(8,128)(2,1)S(1)}, u32[]{:S(2)}, u32[]{:S(2)}) %collective-permute-start.15) | collective-permute-done | bytes 196640 | tf_op jit(solution)/shard_map/ppermute | solution.py:50
  50.5 8.0 %collective-permute-done.16.refs_3_ = bf16[2,48,1024]{2,1,0:T(8,128)(2,1)S(1)} collective-permute-done((bf16[2,48,1024]{2,1,0:T(8,128)(2,1)S(1)}, bf16[2,48,1024]{2,1,0:T(8,128)(2,1)S(1)}, u32[]{:S(2)}, u32[]{:S(2)}) %collective-permute-start.16) | collective-permute-done | bytes 196640 | tf_op jit(solution)/shard_map/ppermute | solution.py:50
  58.5 1.4 %grad_hidden_parts.1 = (bf16[384,1024]{1,0:T(8,128)(2,1)S(1)}, f32[384,768]{1,0:T(8,128)S(1)}, bf16[384,768]{1,0:T(8,128)(2,1)S(1)}) custom-call(bf16[2,48,1024]{2,1,0:T(8,128)(2,1)S(1)} %pad_maximum_fusion.12.refs_0_, bf16[2,48,1024]{2,1,0:T(8,128)(2,1)S(1)} %collective-permute-done.14.refs_1_, bf16[2,48,1024]{2,1,0:T(8,128)(2,1)S(1)} %collective-permute-done.15.refs_2_, ...), custom_call_target="tpu_custom_call" | custom-call | flops 99999997952 | bytes 300000000 | tf_op jit(solution)/shard_map/grad_hidden_parts/pallas_call | solution.py:239
  59.9 1.3 collective-permute-start.17
  61.1 1.4 %collective-permute-done.6.got = bf16[2,384,768]{2,1,0:T(8,128)(2,1)S(1)} collective-permute-done((bf16[2,384,768]{2,1,0:T(8,128)(2,1)S(1)}, bf16[2,384,768]{2,1,0:T(8,128)(2,1)S(1)}, u32[]{:S(2)}, u32[]{:S(2)}) %collective-permute-start.6) | collective-permute-done | bytes 1179680 | tf_op jit(solution)/shard_map/ppermute | solution.py:45
  62.6 2.0 %slot_out.1 = (bf16[384,768]{1,0:T(8,128)(2,1)S(1)}, bf16[4,2,48,1024]{3,2,1,0:T(8,128)(2,1)S(1)}) custom-call(f32[2,384,768]{2,1,0:T(8,128)S(1)} %get-tuple-element.35.own, bf16[2,384,768]{2,1,0:T(8,128)(2,1)S(1)} %collective-permute-done.6.got, bf16[1,768,512]{2,1,0:T(8,128)(2,1)S(1)} %copy-done.1, ...), custom_call_target="tpu_custom_call" | custom-call | flops 3000000000 | bytes 9000000 | tf_op jit(solution)/shard_map/slot_out/pallas_call | solution.py:288
  64.6 4.4 %collective-permute-done.17.got_grad = bf16[384,768]{1,0:T(8,128)(2,1)S(1)} collective-permute-done((bf16[384,768]{1,0:T(8,128)(2,1)S(1)}, bf16[384,768]{1,0:T(8,128)(2,1)S(1)}, u32[]{:S(2)}, u32[]{:S(2)}) %collective-permute-start.17) | collective-permute-done | bytes 589856 | tf_op jit(solution)/shard_map/ppermute | solution.py:45
  69.0 5.8 %slot_grad.1 = (bf16[2,384,768]{2,1,0:T(8,128)(2,1)S(1)}, bf16[4,2,48,1024]{3,2,1,0:T(8,128)(2,1)S(1)}, bf16[2,512,768]{2,1,0:T(8,128)(2,1)S(1)}, bf16[768,512]{1,0:T(8,128)(2,1)S(1)}) custom-call(f32[2,384,768]{2,1,0:T(8,128)S(1)} %get-tuple-element.35.own, bf16[2,384,768]{2,1,0:T(8,128)(2,1)S(1)} %collective-permute-done.6.got, ...), custom_call_target="tpu_custom_call" | custom-call | flops 99999997952 | bytes 300000000 | tf_op jit(solution)/shard_map/slot_grad/pallas_call | solution.py:350
  75.0 1.3 collective-permute-start.7
  76.2 1.1 collective-permute-start.9
  77.3 1.3 collective-permute-start.8
  78.6 1.1 collective-permute-start.21
  79.7 0.3 collective-permute-start.23
  80.1 1.1 collective-permute-start.18
  81.2 1.3 %collective-permute-start.20 = (bf16[2,48,1024]{2,1,0:T(8,128)(2,1)S(1)}, bf16[2,48,1024]{2,1,0:T(8,128)(2,1)S(1)}, u32[]{:S(2)}, u32[]{:S(2)}) collective-permute-start(bf16[2,48,1024]{2,1,0:T(8,128)(2,1)S(1)} %get-tuple-element.51), channel_id=1, source_target_pairs={{0,6},{1,7},{2,4},{3,5},{4,2},{5,3},{6,0},{7,1},{8,14},{9,15},{10,... | collective-permute-start | bytes 589832 | tf_op jit(solution)/shard_map/ppermute | solution.py:50
  82.5 10.1 %collective-permute-done.8 = bf16[2,48,1024]{2,1,0:T(8,128)(2,1)S(1)} collective-permute-done((bf16[2,48,1024]{2,1,0:T(8,128)(2,1)S(1)}, bf16[2,48,1024]{2,1,0:T(8,128)(2,1)S(1)}, u32[]{:S(2)}, u32[]{:S(2)}) %collective-permute-start.8) | collective-permute-done | bytes 196640 | tf_op jit(solution)/shard_map/ppermute | solution.py:50
  92.8 3.5 %collective-permute-start.19 = (bf16[2,48,1024]{2,1,0:T(8,128)(2,1)S(1)}, bf16[2,48,1024]{2,1,0:T(8,128)(2,1)S(1)}, u32[]{:S(2)}, u32[]{:S(2)}) collective-permute-start(bf16[2,48,1024]{2,1,0:T(8,128)(2,1)S(1)} %get-tuple-element.50), channel_id=1, source_target_pairs={{0,4},{1,5},{2,6},{3,7},{4,0},{5,1},{6,2},{7,3},{8,12},{9,13},{10,... | collective-permute-start | bytes 589832 | tf_op jit(solution)/shard_map/ppermute | solution.py:50
  96.3 1.2 collective-permute-start.10
  97.5 7.6 %collective-permute-done.20 = bf16[2,48,1024]{2,1,0:T(8,128)(2,1)S(1)} collective-permute-done((bf16[2,48,1024]{2,1,0:T(8,128)(2,1)S(1)}, bf16[2,48,1024]{2,1,0:T(8,128)(2,1)S(1)}, u32[]{:S(2)}, u32[]{:S(2)}) %collective-permute-start.20) | collective-permute-done | bytes 196640 | tf_op jit(solution)/shard_map/ppermute | solution.py:50
  105.1 2.2 %collective-permute-done.19 = bf16[2,48,1024]{2,1,0:T(8,128)(2,1)S(1)} collective-permute-done((bf16[2,48,1024]{2,1,0:T(8,128)(2,1)S(1)}, bf16[2,48,1024]{2,1,0:T(8,128)(2,1)S(1)}, u32[]{:S(2)}, u32[]{:S(2)}) %collective-permute-start.19) | collective-permute-done | bytes 196640 | tf_op jit(solution)/shard_map/ppermute | solution.py:50
  107.7 7.4 %collective-permute-start.11 = (bf16[2,96,1024]{2,1,0:T(8,128)(2,1)S(1)}, bf16[2,96,1024]{2,1,0:T(8,128)(2,1)S(1)}, u32[]{:S(2)}, u32[]{:S(2)}) collective-permute-start(bf16[2,96,1024]{2,1,0:T(8,128)(2,1)S(1)} %pad_maximum_fusion.3), channel_id=1, source_target_pairs={{0,1},{1,0},{2,3},{3,2},{4,5},{5,4},{6,7},{7,6},{8,9},{9,8},{10,11... | collective-permute-start | bytes 1179656 | tf_op jit(solution)/shard_map/ppermute | solution.py:50
  115.2 1.3 collective-permute-start.22
  116.5 1.5 %fusion.2 = bf16[1,768,512]{2,1,0:T(8,128)(2,1)} fusion(bf16[768,512]{1,0:T(8,128)(2,1)S(1)} %collective-permute-done.21, bf16[384,768]{1,0:T(8,128)(2,1)S(1)} %get-tuple-element.47.hidden, bf16[384,1024]{1,0:T(8,128)(2,1)S(1)} %get-tuple-element.46.grad_rows), kind=kOutput, calls=%fused_computation.5 | convolution fusion | flops 303169536 | bytes 2555904 | tf_op jit(solution)/shard_map/dot_general | solution.py:23
  117.9 1.3 unslot.2
  119.2 3.0 %collective-permute-done.22 = bf16[4,48,1024]{2,1,0:T(8,128)(2,1)S(1)} collective-permute-done((bf16[4,48,1024]{2,1,0:T(8,128)(2,1)S(1)}, bf16[4,48,1024]{2,1,0:T(8,128)(2,1)S(1)}, u32[]{:S(2)}, u32[]{:S(2)}) %collective-permute-start.22) | collective-permute-done | bytes 393248 | tf_op jit(solution)/shard_map/ppermute | solution.py:45
  122.3 1.5 %fusion.4 = bf16[1,512,768]{2,1,0:T(8,128)(2,1)} fusion(bf16[2,512,768]{2,1,0:T(8,128)(2,1)S(1)} %collective-permute-done.23, bf16[2,384,768]{2,1,0:T(8,128)(2,1)S(1)} %get-tuple-element.54, bf16[384,1024]{1,0:T(8,128)(2,1)S(1)} %get-tuple-element.45.rows), kind=kOutput, calls=%fused_computation.7 | convolution fusion | flops 303169536 | bytes 2555904 | tf_op jit(solution)/shard_map/dot_general | solution.py:23
  123.8 1.5 %fusion.3 = bf16[1,512,768]{2,1,0:T(8,128)(2,1)} fusion(bf16[2,512,768]{2,1,0:T(8,128)(2,1)S(1)} %collective-permute-done.23, bf16[2,384,768]{2,1,0:T(8,128)(2,1)S(1)} %get-tuple-element.54, bf16[384,1024]{1,0:T(8,128)(2,1)S(1)} %get-tuple-element.45.rows), kind=kOutput, calls=%fused_computation.6 | convolution fusion | flops 303169536 | bytes 2555904 | tf_op jit(solution)/shard_map/dot_general | solution.py:23
  125.2 0.9 collective-permute-start.24
  126.1 1.3 %collective-permute-done.24.other = bf16[2,96,1024]{2,1,0:T(8,128)(2,1)S(1)} collective-permute-done((bf16[2,96,1024]{2,1,0:T(8,128)(2,1)S(1)}, bf16[2,96,1024]{2,1,0:T(8,128)(2,1)S(1)}, u32[]{:S(2)}, u32[]{:S(2)}) %collective-permute-start.24) | collective-permute-done | bytes 393248 | tf_op jit(solution)/shard_map/ppermute | solution.py:50
  127.5 1.3 unslot.3
  (69 shorter events, 1.5 us)
Async XLA Ops:
  5.2 4.3 %copy-start.6 = (bf16[2,2,96,1024]{3,2,1,0:T(8,128)(2,1)S(1)}, bf16[2,2,96,1024]{3,2,1,0:T(8,128)(2,1)}, u32[]{:S(2)}) copy-start(bf16[2,2,96,1024]{3,2,1,0:T(8,128)(2,1)} %get-tuple-element.33) | copy-start | bytes 2359300
  5.2 4.3 %copy-start.7 = (bf16[2,2,96,1024]{3,2,1,0:T(8,128)(2,1)S(1)}, bf16[2,2,96,1024]{3,2,1,0:T(8,128)(2,1)}, u32[]{:S(2)}) copy-start(bf16[2,2,96,1024]{3,2,1,0:T(8,128)(2,1)} %get-tuple-element.38) | copy-start | bytes 2359300
  6.4 3.2 %collective-permute-start = (bf16[2,96,1024]{2,1,0:T(8,128)(2,1)S(1)}, bf16[2,96,1024]{2,1,0:T(8,128)(2,1)S(1)}, u32[]{:S(2)}, u32[]{:S(2)}) collective-permute-start(bf16[2,96,1024]{2,1,0:T(8,128)(2,1)S(1)} %slice_bitcast_fusion.3), channel_id=1, source_target_pairs={{0,1},{1,0},{2,3},{3,2},{4,5},{5,4},{6,7},{7,6},{8,9},{9,8},{10,11... | collective-permute-start | bytes 1179656 | tf_op jit(solution)/shard_map/ppermute | solution.py:50
  8.2 1.9 %collective-permute-start.12 = (bf16[2,96,1024]{2,1,0:T(8,128)(2,1)S(1)}, bf16[2,96,1024]{2,1,0:T(8,128)(2,1)S(1)}, u32[]{:S(2)}, u32[]{:S(2)}) collective-permute-start(bf16[2,96,1024]{2,1,0:T(8,128)(2,1)S(1)} %slice_bitcast_fusion.2), channel_id=1, source_target_pairs={{0,1},{1,0},{2,3},{3,2},{4,5},{5,4},{6,7},{7,6},{8,9},{9,8},{10,11... | collective-permute-start | bytes 1179656 | tf_op jit(solution)/shard_map/ppermute | solution.py:50
  8.2 36.7 %collective-permute-start.5 = (bf16[4608,256]{1,0:T(8,128)(2,1)}, bf16[4608,256]{1,0:T(8,128)(2,1)S(1)}, u32[]{:S(2)}, u32[]{:S(2)}) collective-permute-start(bf16[4608,256]{1,0:T(8,128)(2,1)} %get-tuple-element.34), channel_id=1, source_target_pairs={{0,8},{1,17},{2,10},{3,19},{4,12},{5,21},{6,14},{7,23},{8,0},{9,25... | collective-permute-start | bytes 7077896 | tf_op jit(solution)/shard_map/ppermute | solution.py:41
  9.7 11.1 %collective-permute-start.1 = (bf16[2,96,1024]{2,1,0:T(8,128)(2,1)S(1)}, bf16[2,96,1024]{2,1,0:T(8,128)(2,1)S(1)}, u32[]{:S(2)}, u32[]{:S(2)}) collective-permute-start(bf16[2,96,1024]{2,1,0:T(8,128)(2,1)S(1)} %pad_maximum_fusion), channel_id=1, source_target_pairs={{0,16},{1,9},{2,18},{3,11},{4,20},{5,13},{6,22},{7,15},{8,24},{9,1... | collective-permute-start | bytes 1179656 | tf_op jit(solution)/shard_map/ppermute | solution.py:45
  20.8 11.2 %collective-permute-start.13 = (bf16[2,96,1024]{2,1,0:T(8,128)(2,1)S(1)}, bf16[2,96,1024]{2,1,0:T(8,128)(2,1)S(1)}, u32[]{:S(2)}, u32[]{:S(2)}) collective-permute-start(bf16[2,96,1024]{2,1,0:T(8,128)(2,1)S(1)} %pad_maximum_fusion.4), channel_id=1, source_target_pairs={{0,16},{1,9},{2,18},{3,11},{4,20},{5,13},{6,22},{7,15},{8,24},{9,1... | collective-permute-start | bytes 1179656 | tf_op jit(solution)/shard_map/ppermute | solution.py:45
  21.2 20.1 %collective-permute-start.3 = (bf16[2,48,1024]{2,1,0:T(8,128)(2,1)S(1)}, bf16[2,48,1024]{2,1,0:T(8,128)(2,1)S(1)}, u32[]{:S(2)}, u32[]{:S(2)}) collective-permute-start(bf16[2,48,1024]{2,1,0:T(8,128)(2,1)S(1)} %pad_maximum_fusion.10), channel_id=1, source_target_pairs={{0,4},{1,5},{2,6},{3,7},{4,0},{5,1},{6,2},{7,3},{8,12},{9,13},{10,... | collective-permute-start | bytes 589832 | tf_op jit(solution)/shard_map/ppermute | solution.py:50
  21.4 19.8 %collective-permute-start.2 = (bf16[2,48,1024]{2,1,0:T(8,128)(2,1)S(1)}, bf16[2,48,1024]{2,1,0:T(8,128)(2,1)S(1)}, u32[]{:S(2)}, u32[]{:S(2)}) collective-permute-start(bf16[2,48,1024]{2,1,0:T(8,128)(2,1)S(1)} %pad_maximum_fusion.9), channel_id=1, source_target_pairs={{0,2},{1,3},{2,0},{3,1},{4,6},{5,7},{6,4},{7,5},{8,10},{9,11},{10,... | collective-permute-start | bytes 589832 | tf_op jit(solution)/shard_map/ppermute | solution.py:50
  22.7 18.5 %collective-permute-start.4 = (bf16[2,48,1024]{2,1,0:T(8,128)(2,1)S(1)}, bf16[2,48,1024]{2,1,0:T(8,128)(2,1)S(1)}, u32[]{:S(2)}, u32[]{:S(2)}) collective-permute-start(bf16[2,48,1024]{2,1,0:T(8,128)(2,1)S(1)} %pad_maximum_fusion.11), channel_id=1, source_target_pairs={{0,6},{1,7},{2,4},{3,5},{4,2},{5,3},{6,0},{7,1},{8,14},{9,15},{10,... | collective-permute-start | bytes 589832 | tf_op jit(solution)/shard_map/ppermute | solution.py:50
  24.1 20.8 %copy-start.2 = (bf16[1,512,768]{2,1,0:T(8,128)(2,1)S(1)}, bf16[1,512,768]{2,1,0:T(8,128)(2,1)}, u32[]{:S(2)}) copy-start(bf16[1,512,768]{2,1,0:T(8,128)(2,1)} %gate.3) | copy-start | bytes 2359300
  24.1 20.8 %copy-start.3 = (bf16[1,512,768]{2,1,0:T(8,128)(2,1)S(1)}, bf16[1,512,768]{2,1,0:T(8,128)(2,1)}, u32[]{:S(2)}) copy-start(bf16[1,512,768]{2,1,0:T(8,128)(2,1)} %up.3) | copy-start | bytes 2359300
  41.3 9.2 %collective-permute-start.15 = (bf16[2,48,1024]{2,1,0:T(8,128)(2,1)S(1)}, bf16[2,48,1024]{2,1,0:T(8,128)(2,1)S(1)}, u32[]{:S(2)}, u32[]{:S(2)}) collective-permute-start(bf16[2,48,1024]{2,1,0:T(8,128)(2,1)S(1)} %pad_maximum_fusion.14), channel_id=1, source_target_pairs={{0,4},{1,5},{2,6},{3,7},{4,0},{5,1},{6,2},{7,3},{8,12},{9,13},{10,... | collective-permute-start | bytes 589832 | tf_op jit(solution)/shard_map/ppermute | solution.py:50
  41.3 9.2 %collective-permute-start.14 = (bf16[2,48,1024]{2,1,0:T(8,128)(2,1)S(1)}, bf16[2,48,1024]{2,1,0:T(8,128)(2,1)S(1)}, u32[]{:S(2)}, u32[]{:S(2)}) collective-permute-start(bf16[2,48,1024]{2,1,0:T(8,128)(2,1)S(1)} %pad_maximum_fusion.13), channel_id=1, source_target_pairs={{0,2},{1,3},{2,0},{3,1},{4,6},{5,7},{6,4},{7,5},{8,10},{9,11},{10,... | collective-permute-start | bytes 589832 | tf_op jit(solution)/shard_map/ppermute | solution.py:50
  41.8 16.7 %collective-permute-start.16 = (bf16[2,48,1024]{2,1,0:T(8,128)(2,1)S(1)}, bf16[2,48,1024]{2,1,0:T(8,128)(2,1)S(1)}, u32[]{:S(2)}, u32[]{:S(2)}) collective-permute-start(bf16[2,48,1024]{2,1,0:T(8,128)(2,1)S(1)} %pad_maximum_fusion.15), channel_id=1, source_target_pairs={{0,6},{1,7},{2,4},{3,5},{4,2},{5,3},{6,0},{7,1},{8,14},{9,15},{10,... | collective-permute-start | bytes 589832 | tf_op jit(solution)/shard_map/ppermute | solution.py:50
  44.0 14.5 %copy-start.1 = (bf16[1,768,512]{2,1,0:T(8,128)(2,1)S(1)}, bf16[1,768,512]{2,1,0:T(8,128)(2,1)}, u32[]{:S(2)}) copy-start(bf16[1,768,512]{2,1,0:T(8,128)(2,1)} %refs_4_.3) | copy-start | bytes 2359300
  44.9 17.6 %copy-start = (bf16[4608,256]{1,0:T(8,128)(2,1)}, bf16[4608,256]{1,0:T(8,128)(2,1)S(1)}, u32[]{:S(2)}) copy-start(bf16[4608,256]{1,0:T(8,128)(2,1)S(1)} %collective-permute-done.5.refs_6_.refs_7_.refs_0_.refs_1_.refs_5_.far_gate.far_up) | copy-start | bytes 7077892
  47.1 15.4 %collective-permute-start.6 = (bf16[2,384,768]{2,1,0:T(8,128)(2,1)S(1)}, bf16[2,384,768]{2,1,0:T(8,128)(2,1)S(1)}, u32[]{:S(2)}, u32[]{:S(2)}) collective-permute-start(bf16[2,384,768]{2,1,0:T(8,128)(2,1)S(1)} %get-tuple-element.36), channel_id=1, source_target_pairs={{0,16},{1,9},{2,18},{3,11},{4,20},{5,13},{6,22},{7,15},{8,24},{9,1... | collective-permute-start | bytes 3538952 | tf_op jit(solution)/shard_map/ppermute | solution.py:45
  59.9 9.1 %collective-permute-start.17 = (bf16[384,768]{1,0:T(8,128)(2,1)S(1)}, bf16[384,768]{1,0:T(8,128)(2,1)S(1)}, u32[]{:S(2)}, u32[]{:S(2)}) collective-permute-start(bf16[384,768]{1,0:T(8,128)(2,1)S(1)} %get-tuple-element.44), channel_id=1, source_target_pairs={{0,16},{1,9},{2,18},{3,11},{4,20},{5,13},{6,22},{7,15},{8,24},{9,1... | collective-permute-start | bytes 1769480 | tf_op jit(solution)/shard_map/ppermute | solution.py:45
  75.0 5.1 %collective-permute-start.7 = (bf16[2,48,1024]{2,1,0:T(8,128)(2,1)S(1)}, bf16[2,48,1024]{2,1,0:T(8,128)(2,1)S(1)}, u32[]{:S(2)}, u32[]{:S(2)}) collective-permute-start(bf16[2,48,1024]{2,1,0:T(8,128)(2,1)S(1)} %get-tuple-element.66), channel_id=1, source_target_pairs={{0,2},{1,3},{2,0},{3,1},{4,6},{5,7},{6,4},{7,5},{8,10},{9,11},{10,... | collective-permute-start | bytes 589832 | tf_op jit(solution)/shard_map/ppermute | solution.py:50
  76.2 4.9 %collective-permute-start.9 = (bf16[2,48,1024]{2,1,0:T(8,128)(2,1)S(1)}, bf16[2,48,1024]{2,1,0:T(8,128)(2,1)S(1)}, u32[]{:S(2)}, u32[]{:S(2)}) collective-permute-start(bf16[2,48,1024]{2,1,0:T(8,128)(2,1)S(1)} %get-tuple-element.67), channel_id=1, source_target_pairs={{0,6},{1,7},{2,4},{3,5},{4,2},{5,3},{6,0},{7,1},{8,14},{9,15},{10,... | collective-permute-start | bytes 589832 | tf_op jit(solution)/shard_map/ppermute | solution.py:50
  77.3 15.3 %collective-permute-start.8 = (bf16[2,48,1024]{2,1,0:T(8,128)(2,1)S(1)}, bf16[2,48,1024]{2,1,0:T(8,128)(2,1)S(1)}, u32[]{:S(2)}, u32[]{:S(2)}) collective-permute-start(bf16[2,48,1024]{2,1,0:T(8,128)(2,1)S(1)} %get-tuple-element.68), channel_id=1, source_target_pairs={{0,4},{1,5},{2,6},{3,7},{4,0},{5,1},{6,2},{7,3},{8,12},{9,13},{10,... | collective-permute-start | bytes 589832 | tf_op jit(solution)/shard_map/ppermute | solution.py:50
  78.6 36.6 %collective-permute-start.21 = (bf16[768,512]{1,0:T(8,128)(2,1)S(1)}, bf16[768,512]{1,0:T(8,128)(2,1)S(1)}, u32[]{:S(2)}, u32[]{:S(2)}) collective-permute-start(bf16[768,512]{1,0:T(8,128)(2,1)S(1)} %get-tuple-element.52), channel_id=1, source_target_pairs={{0,8},{1,17},{2,10},{3,19},{4,12},{5,21},{6,14},{7,23},{8,0},{9,25... | collective-permute-start | bytes 2359304 | tf_op jit(solution)/shard_map/ppermute | solution.py:41
  79.7 42.5 %collective-permute-start.23 = (bf16[2,512,768]{2,1,0:T(8,128)(2,1)S(1)}, bf16[2,512,768]{2,1,0:T(8,128)(2,1)S(1)}, u32[]{:S(2)}, u32[]{:S(2)}) collective-permute-start(bf16[2,512,768]{2,1,0:T(8,128)(2,1)S(1)} %get-tuple-element.55), channel_id=1, source_target_pairs={{0,8},{1,17},{2,10},{3,19},{4,12},{5,21},{6,14},{7,23},{8,0},{9,25... | collective-permute-start | bytes 4718600 | tf_op jit(solution)/shard_map/ppermute | solution.py:41
  80.1 16.2 %collective-permute-start.18 = (bf16[2,48,1024]{2,1,0:T(8,128)(2,1)S(1)}, bf16[2,48,1024]{2,1,0:T(8,128)(2,1)S(1)}, u32[]{:S(2)}, u32[]{:S(2)}) collective-permute-start(bf16[2,48,1024]{2,1,0:T(8,128)(2,1)S(1)} %get-tuple-element.49), channel_id=1, source_target_pairs={{0,2},{1,3},{2,0},{3,1},{4,6},{5,7},{6,4},{7,5},{8,10},{9,11},{10,... | collective-permute-start | bytes 589832 | tf_op jit(solution)/shard_map/ppermute | solution.py:50
  81.2 23.9 %collective-permute-start.20 = (bf16[2,48,1024]{2,1,0:T(8,128)(2,1)S(1)}, bf16[2,48,1024]{2,1,0:T(8,128)(2,1)S(1)}, u32[]{:S(2)}, u32[]{:S(2)}) collective-permute-start(bf16[2,48,1024]{2,1,0:T(8,128)(2,1)S(1)} %get-tuple-element.51), channel_id=1, source_target_pairs={{0,6},{1,7},{2,4},{3,5},{4,2},{5,3},{6,0},{7,1},{8,14},{9,15},{10,... | collective-permute-start | bytes 589832 | tf_op jit(solution)/shard_map/ppermute | solution.py:50
  92.8 14.6 %collective-permute-start.19 = (bf16[2,48,1024]{2,1,0:T(8,128)(2,1)S(1)}, bf16[2,48,1024]{2,1,0:T(8,128)(2,1)S(1)}, u32[]{:S(2)}, u32[]{:S(2)}) collective-permute-start(bf16[2,48,1024]{2,1,0:T(8,128)(2,1)S(1)} %get-tuple-element.50), channel_id=1, source_target_pairs={{0,4},{1,5},{2,6},{3,7},{4,0},{5,1},{6,2},{7,3},{8,12},{9,13},{10,... | collective-permute-start | bytes 589832 | tf_op jit(solution)/shard_map/ppermute | solution.py:50
  96.3 11.3 %collective-permute-start.10 = (bf16[4,48,1024]{2,1,0:T(8,128)(2,1)S(1)}, bf16[4,48,1024]{2,1,0:T(8,128)(2,1)S(1)}, u32[]{:S(2)}, u32[]{:S(2)}) collective-permute-start(bf16[4,48,1024]{2,1,0:T(8,128)(2,1)S(1)} %pad_maximum_fusion.2), channel_id=1, source_target_pairs={{0,16},{1,9},{2,18},{3,11},{4,20},{5,13},{6,22},{7,15},{8,24},{9,1... | collective-permute-start | bytes 1179656 | tf_op jit(solution)/shard_map/ppermute | solution.py:45
  107.7 10.3 %collective-permute-start.11 = (bf16[2,96,1024]{2,1,0:T(8,128)(2,1)S(1)}, bf16[2,96,1024]{2,1,0:T(8,128)(2,1)S(1)}, u32[]{:S(2)}, u32[]{:S(2)}) collective-permute-start(bf16[2,96,1024]{2,1,0:T(8,128)(2,1)S(1)} %pad_maximum_fusion.3), channel_id=1, source_target_pairs={{0,1},{1,0},{2,3},{3,2},{4,5},{5,4},{6,7},{7,6},{8,9},{9,8},{10,11... | collective-permute-start | bytes 1179656 | tf_op jit(solution)/shard_map/ppermute | solution.py:50
  115.1 2.8 %copy-start.4 = (bf16[128,192]{1,0:T(8,128)(2,1)S(1)}, bf16[128,192]{1,0:T(8,128)(2,1)}, u32[]{:S(2)}) copy-start(bf16[128,192]{1,0:T(8,128)(2,1)} %get-tuple-element.31.pick) | copy-start | bytes 147460
  115.1 2.8 %copy-start.5 = (f32[128,128]{1,0:T(8,128)S(1)}, f32[128,128]{1,0:T(8,128)}, u32[]{:S(2)}) copy-start(f32[128,128]{1,0:T(8,128)} %get-tuple-element.32.weight) | copy-start | bytes 196612
  115.2 7.0 %collective-permute-start.22 = (bf16[4,48,1024]{2,1,0:T(8,128)(2,1)S(1)}, bf16[4,48,1024]{2,1,0:T(8,128)(2,1)S(1)}, u32[]{:S(2)}, u32[]{:S(2)}) collective-permute-start(bf16[4,48,1024]{2,1,0:T(8,128)(2,1)S(1)} %pad_maximum_fusion.6), channel_id=1, source_target_pairs={{0,16},{1,9},{2,18},{3,11},{4,20},{5,13},{6,22},{7,15},{8,24},{9,1... | collective-permute-start | bytes 1179656 | tf_op jit(solution)/shard_map/ppermute | solution.py:45
  125.2 2.2 %collective-permute-start.24 = (bf16[2,96,1024]{2,1,0:T(8,128)(2,1)S(1)}, bf16[2,96,1024]{2,1,0:T(8,128)(2,1)S(1)}, u32[]{:S(2)}, u32[]{:S(2)}) collective-permute-start(bf16[2,96,1024]{2,1,0:T(8,128)(2,1)S(1)} %pad_maximum_fusion.7), channel_id=1, source_target_pairs={{0,1},{1,0},{2,3},{3,2},{4,5},{5,4},{6,7},{7,6},{8,9},{9,8},{10,11... | collective-permute-start | bytes 1179656 | tf_op jit(solution)/shard_map/ppermute | solution.py:50

commit v3 on v2

v3 whole, which is shorter than its diff:
```python
import functools

import jax
import jax.numpy as jnp
from jax import lax
from jax.experimental import pallas as pl
from jax.experimental.pallas import tpu as pltpu
from jax.sharding import PartitionSpec as P

BOTH = ("dp", "expert")
VMEM_BYTES = 40 * 2**20
F32 = jnp.float32
BF16 = jnp.bfloat16


def contract_last(left_side, right_side):
    return lax.dot_general(
        left_side, right_side, (((1,), (1,)), ((), ())), preferred_element_type=F32
    )


def contract_first(left_side, right_side):
    return lax.dot_general(
        left_side, right_side, (((0,), (0,)), ((), ())), preferred_element_type=F32
    )


def plain_dot(left_side, right_side):
    return jnp.dot(left_side, right_side, preferred_element_type=F32)


def pair_list(experts, masks):
    return [
        (replica * experts + expert, (replica ^ masks[expert % 2]) * experts + expert)
        for replica in range(4)
        for expert in range(experts)
    ]


def swap_weight(value):
    return lax.ppermute(value, BOTH, pair_list(lax.axis_size("expert"), (1, 2)))


def swap_rows(value):
    return lax.ppermute(value, BOTH, pair_list(lax.axis_size("expert"), (2, 1)))


def swap_expert(value, mask):
    experts = lax.axis_size("expert")
    return lax.ppermute(value, "expert", [(i, i ^ mask) for i in range(experts)])


def offset(expert, j):
    side = 1 + (expert & 1)
    return (0, side, 3 - side, 3)[j]


def after(value, *earlier):
    return lax.optimization_barrier((value,) + earlier)[0]


def params(limit=VMEM_BYTES):
    return pltpu.CompilerParams(vmem_limit_bytes=limit)


def cost(microseconds):
    return pl.CostEstimate(
        flops=int(microseconds * 1e9), bytes_accessed=int(microseconds * 3e6), transcendentals=0
    )


def whole(shape):
    return pl.BlockSpec(shape, lambda *_: (0,) * len(shape))


def choose(experts, capacity, route, fixed):
    chips = experts // 2
    tokens = route.shape[1]
    routes = route[...]
    expert = lax.axis_index("expert")
    expert_row = lax.broadcasted_iota(jnp.int32, (experts, tokens), 0)
    one_hot = jnp.where(expert_row == routes, 1.0, 0.0)
    earlier = jnp.where(
        lax.broadcasted_iota(jnp.int32, (tokens, tokens), 0)
        < lax.broadcasted_iota(jnp.int32, (tokens, tokens), 1),
        1.0,
        0.0,
    )
    before = plain_dot(one_hot.astype(BF16), earlier.astype(BF16))
    position = jnp.sum(before * one_hot, axis=0, keepdims=True).astype(jnp.int32)
    relative = routes ^ expert
    slot = ((relative & 1) * chips + (relative >> 1)) * capacity + position
    rows = experts * capacity
    chosen = jnp.where(lax.broadcasted_iota(jnp.int32, (rows, tokens), 0) == slot, 1.0, 0.0)
    return chosen, fixed[...].astype(F32) / 65536.0


def fill(chosen, scale, source, *outs):
    half_rows = chosen.shape[0] // 2
    block = source.shape[1] // 4
    replica, expert = lax.axis_index("dp"), lax.axis_index("expert")
    chosen = chosen.astype(BF16)
    for core, out in enumerate(outs):
        part = chosen[core * half_rows : (core + 1) * half_rows]
        for j in range(4):
            start = pl.multiple_of((replica ^ offset(expert + core, j)) * block, block)
            value = plain_dot(part, source[:, pl.ds(start, block)])
            if scale is not None:
                value = scale[core * half_rows : (core + 1) * half_rows] * value
            out[j // 2, :, pl.ds((j % 2) * block, block)] = value.astype(BF16)


def slot_kernel(experts, capacity, tok, route, fixed, own, other):
    chosen, _ = choose(experts, capacity, route, fixed)
    fill(chosen, None, tok, own, other)


def grad_kernel(experts, capacity, cot, route, fixed, own, other, pick, weight):
    chosen, route_weight = choose(experts, capacity, route, fixed)
    tokens = cot.shape[0]
    pick[...] = jnp.transpose(chosen).astype(BF16)
    weight[...] = jnp.transpose(jnp.broadcast_to(route_weight, (tokens, tokens)))
    fill(chosen, jnp.sum(chosen * route_weight, axis=1, keepdims=True), cot, own, other)


def make_slots(tokens, routes, gate_fixed, experts, capacity):
    count, width = tokens.shape
    slot_shape = jax.ShapeDtypeStruct((2, experts * capacity // 2, width // 2), BF16)
    return pl.pallas_call(
        functools.partial(slot_kernel, experts, capacity),
        out_shape=[slot_shape] * 2,
        compiler_params=params(60 * 2**20),
        cost_estimate=cost(0.01),
        name="make_slots",
    )(tokens, routes.reshape(1, count), gate_fixed.reshape(1, count))


def make_grads(cotangent, routes, gate_fixed, experts, capacity):
    count, width = cotangent.shape
    slot_shape = jax.ShapeDtypeStruct((2, experts * capacity // 2, width // 2), BF16)
    return pl.pallas_call(
        functools.partial(grad_kernel, experts, capacity),
        out_shape=[slot_shape] * 2
        + [
            jax.ShapeDtypeStruct((count, experts * capacity), BF16),
            jax.ShapeDtypeStruct((count, count), F32),
        ],
        compiler_params=params(60 * 2**20),
        cost_estimate=cost(0.01),
        name="make_grads",
    )(cotangent, routes.reshape(1, count), gate_fixed.reshape(1, count))


def gather_rows(parts, places, out):
    for part, blocks in zip(parts, places):
        step = part.shape[1]
        for i, block in enumerate(blocks):
            out[pl.ds(block * step, step), :] = part[i]


def spread_rows(value, parts, places):
    for part, blocks in zip(parts, places):
        step = part.shape[1]
        for i, block in enumerate(blocks):
            part[i] = value[block * step : (block + 1) * step].astype(BF16)


def row_count(parts):
    return sum(part.shape[0] * part.shape[1] for part in parts)


def part_shapes(rows, width, places):
    step = rows // sum(len(blocks) for blocks in places)
    return [(len(blocks), step, width) for blocks in places]


def add_swapped(own, got):
    rows = own.shape[0] // 2
    return own + jnp.concatenate([got[rows:], got[:rows]], axis=0).astype(F32)


def gate_up_kernel(places, *refs):
    count = len(places)
    parts, (gate, up, far_gate, far_up, rows, own, send) = refs[:count], refs[count:]

    @pl.when(pl.program_id(0) == 0)
    def _():
        gather_rows(parts, places, rows)

    block = gate.shape[1]
    near_x, far_x = rows[:, :block], rows[:, block:]
    for k, (near_w, far_w) in enumerate(((gate, far_gate), (up, far_up))):
        part = plain_dot(near_x, near_w[0]) + plain_dot(far_x, far_w[0])
        own[k] = part
        send[k] = part.astype(BF16)


def gate_up_parts(parts, places, w_gate, w_up, far_gate, far_up, tile):
    rows, half = row_count(parts), parts[0].shape[-1]
    _, block, hidden = w_gate.shape
    near = pl.BlockSpec((1, block, tile), lambda j: (0, 0, j))
    part = pl.BlockSpec((2, rows, tile), lambda j: (0, 0, j))
    return pl.pallas_call(
        functools.partial(gate_up_kernel, places),
        grid=(hidden // tile,),
        in_specs=[whole(part.shape) for part in parts]
        + [
            near,
            near,
            near,
            near,
        ],
        out_specs=[whole((rows, half)), part, part],
        out_shape=[
            jax.ShapeDtypeStruct((rows, half), BF16),
            jax.ShapeDtypeStruct((2, rows, hidden), F32),
            jax.ShapeDtypeStruct((2, rows, hidden), BF16),
        ],
        compiler_params=params(),
        cost_estimate=cost(0.01),
        name="gate_up_parts",
    )(*parts, w_gate, w_up, far_gate, far_up)


def grad_hidden_kernel(places, *refs):
    count = len(places)
    parts, (down, far_down, rows, own, send) = refs[:count], refs[count:]

    @pl.when(pl.program_id(0) == 0)
    def _():
        gather_rows(parts, places, rows)

    block = down.shape[2]
    part = contract_last(rows[:, :block], down[0]) + contract_last(rows[:, block:], far_down[0])
    own[...] = part
    send[...] = part.astype(BF16)


def grad_hidden_parts(parts, places, w_down, far_down, tile):
    rows, half = row_count(parts), parts[0].shape[-1]
    _, hidden, block = w_down.shape
    part = pl.BlockSpec((rows, tile), lambda j: (0, j))
    near = pl.BlockSpec((1, tile, block), lambda j: (0, j, 0))
    return pl.pallas_call(
        functools.partial(grad_hidden_kernel, places),
        grid=(hidden // tile,),
        in_specs=[whole(part.shape) for part in parts]
        + [
            near,
            near,
        ],
        out_specs=[whole((rows, half)), part, part],
        out_shape=[
            jax.ShapeDtypeStruct((rows, half), BF16),
            jax.ShapeDtypeStruct((rows, hidden), F32),
            jax.ShapeDtypeStruct((rows, hidden), BF16),
        ],
        compiler_params=params(),
        cost_estimate=cost(1),
        name="grad_hidden_parts",
    )(*parts, w_down, far_down)


def slot_out_kernel(places, own, got, down, far_down, grad_rows, hidden, far_grad, *refs):
    *out, total = refs
    step = pl.program_id(0)
    block = down.shape[2]
    gate_pre = add_swapped(own[0], got[0])
    up_pre = add_swapped(own[1], got[1])
    value = (gate_pre * jax.nn.sigmoid(gate_pre) * up_pre).astype(BF16)
    hidden[...] = value

    @pl.when(step == 0)
    def _():
        total[...] = jnp.zeros_like(total)

    total[:, :block] += plain_dot(value, down[0])
    total[:, block:] += plain_dot(value, far_down[0])
    far_grad[...] = contract_first(value, grad_rows[:, block:]).astype(BF16)

    @pl.when(step == pl.num_programs(0) - 1)
    def _():
        spread_rows(total[...], out, places)


def slot_out_parts(own, got, w_down, far_down, y, tile, places):
    _, rows, hidden = own.shape
    block = w_down.shape[2]
    part = pl.BlockSpec((2, rows, tile), lambda j: (0, 0, j))
    shapes = part_shapes(rows, 2 * block, places)
    near = pl.BlockSpec((1, tile, block), lambda j: (0, j, 0))
    return pl.pallas_call(
        functools.partial(slot_out_kernel, places),
        grid=(hidden // tile,),
        in_specs=[
            part,
            part,
            near,
            near,
            whole(y.shape),
        ],
        out_specs=[
            pl.BlockSpec((rows, tile), lambda j: (0, j)),
            pl.BlockSpec((tile, block), lambda j: (j, 0)),
        ]
        + [whole(shape) for shape in shapes],
        out_shape=[
            jax.ShapeDtypeStruct((rows, hidden), BF16),
            jax.ShapeDtypeStruct((hidden, block), BF16),
        ]
        + [jax.ShapeDtypeStruct(shape, BF16) for shape in shapes],
        scratch_shapes=[pltpu.VMEM((rows, 2 * block), F32)],
        compiler_params=params(),
        cost_estimate=cost(0.01),
        name="slot_out",
    )(own, got, w_down, far_down, y)


def slot_grad_kernel(
    places, own, got, own_grad, got_grad, gate, up, far_gate, far_up, rows,
    grads, far_grads, *refs,
):
    *out, total = refs
    step = pl.program_id(0)
    block = gate.shape[1]
    gate_pre = add_swapped(own[0], got[0])
    up_pre = add_swapped(own[1], got[1])
    grad_hidden = add_swapped(own_grad[...], got_grad[...])
    sigmoid_gate = jax.nn.sigmoid(gate_pre)
    grad_gate = (
        grad_hidden * up_pre * sigmoid_gate * (1.0 + gate_pre * (1.0 - sigmoid_gate))
    ).astype(BF16)
    grad_up = (grad_hidden * gate_pre * sigmoid_gate).astype(BF16)
    grads[0] = grad_gate
    grads[1] = grad_up
    far_grads[0] = contract_first(rows[:, block:], grad_gate).astype(BF16)
    far_grads[1] = contract_first(rows[:, block:], grad_up).astype(BF16)

    @pl.when(step == 0)
    def _():
        total[...] = jnp.zeros_like(total)

    total[:, :block] += contract_last(grad_gate, gate[0]) + contract_last(grad_up, up[0])
    total[:, block:] += contract_last(grad_gate, far_gate[0]) + contract_last(
        grad_up, far_up[0]
    )

    @pl.when(step == pl.num_programs(0) - 1)
    def _():
        spread_rows(total[...], out, places)


def slot_grad_parts(own, got, own_grad, got_grad, w_gate, w_up, far_gate, far_up, x, tile, places):
    _, rows, hidden = own.shape
    block = w_gate.shape[1]
    part = pl.BlockSpec((2, rows, tile), lambda j: (0, 0, j))
    near = pl.BlockSpec((1, block, tile), lambda j: (0, 0, j))
    grad_part = pl.BlockSpec((rows, tile), lambda j: (0, j))
    shapes = part_shapes(rows, 2 * block, places)
    return pl.pallas_call(
        functools.partial(slot_grad_kernel, places),
        grid=(hidden // tile,),
        in_specs=[
            part,
            part,
            grad_part,
            grad_part,
            near,
            near,
            near,
            near,
            whole(x.shape),
        ],
        out_specs=[
            part,
            pl.BlockSpec((2, block, tile), lambda j: (0, 0, j)),
        ]
        + [whole(shape) for shape in shapes],
        out_shape=[
            jax.ShapeDtypeStruct((2, rows, hidden), BF16),
            jax.ShapeDtypeStruct((2, block, hidden), BF16),
        ]
        + [jax.ShapeDtypeStruct(shape, BF16) for shape in shapes],
        scratch_shapes=[pltpu.VMEM((rows, 2 * block), F32)],
        compiler_params=params(),
        cost_estimate=cost(0),
        name="slot_grad",
    )(own, got, own_grad, got_grad, w_gate, w_up, far_gate, far_up, x)


def unslot_kernel(weighted, pick, weight, near, far, other, out):
    half_rows, half = near.shape
    block = half // 2
    replica, expert = lax.axis_index("dp"), lax.axis_index("expert")
    for j in range(4):
        start = pl.multiple_of((replica ^ offset(expert, j)) * block, block)
        own = (near if j < 2 else far)[:, pl.ds((j % 2) * block, block)]
        k = (0, 2, 1, 3)[j]
        rest = other[k // 2, :, pl.ds((k % 2) * block, block)]
        value = plain_dot(pick[:, :half_rows], own) + plain_dot(pick[:, half_rows:], rest)
        if weighted:
            value = weight[:, :1] * value
        out[:, pl.ds(start, block)] = value.astype(BF16)


def unslot(pick, weight, near, far, other, weighted):
    count = pick.shape[0]
    half_rows, half = near.shape
    return pl.pallas_call(
        functools.partial(unslot_kernel, weighted),
        out_shape=jax.ShapeDtypeStruct((count, 2 * half), BF16),
        compiler_params=params(),
        cost_estimate=cost(0.01),
        name="unslot",
    )(pick, weight, near, far, other)


def swap_chips(parts, chips, *earlier):
    got = list(parts)
    for first in range(0, len(parts), chips):
        for k in range(1, chips):
            got[first + k] = swap_expert(after(parts[first + k], *earlier), 2 * k)
    return got


def send_slots(slots, others, chips, capacity, apart, before_rows, before_near, before_far):
    half = slots.shape[-1]
    other = swap_expert(others, 1)
    far = swap_rows(after(jnp.stack([slots[1], other[1]], axis=0), *before_rows))

    def by_chip(own, rest):
        shape = (chips, 1, capacity, half)
        both = jnp.concatenate([own.reshape(shape), rest.reshape(shape)], axis=1)
        return [both[k].reshape(1, 2 * capacity, half) for k in range(chips)]

    near_parts, far_parts = by_chip(slots[0], other[0]), by_chip(far[0], far[1])
    if apart:
        near_parts = swap_chips(near_parts, chips, *before_near)
        return far, near_parts + swap_chips(far_parts, chips, *before_far)
    parts = [jnp.concatenate(pair, axis=0) for pair in zip(near_parts, far_parts)]
    return far, swap_chips(parts, chips, *before_near)


def return_slots(parts, chips, capacity, before_rows, before_core):
    half = parts[0].shape[-1]
    if len(parts) == chips:
        parts = [part[:1] for part in parts] + [part[1:] for part in parts]
    shape = (chips, 2, capacity, half)
    far = swap_rows(after(jnp.concatenate(parts[chips:], axis=0), *before_rows)).reshape(shape)
    near = jnp.concatenate(parts[:chips], axis=0).reshape(shape)
    rows = chips * capacity
    other = jnp.stack([near[:, 1].reshape(rows, half), far[:, 1].reshape(rows, half)], axis=0)
    other = swap_expert(after(other, *before_core), 1)
    return near[:, 0].reshape(rows, half), far[:, 0].reshape(rows, half), other


def body(tokens, cotangent, routes, gate_fixed, w_gate, w_up, w_down):
    tok_count, model_width = tokens.shape
    hidden_width = w_gate.shape[2]
    experts = lax.axis_size("expert")
    chips = experts // 2
    capacity = 3 * tok_count // (2 * experts)
    block = model_width // 4
    tile = 256 if hidden_width % 256 == 0 else hidden_width
    far_gate = swap_weight(w_gate)
    slots, others = make_slots(tokens, routes, gate_fixed, experts, capacity)
    grad_slots, grad_others, pick, weight = make_grads(
        cotangent, routes, gate_fixed, experts, capacity
    )
    far, got_parts = send_slots(
        slots, others, chips, capacity, True, (), (), ()
    )
    far_up = swap_weight(w_up)
    far_down = swap_weight(after(w_down, *(far,)))
    grad_far, got_grad_parts = send_slots(
        grad_slots, grad_others, chips, capacity, False, (far_up,), got_parts, got_parts
    )
    if (2 * capacity) % 16 == 0:
        apart = tuple((k,) for k in range(2 * chips))
        paired = tuple((k, k + chips) for k in range(chips))
    else:
        apart = paired = ((0,),)

    def joined(parts):
        if apart != paired:
            return parts
        if len(parts) == chips:
            parts = [part[:1] for part in parts] + [part[1:] for part in parts]
        return [jnp.concatenate(parts, axis=1)]

    def cut(parts):
        if apart != paired:
            return parts
        return jnp.split(parts[0], 2 * chips, axis=1)

    rows, own, send = gate_up_parts(
        joined(got_parts), apart, w_gate, w_up, far_gate, far_up, tile
    )
    got = swap_rows(send)
    grad_rows, own_grad, send_grad = grad_hidden_parts(
        joined(got_grad_parts), paired, after(w_down, *(send,)), far_down, tile
    )
    got_grad = swap_rows(send_grad)

    hidden, far_grad_down, *slot_out = slot_out_parts(
        own, got, w_down, far_down, grad_rows, tile, paired
    )
    out_parts = swap_chips(cut(slot_out), chips)
    sent = [part for k, part in enumerate(out_parts) if k % chips]
    got_down = swap_weight(far_grad_down)
    grads, far_grads, *slot_grad = slot_grad_parts(
        own,
        got,
        own_grad,
        after(got_grad, *(hidden,)),
        w_gate,
        w_up,
        far_gate,
        far_up,
        rows,
        tile,
        paired,
    )
    grad_out_parts = swap_chips(cut(slot_grad), chips, *sent)
    got_far = swap_weight(after(far_grads, *sent[:1]))

    grad_w_gate = contract_first(rows[:, :block], grads[0]) + got_far[0].astype(F32)
    grad_w_up = contract_first(rows[:, :block], grads[1]) + got_far[1].astype(F32)
    grad_w_down = contract_first(hidden, grad_rows[:, :block]) + got_down.astype(F32)
    grad_w_gate, grad_w_up, grad_w_down = (
        value.astype(BF16)[None] for value in (grad_w_gate, grad_w_up, grad_w_down)
    )

    back = return_slots(out_parts, chips, capacity, (slot_grad[0],), ())
    mixed = unslot(pick, weight, *back, True)
    grad_back = return_slots(grad_out_parts, chips, capacity, (got_down,), (mixed, grad_w_gate, grad_w_up, grad_w_down))
    grad_tokens = unslot(pick, weight, *grad_back, False)
    return (
        mixed,
        grad_tokens,
        grad_w_gate,
        grad_w_up,
        grad_w_down,
    )


def solution(mesh):
    return jax.shard_map(
        body,
        mesh=mesh,
        in_specs=(
            P(("dp", "expert"), None),
            P(("dp", "expert"), None),
            P(("dp", "expert"), None),
            P(("dp", "expert"), None),
            P("expert", "dp", None),
            P("expert", "dp", None),
            P("expert", None, "dp"),
        ),
        out_specs=(
            P(("dp", "expert"), None),
            P(("dp", "expert"), None),
            P("expert", "dp", None),
            P("expert", "dp", None),
            P("expert", None, "dp"),
        ),
        check_vma=False,
    )
```

time: 131 us -> 115 us (0.88); the launches traced: 129 us -> 115 us
  waiting for transfers between devices: 69.7 us -> 63 us
  starting transfers between devices: 31.6 us -> 25.5 us
    ppermute x6, waiting for transfers between devices: 27.4 us -> 12.1 us  [swap_rows(): return lax.ppermute(value, BOTH, pair_list(lax.axis_size('expert'), (2, 1)))]
    ppermute x16 -> x19, starting transfers between devices: 24.1 us -> 15.9 us  [swap_expert(): lax.ppermute(value, 'expert', [(i, i ^ mask) for i in range(experts)])]
    ppermute x3 -> x5, waiting for transfers between devices: 0.92 us -> 7.55 us  [swap_weight(): return lax.ppermute(value, BOTH, pair_list(lax.axis_size('expert'), (1, 2)))]
    pallas_call x1, Pallas kernels: 4.61 us -> 2.34 us  [make_slots(): pl.pallas_call(functools.partial(slot_kernel, experts, capacity), out_sha...]
    squeeze x4 -> x0, local copies, waits for them, and re-layouts: 2.26 us -> none  [the longest x2 2.16 us: send_slots(): other = swap_expert(slots[1], 1)]
    ppermute x3 -> x5, starting transfers between devices: 2.77 us -> 4.82 us  [swap_weight(): return lax.ppermute(value, BOTH, pair_list(lax.axis_size('expert'), (1, 2)))]
    slice x13 -> x14, local copies, waits for them, and re-layouts: 0.27 us -> 2.32 us  [the longest x1 1.05 us: send_slots(): slots[1]]
    ppermute x16 -> x19, waiting for transfers between devices: 41.4 us -> 43.3 us  [swap_expert(): lax.ppermute(value, 'expert', [(i, i ^ mask) for i in range(experts)])]
  transfers between devices with their start and end apart: 25 -> 30, of which waited for: 14 -> 14; matrix products, arithmetic and copies ran while one was open for 3% -> 4% of each run, Pallas kernels for 5% -> 12%
where the time goes in v3:
time: 115 us
  waiting for transfers between devices  63 us (55%)
  starting transfers between devices  25.5 us (22%)
  Pallas kernels  18 us (16%)
  matrix products  4.45 us (4%)
  local copies, waits for them, and re-layouts  2.45 us (2%)
    ppermute x19, waiting for transfers between devices, swap_expert(): lax.ppermute(value, 'expert', [(i, i ^ mask) for i in range(experts)])  43.3 us
    ppermute x19, starting transfers between devices, swap_expert(): lax.ppermute(value, 'expert', [(i, i ^ mask) for i in range(experts)])  15.9 us
    ppermute x6, waiting for transfers between devices, swap_rows(): return lax.ppermute(value, BOTH, pair_list(lax.axis_size('expert'), (2, 1)))  12.1 us
    ppermute x5, waiting for transfers between devices, swap_weight(): return lax.ppermute(value, BOTH, pair_list(lax.axis_size('expert'), (1, 2)))  7.55 us
    ppermute x5, starting transfers between devices, swap_weight(): return lax.ppermute(value, BOTH, pair_list(lax.axis_size('expert'), (1, 2)))  4.82 us
    ppermute x6, starting transfers between devices, swap_rows(): return lax.ppermute(value, BOTH, pair_list(lax.axis_size('expert'), (2, 1)))  4.81 us
    pallas_call x1, Pallas kernels, slot_grad_parts(): pl.pallas_call(functools.partial(slot_grad_kernel, places), grid=(hidden...  4.62 us
    dot_general x3, matrix products, contract_first(): lax.dot_general(left_side, right_side, (((0,), (0,)), ((), ())), preferre...  4.45 us
  transfers between devices with their start and end apart: 30, of which 14 were waited for; matrix products, arithmetic and copies ran while one was open for 4% of the time, Pallas kernels for 12%

profile of v3, /device:TPU:19, one launch (start us, length us, event | category | flops | bytes accessed | tf_op | source)
XLA Modules:
  0.0 114.9 jit_solution(17371643114929988903)
XLA Ops:
  0.6 2.4 %make_grads.1 = (bf16[2,96,1024]{2,1,0:T(8,128)(2,1)}, bf16[2,96,1024]{2,1,0:T(8,128)(2,1)}, bf16[128,192]{1,0:T(8,128)(2,1)}, f32[128,128]{1,0:T(8,128)}) custom-call(bf16[128,2048]{1,0:T(8,128)(2,1)} %cot.1, s32[1,128]{1,0:T(1,128)} %bitcast.129, s32[1,128]{1,0:T(1,128)} %bitcast.131), custom_call_target="tpu_custom_call" | custom-call | flops 10000000 | bytes 30000 | tf_op jit(solution)/shard_map/make_grads/pallas_call | solution.py:141
  3.0 0.7 collective-permute-start.12
  3.7 1.2 %collective-permute-start.9 = (bf16[1,512,768]{2,1,0:T(8,128)(2,1)}, bf16[1,512,768]{2,1,0:T(8,128)(2,1)S(1)}, u32[]{:S(2)}, u32[]{:S(2)}) collective-permute-start(bf16[1,512,768]{2,1,0:T(8,128)(2,1)} %up.1), channel_id=1, source_target_pairs={{0,8},{1,17},{2,10},{3,19},{4,12},{5,21},{6,14},{7,23},{8,0},{9,25... | collective-permute-start | bytes 2359304 | tf_op jit(solution)/shard_map/ppermute | solution.py:41
  4.9 2.3 %make_slots.1 = (bf16[2,96,1024]{2,1,0:T(8,128)(2,1)}, bf16[2,96,1024]{2,1,0:T(8,128)(2,1)}) custom-call(bf16[128,2048]{1,0:T(8,128)(2,1)} %tok.1, s32[1,128]{1,0:T(1,128)} %bitcast.130, s32[1,128]{1,0:T(1,128)} %bitcast.132), custom_call_target="tpu_custom_call" | custom-call | flops 10000000 | bytes 30000 | tf_op jit(solution)/shard_map/make_slots/pallas_call | solution.py:129
  7.3 0.5 collective-permute-start.8
  7.8 1.0 fusion.29
  8.9 1.1 fusion.32
  10.0 1.3 %collective-permute-start.4 = (bf16[2,96,1024]{2,1,0:T(8,128)(2,1)S(1)}, bf16[2,96,1024]{2,1,0:T(8,128)(2,1)S(1)}, u32[]{:S(2)}, u32[]{:S(2)}) collective-permute-start(bf16[2,96,1024]{2,1,0:T(8,128)(2,1)S(1)} %pad_maximum_fusion), channel_id=1, source_target_pairs={{0,16},{1,9},{2,18},{3,11},{4,20},{5,13},{6,22},{7,15},{8,24},{9,1... | collective-permute-start | bytes 1179656 | tf_op jit(solution)/shard_map/ppermute | solution.py:45
  11.3 1.3 %collective-permute-start.1 = (bf16[1,48,1024]{2,1,0:T(8,128)(2,1)S(1)}, bf16[1,48,1024]{2,1,0:T(8,128)(2,1)S(1)}, u32[]{:S(2)}, u32[]{:S(2)}) collective-permute-start(bf16[1,48,1024]{2,1,0:T(8,128)(2,1)S(1)} %bitcast.125), channel_id=1, source_target_pairs={{0,2},{1,3},{2,0},{3,1},{4,6},{5,7},{6,4},{7,5},{8,10},{9,11},{10,... | collective-permute-start | bytes 294920 | tf_op jit(solution)/shard_map/ppermute | solution.py:50
  12.8 3.4 %collective-permute-done.9.refs_11_.far_up = bf16[1,512,768]{2,1,0:T(8,128)(2,1)S(1)} collective-permute-done((bf16[1,512,768]{2,1,0:T(8,128)(2,1)}, bf16[1,512,768]{2,1,0:T(8,128)(2,1)S(1)}, u32[]{:S(2)}, u32[]{:S(2)}) %collective-permute-start.9) | collective-permute-done | bytes 786464 | tf_op jit(solution)/shard_map/ppermute | solution.py:41
  16.4 4.8 %collective-permute-done.4 = bf16[2,96,1024]{2,1,0:T(8,128)(2,1)S(1)} collective-permute-done((bf16[2,96,1024]{2,1,0:T(8,128)(2,1)S(1)}, bf16[2,96,1024]{2,1,0:T(8,128)(2,1)S(1)}, u32[]{:S(2)}, u32[]{:S(2)}) %collective-permute-start.4) | collective-permute-done | bytes 393248 | tf_op jit(solution)/shard_map/ppermute | solution.py:45
  21.3 1.2 %collective-permute-start.13 = (bf16[2,96,1024]{2,1,0:T(8,128)(2,1)S(1)}, bf16[2,96,1024]{2,1,0:T(8,128)(2,1)S(1)}, u32[]{:S(2)}, u32[]{:S(2)}) collective-permute-start(bf16[2,96,1024]{2,1,0:T(8,128)(2,1)S(1)} %pad_maximum_fusion.1), channel_id=1, source_target_pairs={{0,16},{1,9},{2,18},{3,11},{4,20},{5,13},{6,22},{7,15},{8,24},{9,1... | collective-permute-start | bytes 1179656 | tf_op jit(solution)/shard_map/ppermute | solution.py:45
  22.6 1.3 %collective-permute-start.5 = (bf16[1,48,1024]{2,1,0:T(8,128)(2,1)S(1)}, bf16[1,48,1024]{2,1,0:T(8,128)(2,1)S(1)}, u32[]{:S(2)}, u32[]{:S(2)}) collective-permute-start(bf16[1,48,1024]{2,1,0:T(8,128)(2,1)S(1)} %bitcast.128), channel_id=1, source_target_pairs={{0,2},{1,3},{2,0},{3,1},{4,6},{5,7},{6,4},{7,5},{8,10},{9,11},{10,... | collective-permute-start | bytes 294920 | tf_op jit(solution)/shard_map/ppermute | solution.py:50
  24.0 1.3 %collective-permute-start.7 = (bf16[1,48,1024]{2,1,0:T(8,128)(2,1)S(1)}, bf16[1,48,1024]{2,1,0:T(8,128)(2,1)S(1)}, u32[]{:S(2)}, u32[]{:S(2)}) collective-permute-start(bf16[1,48,1024]{2,1,0:T(8,128)(2,1)S(1)} %bitcast.126), channel_id=1, source_target_pairs={{0,6},{1,7},{2,4},{3,5},{4,2},{5,3},{6,0},{7,1},{8,14},{9,15},{10,... | collective-permute-start | bytes 294920 | tf_op jit(solution)/shard_map/ppermute | solution.py:50
  25.3 4.1 %collective-permute-done.8.refs_10_.far_gate = bf16[1,512,768]{2,1,0:T(8,128)(2,1)S(1)} collective-permute-done((bf16[1,512,768]{2,1,0:T(8,128)(2,1)}, bf16[1,512,768]{2,1,0:T(8,128)(2,1)S(1)}, u32[]{:S(2)}, u32[]{:S(2)}) %collective-permute-start.8) | collective-permute-done | bytes 786464 | tf_op jit(solution)/shard_map/ppermute | solution.py:41
  29.5 1.5 %collective-permute-start.11 = (bf16[1,768,512]{2,1,0:T(8,128)(2,1)S(1)}, bf16[1,768,512]{2,1,0:T(8,128)(2,1)S(1)}, u32[]{:S(2)}, u32[]{:S(2)}) collective-permute-start(bf16[1,768,512]{2,1,0:T(8,128)(2,1)S(1)} %copy-done.2), channel_id=1, source_target_pairs={{0,8},{1,17},{2,10},{3,19},{4,12},{5,21},{6,14},{7,23},{8,0},{9,25... | collective-permute-start | bytes 2359304 | tf_op jit(solution)/shard_map/ppermute | solution.py:41
  31.0 2.1 %collective-permute-done.7.refs_7_ = bf16[1,48,1024]{2,1,0:T(8,128)(2,1)S(1)} collective-permute-done((bf16[1,48,1024]{2,1,0:T(8,128)(2,1)S(1)}, bf16[1,48,1024]{2,1,0:T(8,128)(2,1)S(1)}, u32[]{:S(2)}, u32[]{:S(2)}) %collective-permute-start.7) | collective-permute-done | bytes 98336 | tf_op jit(solution)/shard_map/ppermute | solution.py:50
  33.1 2.3 %gate_up_parts.1 = (bf16[384,1024]{1,0:T(8,128)(2,1)S(1)}, f32[2,384,768]{2,1,0:T(8,128)S(1)}, bf16[2,384,768]{2,1,0:T(8,128)(2,1)S(1)}) custom-call(bf16[1,48,1024]{2,1,0:T(8,128)(2,1)S(1)} %bitcast.97, bf16[1,48,1024]{2,1,0:T(8,128)(2,1)S(1)} %collective-permute-done.1.refs_1_, bf16[1,48,1024]{2,1,0:T(8,128)(2,1)S(1)} %collective-permute-done.2.refs_2_, ...), custom_call_target="tpu_custom_call" | custom-call | flops 10000000 | bytes 30000 | tf_op jit(solution)/shard_map/gate_up_parts/pallas_call | solution.py:203
  35.7 0.6 collective-permute-start.16
  36.3 0.8 collective-permute-start.15
  37.1 1.5 %collective-permute-start.14 = (bf16[2,48,1024]{2,1,0:T(8,128)(2,1)S(1)}, bf16[2,48,1024]{2,1,0:T(8,128)(2,1)S(1)}, u32[]{:S(2)}, u32[]{:S(2)}) collective-permute-start(bf16[2,48,1024]{2,1,0:T(8,128)(2,1)S(1)} %pad_maximum_fusion.9), channel_id=1, source_target_pairs={{0,2},{1,3},{2,0},{3,1},{4,6},{5,7},{6,4},{7,5},{8,10},{9,11},{10,... | collective-permute-start | bytes 589832 | tf_op jit(solution)/shard_map/ppermute | solution.py:50
  38.6 12.2 %collective-permute-done.16.refs_3_ = bf16[2,48,1024]{2,1,0:T(8,128)(2,1)S(1)} collective-permute-done((bf16[2,48,1024]{2,1,0:T(8,128)(2,1)S(1)}, bf16[2,48,1024]{2,1,0:T(8,128)(2,1)S(1)}, u32[]{:S(2)}, u32[]{:S(2)}) %collective-permute-start.16) | collective-permute-done | bytes 196640 | tf_op jit(solution)/shard_map/ppermute | solution.py:50
  50.8 2.7 %collective-permute-done.15.refs_2_ = bf16[2,48,1024]{2,1,0:T(8,128)(2,1)S(1)} collective-permute-done((bf16[2,48,1024]{2,1,0:T(8,128)(2,1)S(1)}, bf16[2,48,1024]{2,1,0:T(8,128)(2,1)S(1)}, u32[]{:S(2)}, u32[]{:S(2)}) %collective-permute-start.15) | collective-permute-done | bytes 196640 | tf_op jit(solution)/shard_map/ppermute | solution.py:50
  53.5 1.4 %grad_hidden_parts.1 = (bf16[384,1024]{1,0:T(8,128)(2,1)S(1)}, f32[384,768]{1,0:T(8,128)S(1)}, bf16[384,768]{1,0:T(8,128)(2,1)S(1)}) custom-call(bf16[2,48,1024]{2,1,0:T(8,128)(2,1)S(1)} %pad_maximum_fusion.8.refs_0_, bf16[2,48,1024]{2,1,0:T(8,128)(2,1)S(1)} %collective-permute-done.14.refs_1_, bf16[2,48,1024]{2,1,0:T(8,128)(2,1)S(1)} %collective-permute-done.15.refs_2_, ...), custom_call_target="tpu_custom_call" | custom-call | flops 1000000000 | bytes 3000000 | tf_op jit(solution)/shard_map/grad_hidden_parts/pallas_call | solution.py:244
  54.9 1.3 %collective-permute-start.20 = (bf16[384,768]{1,0:T(8,128)(2,1)S(1)}, bf16[384,768]{1,0:T(8,128)(2,1)S(1)}, u32[]{:S(2)}, u32[]{:S(2)}) collective-permute-start(bf16[384,768]{1,0:T(8,128)(2,1)S(1)} %get-tuple-element.63), channel_id=1, source_target_pairs={{0,16},{1,9},{2,18},{3,11},{4,20},{5,13},{6,22},{7,15},{8,24},{9,1... | collective-permute-start | bytes 1769480 | tf_op jit(solution)/shard_map/ppermute | solution.py:45
  56.5 2.4 %slot_out.1 = (bf16[384,768]{1,0:T(8,128)(2,1)S(1)}, bf16[768,512]{1,0:T(8,128)(2,1)S(1)}, bf16[2,48,1024]{2,1,0:T(8,128)(2,1)S(1)}, bf16[2,48,1024]{2,1,0:T(8,1...) custom-call(f32[2,384,768]{2,1,0:T(8,128)S(1)} %get-tuple-element.47.own, ...), custom_call_target="tpu_custom_call" | custom-call | flops 10000000 | bytes 30000 | tf_op jit(solution)/shard_map/slot_out/pallas_call | solution.py:292
  58.9 1.4 %collective-permute-start.26 = (bf16[768,512]{1,0:T(8,128)(2,1)S(1)}, bf16[768,512]{1,0:T(8,128)(2,1)S(1)}, u32[]{:S(2)}, u32[]{:S(2)}) collective-permute-start(bf16[768,512]{1,0:T(8,128)(2,1)S(1)} %get-tuple-element.75), channel_id=1, source_target_pairs={{0,8},{1,17},{2,10},{3,19},{4,12},{5,21},{6,14},{7,23},{8,0},{9,25... | collective-permute-start | bytes 2359304 | tf_op jit(solution)/shard_map/ppermute | solution.py:41
  60.4 1.3 %collective-permute-start.17 = (bf16[2,48,1024]{2,1,0:T(8,128)(2,1)S(1)}, bf16[2,48,1024]{2,1,0:T(8,128)(2,1)S(1)}, u32[]{:S(2)}, u32[]{:S(2)}) collective-permute-start(bf16[2,48,1024]{2,1,0:T(8,128)(2,1)S(1)} %get-tuple-element.59), channel_id=1, source_target_pairs={{0,2},{1,3},{2,0},{3,1},{4,6},{5,7},{6,4},{7,5},{8,10},{9,11},{10,... | collective-permute-start | bytes 589832 | tf_op jit(solution)/shard_map/ppermute | solution.py:50
  61.9 1.1 collective-permute-start.19
  63.1 3.2 %collective-permute-done.20.got_grad = bf16[384,768]{1,0:T(8,128)(2,1)S(1)} collective-permute-done((bf16[384,768]{1,0:T(8,128)(2,1)S(1)}, bf16[384,768]{1,0:T(8,128)(2,1)S(1)}, u32[]{:S(2)}, u32[]{:S(2)}) %collective-permute-start.20) | collective-permute-done | bytes 589856 | tf_op jit(solution)/shard_map/ppermute | solution.py:45
  66.2 4.6 %slot_grad.1 = (bf16[2,384,768]{2,1,0:T(8,128)(2,1)S(1)}, bf16[2,512,768]{2,1,0:T(8,128)(2,1)S(1)}, bf16[2,48,1024]{2,1,0:T(8,128)(2,1)S(1)}, bf16[2,48,1024]{2,...) custom-call(f32[2,384,768]{2,1,0:T(8,128)S(1)} %get-tuple-element.47.own, ...), custom_call_target="tpu_custom_call" | custom-call | tf_op jit(solution)/shard_map/slot_grad/pallas_call | solution.py:360
  71.0 8.9 %collective-permute-done.19 = bf16[2,48,1024]{2,1,0:T(8,128)(2,1)S(1)} collective-permute-done((bf16[2,48,1024]{2,1,0:T(8,128)(2,1)S(1)}, bf16[2,48,1024]{2,1,0:T(8,128)(2,1)S(1)}, u32[]{:S(2)}, u32[]{:S(2)}) %collective-permute-start.19) | collective-permute-done | bytes 196640 | tf_op jit(solution)/shard_map/ppermute | solution.py:50
  79.9 1.2 %collective-permute-start.24 = (bf16[2,48,1024]{2,1,0:T(8,128)(2,1)S(1)}, bf16[2,48,1024]{2,1,0:T(8,128)(2,1)S(1)}, u32[]{:S(2)}, u32[]{:S(2)}) collective-permute-start(bf16[2,48,1024]{2,1,0:T(8,128)(2,1)S(1)} %get-tuple-element.72), channel_id=1, source_target_pairs={{0,4},{1,5},{2,6},{3,7},{4,0},{5,1},{6,2},{7,3},{8,12},{9,13},{10,... | collective-permute-start | bytes 589832 | tf_op jit(solution)/shard_map/ppermute | solution.py:50
  81.1 1.5 %collective-permute-start.25 = (bf16[2,48,1024]{2,1,0:T(8,128)(2,1)S(1)}, bf16[2,48,1024]{2,1,0:T(8,128)(2,1)S(1)}, u32[]{:S(2)}, u32[]{:S(2)}) collective-permute-start(bf16[2,48,1024]{2,1,0:T(8,128)(2,1)S(1)} %get-tuple-element.74), channel_id=1, source_target_pairs={{0,6},{1,7},{2,4},{3,5},{4,2},{5,3},{6,0},{7,1},{8,14},{9,15},{10,... | collective-permute-start | bytes 589832 | tf_op jit(solution)/shard_map/ppermute | solution.py:50
  82.8 2.0 %collective-permute-done.23 = bf16[2,48,1024]{2,1,0:T(8,128)(2,1)S(1)} collective-permute-done((bf16[2,48,1024]{2,1,0:T(8,128)(2,1)S(1)}, bf16[2,48,1024]{2,1,0:T(8,128)(2,1)S(1)}, u32[]{:S(2)}, u32[]{:S(2)}) %collective-permute-start.23) | collective-permute-done | bytes 196640 | tf_op jit(solution)/shard_map/ppermute | solution.py:50
  84.8 0.4 collective-permute-start.21
  85.2 2.8 %collective-permute-done.24 = bf16[2,48,1024]{2,1,0:T(8,128)(2,1)S(1)} collective-permute-done((bf16[2,48,1024]{2,1,0:T(8,128)(2,1)S(1)}, bf16[2,48,1024]{2,1,0:T(8,128)(2,1)S(1)}, u32[]{:S(2)}, u32[]{:S(2)}) %collective-permute-start.24) | collective-permute-done | bytes 196640 | tf_op jit(solution)/shard_map/ppermute | solution.py:50
  88.0 11.3 %collective-permute-done.25 = bf16[2,48,1024]{2,1,0:T(8,128)(2,1)S(1)} collective-permute-done((bf16[2,48,1024]{2,1,0:T(8,128)(2,1)S(1)}, bf16[2,48,1024]{2,1,0:T(8,128)(2,1)S(1)}, u32[]{:S(2)}, u32[]{:S(2)}) %collective-permute-start.25) | collective-permute-done | bytes 196640 | tf_op jit(solution)/shard_map/ppermute | solution.py:50
  99.6 1.8 %collective-permute-start.22 = (bf16[2,96,1024]{2,1,0:T(8,128)(2,1)S(1)}, bf16[2,96,1024]{2,1,0:T(8,128)(2,1)S(1)}, u32[]{:S(2)}, u32[]{:S(2)}) collective-permute-start(bf16[2,96,1024]{2,1,0:T(8,128)(2,1)S(1)} %pad_maximum_fusion.4), channel_id=1, source_target_pairs={{0,1},{1,0},{2,3},{3,2},{4,5},{5,4},{6,7},{7,6},{8,9},{9,8},{10,11... | collective-permute-start | bytes 1179656 | tf_op jit(solution)/shard_map/ppermute | solution.py:50
  101.4 0.4 collective-permute-start.27
  101.9 1.5 %fusion.2 = bf16[1,768,512]{2,1,0:T(8,128)(2,1)} fusion(bf16[768,512]{1,0:T(8,128)(2,1)S(1)} %collective-permute-done.26, bf16[384,768]{1,0:T(8,128)(2,1)S(1)} %get-tuple-element.64, bf16[384,1024]{1,0:T(8,128)(2,1)S(1)} %get-tuple-element.57.grad_rows), kind=kOutput, calls=%fused_computation.5 | convolution fusion | flops 303169536 | bytes 2555904 | tf_op jit(solution)/shard_map/dot_general | solution.py:23
  103.3 1.3 %unslot.2 = bf16[128,2048]{1,0:T(8,128)(2,1)} custom-call(bf16[128,192]{1,0:T(8,128)(2,1)S(1)} %copy-done.3, f32[128,128]{1,0:T(8,128)S(1)} %copy-done.4, bf16[96,1024]{1,0:T(8,128)(2,1)S(1)} %bitcast.93, bf16[96,1024]{1,0:T(8,128)(2,1)S(1)} %bitcast.95, bf16[2,96,1024]{2,1,0:T(8,128)(2,1)S(1)} %collective-permute-done.22.other), custom_call_target="tpu_custom_call" | custom-call | flops 10000000 | bytes 30000 | tf_op jit(solution)/shard_map/unslot/pallas_call | solution.py:409
  104.6 3.7 %collective-permute-done.27 = bf16[4,48,1024]{2,1,0:T(8,128)(2,1)S(1)} collective-permute-done((bf16[4,48,1024]{2,1,0:T(8,128)(2,1)S(1)}, bf16[4,48,1024]{2,1,0:T(8,128)(2,1)S(1)}, u32[]{:S(2)}, u32[]{:S(2)}) %collective-permute-start.27) | collective-permute-done | bytes 393248 | tf_op jit(solution)/shard_map/ppermute | solution.py:45
  108.4 1.5 %fusion.4 = bf16[1,512,768]{2,1,0:T(8,128)(2,1)} fusion(bf16[2,512,768]{2,1,0:T(8,128)(2,1)S(1)} %collective-permute-done.28, bf16[2,384,768]{2,1,0:T(8,128)(2,1)S(1)} %get-tuple-element.77, bf16[384,1024]{1,0:T(8,128)(2,1)S(1)} %get-tuple-element.66.rows), kind=kOutput, calls=%fused_computation.7 | convolution fusion | flops 303169536 | bytes 2555904 | tf_op jit(solution)/shard_map/dot_general | solution.py:23
  109.9 1.5 %fusion.3 = bf16[1,512,768]{2,1,0:T(8,128)(2,1)} fusion(bf16[2,512,768]{2,1,0:T(8,128)(2,1)S(1)} %collective-permute-done.28, bf16[2,384,768]{2,1,0:T(8,128)(2,1)S(1)} %get-tuple-element.77, bf16[384,1024]{1,0:T(8,128)(2,1)S(1)} %get-tuple-element.66.rows), kind=kOutput, calls=%fused_computation.6 | convolution fusion | flops 303169536 | bytes 2555904 | tf_op jit(solution)/shard_map/dot_general | solution.py:23
  111.4 0.9 collective-permute-start.29
  112.3 1.3 %collective-permute-done.29.other = bf16[2,96,1024]{2,1,0:T(8,128)(2,1)S(1)} collective-permute-done((bf16[2,96,1024]{2,1,0:T(8,128)(2,1)S(1)}, bf16[2,96,1024]{2,1,0:T(8,128)(2,1)S(1)}, u32[]{:S(2)}, u32[]{:S(2)}) %collective-permute-start.29) | collective-permute-done | bytes 393248 | tf_op jit(solution)/shard_map/ppermute | solution.py:50
  113.7 1.3 %unslot.3 = bf16[128,2048]{1,0:T(8,128)(2,1)} custom-call(bf16[128,192]{1,0:T(8,128)(2,1)S(1)} %copy-done.3, f32[128,128]{1,0:T(8,128)S(1)} %copy-done.4, bf16[96,1024]{1,0:T(8,128)(2,1)S(1)} %bitcast.94, bf16[96,1024]{1,0:T(8,128)(2,1)S(1)} %bitcast.96, bf16[2,96,1024]{2,1,0:T(8,128)(2,1)S(1)} %collective-permute-done.29.other), custom_call_target="tpu_custom_call" | custom-call | flops 10000000 | bytes 30000 | tf_op jit(solution)/shard_map/unslot/pallas_call | solution.py:409
  (66 shorter events, 2.2 us)
Async XLA Ops:
  3.0 9.7 %collective-permute-start.12 = (bf16[2,96,1024]{2,1,0:T(8,128)(2,1)}, bf16[2,96,1024]{2,1,0:T(8,128)(2,1)S(1)}, u32[]{:S(2)}, u32[]{:S(2)}) collective-permute-start(bf16[2,96,1024]{2,1,0:T(8,128)(2,1)} %get-tuple-element.51), channel_id=1, source_target_pairs={{0,1},{1,0},{2,3},{3,2},{4,5},{5,4},{6,7},{7,6},{8,9},{9,8},{10,11... | collective-permute-start | bytes 1179656 | tf_op jit(solution)/shard_map/ppermute | solution.py:50
  3.7 12.6 %collective-permute-start.9 = (bf16[1,512,768]{2,1,0:T(8,128)(2,1)}, bf16[1,512,768]{2,1,0:T(8,128)(2,1)S(1)}, u32[]{:S(2)}, u32[]{:S(2)}) collective-permute-start(bf16[1,512,768]{2,1,0:T(8,128)(2,1)} %up.1), channel_id=1, source_target_pairs={{0,8},{1,17},{2,10},{3,19},{4,12},{5,21},{6,14},{7,23},{8,0},{9,25... | collective-permute-start | bytes 2359304 | tf_op jit(solution)/shard_map/ppermute | solution.py:41
  7.3 2.6 %collective-permute-start = (bf16[2,96,1024]{2,1,0:T(8,128)(2,1)}, bf16[2,96,1024]{2,1,0:T(8,128)(2,1)S(1)}, u32[]{:S(2)}, u32[]{:S(2)}) collective-permute-start(bf16[2,96,1024]{2,1,0:T(8,128)(2,1)} %get-tuple-element.46), channel_id=1, source_target_pairs={{0,1},{1,0},{2,3},{3,2},{4,5},{5,4},{6,7},{7,6},{8,9},{9,8},{10,11... | collective-permute-start | bytes 1179656 | tf_op jit(solution)/shard_map/ppermute | solution.py:50
  7.3 22.2 %collective-permute-start.8 = (bf16[1,512,768]{2,1,0:T(8,128)(2,1)}, bf16[1,512,768]{2,1,0:T(8,128)(2,1)S(1)}, u32[]{:S(2)}, u32[]{:S(2)}) collective-permute-start(bf16[1,512,768]{2,1,0:T(8,128)(2,1)} %gate.1), channel_id=1, source_target_pairs={{0,8},{1,17},{2,10},{3,19},{4,12},{5,21},{6,14},{7,23},{8,0},{9,25... | collective-permute-start | bytes 2359304 | tf_op jit(solution)/shard_map/ppermute | solution.py:41
  10.0 11.3 %collective-permute-start.4 = (bf16[2,96,1024]{2,1,0:T(8,128)(2,1)S(1)}, bf16[2,96,1024]{2,1,0:T(8,128)(2,1)S(1)}, u32[]{:S(2)}, u32[]{:S(2)}) collective-permute-start(bf16[2,96,1024]{2,1,0:T(8,128)(2,1)S(1)} %pad_maximum_fusion), channel_id=1, source_target_pairs={{0,16},{1,9},{2,18},{3,11},{4,20},{5,13},{6,22},{7,15},{8,24},{9,1... | collective-permute-start | bytes 1179656 | tf_op jit(solution)/shard_map/ppermute | solution.py:45
  11.3 11.2 %collective-permute-start.1 = (bf16[1,48,1024]{2,1,0:T(8,128)(2,1)S(1)}, bf16[1,48,1024]{2,1,0:T(8,128)(2,1)S(1)}, u32[]{:S(2)}, u32[]{:S(2)}) collective-permute-start(bf16[1,48,1024]{2,1,0:T(8,128)(2,1)S(1)} %bitcast.125), channel_id=1, source_target_pairs={{0,2},{1,3},{2,0},{3,1},{4,6},{5,7},{6,4},{7,5},{8,10},{9,11},{10,... | collective-permute-start | bytes 294920 | tf_op jit(solution)/shard_map/ppermute | solution.py:50
  12.7 11.2 %collective-permute-start.2 = (bf16[1,48,1024]{2,1,0:T(8,128)(2,1)S(1)}, bf16[1,48,1024]{2,1,0:T(8,128)(2,1)S(1)}, u32[]{:S(2)}, u32[]{:S(2)}) collective-permute-start(bf16[1,48,1024]{2,1,0:T(8,128)(2,1)S(1)} %bitcast.124), channel_id=1, source_target_pairs={{0,4},{1,5},{2,6},{3,7},{4,0},{5,1},{6,2},{7,3},{8,12},{9,13},{10,... | collective-permute-start | bytes 294920 | tf_op jit(solution)/shard_map/ppermute | solution.py:50
  12.8 16.7 %copy-start.2 = (bf16[1,768,512]{2,1,0:T(8,128)(2,1)S(1)}, bf16[1,768,512]{2,1,0:T(8,128)(2,1)}, u32[]{:S(2)}) copy-start(bf16[1,768,512]{2,1,0:T(8,128)(2,1)} %down.1) | copy-start | bytes 2359300
  12.8 20.3 %copy-start = (bf16[1,512,768]{2,1,0:T(8,128)(2,1)S(1)}, bf16[1,512,768]{2,1,0:T(8,128)(2,1)}, u32[]{:S(2)}) copy-start(bf16[1,512,768]{2,1,0:T(8,128)(2,1)} %gate.1) | copy-start | bytes 2359300
  12.8 20.3 %copy-start.1 = (bf16[1,512,768]{2,1,0:T(8,128)(2,1)S(1)}, bf16[1,512,768]{2,1,0:T(8,128)(2,1)}, u32[]{:S(2)}) copy-start(bf16[1,512,768]{2,1,0:T(8,128)(2,1)} %up.1) | copy-start | bytes 2359300
  16.2 7.7 %collective-permute-start.3 = (bf16[1,48,1024]{2,1,0:T(8,128)(2,1)S(1)}, bf16[1,48,1024]{2,1,0:T(8,128)(2,1)S(1)}, u32[]{:S(2)}, u32[]{:S(2)}) collective-permute-start(bf16[1,48,1024]{2,1,0:T(8,128)(2,1)S(1)} %bitcast.123), channel_id=1, source_target_pairs={{0,6},{1,7},{2,4},{3,5},{4,2},{5,3},{6,0},{7,1},{8,14},{9,15},{10,... | collective-permute-start | bytes 294920 | tf_op jit(solution)/shard_map/ppermute | solution.py:50
  21.3 14.3 %collective-permute-start.13 = (bf16[2,96,1024]{2,1,0:T(8,128)(2,1)S(1)}, bf16[2,96,1024]{2,1,0:T(8,128)(2,1)S(1)}, u32[]{:S(2)}, u32[]{:S(2)}) collective-permute-start(bf16[2,96,1024]{2,1,0:T(8,128)(2,1)S(1)} %pad_maximum_fusion.1), channel_id=1, source_target_pairs={{0,16},{1,9},{2,18},{3,11},{4,20},{5,13},{6,22},{7,15},{8,24},{9,1... | collective-permute-start | bytes 1179656 | tf_op jit(solution)/shard_map/ppermute | solution.py:45
  22.6 8.4 %collective-permute-start.5 = (bf16[1,48,1024]{2,1,0:T(8,128)(2,1)S(1)}, bf16[1,48,1024]{2,1,0:T(8,128)(2,1)S(1)}, u32[]{:S(2)}, u32[]{:S(2)}) collective-permute-start(bf16[1,48,1024]{2,1,0:T(8,128)(2,1)S(1)} %bitcast.128), channel_id=1, source_target_pairs={{0,2},{1,3},{2,0},{3,1},{4,6},{5,7},{6,4},{7,5},{8,10},{9,11},{10,... | collective-permute-start | bytes 294920 | tf_op jit(solution)/shard_map/ppermute | solution.py:50
  23.9 7.1 %collective-permute-start.6 = (bf16[1,48,1024]{2,1,0:T(8,128)(2,1)S(1)}, bf16[1,48,1024]{2,1,0:T(8,128)(2,1)S(1)}, u32[]{:S(2)}, u32[]{:S(2)}) collective-permute-start(bf16[1,48,1024]{2,1,0:T(8,128)(2,1)S(1)} %bitcast.127), channel_id=1, source_target_pairs={{0,4},{1,5},{2,6},{3,7},{4,0},{5,1},{6,2},{7,3},{8,12},{9,13},{10,... | collective-permute-start | bytes 294920 | tf_op jit(solution)/shard_map/ppermute | solution.py:50
  24.0 9.1 %collective-permute-start.7 = (bf16[1,48,1024]{2,1,0:T(8,128)(2,1)S(1)}, bf16[1,48,1024]{2,1,0:T(8,128)(2,1)S(1)}, u32[]{:S(2)}, u32[]{:S(2)}) collective-permute-start(bf16[1,48,1024]{2,1,0:T(8,128)(2,1)S(1)} %bitcast.126), channel_id=1, source_target_pairs={{0,6},{1,7},{2,4},{3,5},{4,2},{5,3},{6,0},{7,1},{8,14},{9,15},{10,... | collective-permute-start | bytes 294920 | tf_op jit(solution)/shard_map/ppermute | solution.py:50
  29.5 24.1 %collective-permute-start.11 = (bf16[1,768,512]{2,1,0:T(8,128)(2,1)S(1)}, bf16[1,768,512]{2,1,0:T(8,128)(2,1)S(1)}, u32[]{:S(2)}, u32[]{:S(2)}) collective-permute-start(bf16[1,768,512]{2,1,0:T(8,128)(2,1)S(1)} %copy-done.2), channel_id=1, source_target_pairs={{0,8},{1,17},{2,10},{3,19},{4,12},{5,21},{6,14},{7,23},{8,0},{9,25... | collective-permute-start | bytes 2359304 | tf_op jit(solution)/shard_map/ppermute | solution.py:41
  35.4 21.2 %collective-permute-start.10 = (bf16[2,384,768]{2,1,0:T(8,128)(2,1)S(1)}, bf16[2,384,768]{2,1,0:T(8,128)(2,1)S(1)}, u32[]{:S(2)}, u32[]{:S(2)}) collective-permute-start(bf16[2,384,768]{2,1,0:T(8,128)(2,1)S(1)} %get-tuple-element.48), channel_id=1, source_target_pairs={{0,16},{1,9},{2,18},{3,11},{4,20},{5,13},{6,22},{7,15},{8,24},{9,1... | collective-permute-start | bytes 3538952 | tf_op jit(solution)/shard_map/ppermute | solution.py:45
  35.7 15.1 %collective-permute-start.16 = (bf16[2,48,1024]{2,1,0:T(8,128)(2,1)S(1)}, bf16[2,48,1024]{2,1,0:T(8,128)(2,1)S(1)}, u32[]{:S(2)}, u32[]{:S(2)}) collective-permute-start(bf16[2,48,1024]{2,1,0:T(8,128)(2,1)S(1)} %pad_maximum_fusion.11), channel_id=1, source_target_pairs={{0,6},{1,7},{2,4},{3,5},{4,2},{5,3},{6,0},{7,1},{8,14},{9,15},{10,... | collective-permute-start | bytes 589832 | tf_op jit(solution)/shard_map/ppermute | solution.py:50
  36.3 17.2 %collective-permute-start.15 = (bf16[2,48,1024]{2,1,0:T(8,128)(2,1)S(1)}, bf16[2,48,1024]{2,1,0:T(8,128)(2,1)S(1)}, u32[]{:S(2)}, u32[]{:S(2)}) collective-permute-start(bf16[2,48,1024]{2,1,0:T(8,128)(2,1)S(1)} %pad_maximum_fusion.10), channel_id=1, source_target_pairs={{0,4},{1,5},{2,6},{3,7},{4,0},{5,1},{6,2},{7,3},{8,12},{9,13},{10,... | collective-permute-start | bytes 589832 | tf_op jit(solution)/shard_map/ppermute | solution.py:50
  37.1 16.4 %collective-permute-start.14 = (bf16[2,48,1024]{2,1,0:T(8,128)(2,1)S(1)}, bf16[2,48,1024]{2,1,0:T(8,128)(2,1)S(1)}, u32[]{:S(2)}, u32[]{:S(2)}) collective-permute-start(bf16[2,48,1024]{2,1,0:T(8,128)(2,1)S(1)} %pad_maximum_fusion.9), channel_id=1, source_target_pairs={{0,2},{1,3},{2,0},{3,1},{4,6},{5,7},{6,4},{7,5},{8,10},{9,11},{10,... | collective-permute-start | bytes 589832 | tf_op jit(solution)/shard_map/ppermute | solution.py:50
  54.9 11.3 %collective-permute-start.20 = (bf16[384,768]{1,0:T(8,128)(2,1)S(1)}, bf16[384,768]{1,0:T(8,128)(2,1)S(1)}, u32[]{:S(2)}, u32[]{:S(2)}) collective-permute-start(bf16[384,768]{1,0:T(8,128)(2,1)S(1)} %get-tuple-element.63), channel_id=1, source_target_pairs={{0,16},{1,9},{2,18},{3,11},{4,20},{5,13},{6,22},{7,15},{8,24},{9,1... | collective-permute-start | bytes 1769480 | tf_op jit(solution)/shard_map/ppermute | solution.py:45
  58.9 42.4 %collective-permute-start.26 = (bf16[768,512]{1,0:T(8,128)(2,1)S(1)}, bf16[768,512]{1,0:T(8,128)(2,1)S(1)}, u32[]{:S(2)}, u32[]{:S(2)}) collective-permute-start(bf16[768,512]{1,0:T(8,128)(2,1)S(1)} %get-tuple-element.75), channel_id=1, source_target_pairs={{0,8},{1,17},{2,10},{3,19},{4,12},{5,21},{6,14},{7,23},{8,0},{9,25... | collective-permute-start | bytes 2359304 | tf_op jit(solution)/shard_map/ppermute | solution.py:41
  60.4 10.5 %collective-permute-start.17 = (bf16[2,48,1024]{2,1,0:T(8,128)(2,1)S(1)}, bf16[2,48,1024]{2,1,0:T(8,128)(2,1)S(1)}, u32[]{:S(2)}, u32[]{:S(2)}) collective-permute-start(bf16[2,48,1024]{2,1,0:T(8,128)(2,1)S(1)} %get-tuple-element.59), channel_id=1, source_target_pairs={{0,2},{1,3},{2,0},{3,1},{4,6},{5,7},{6,4},{7,5},{8,10},{9,11},{10,... | collective-permute-start | bytes 589832 | tf_op jit(solution)/shard_map/ppermute | solution.py:50
  61.6 9.3 %collective-permute-start.18 = (bf16[2,48,1024]{2,1,0:T(8,128)(2,1)S(1)}, bf16[2,48,1024]{2,1,0:T(8,128)(2,1)S(1)}, u32[]{:S(2)}, u32[]{:S(2)}) collective-permute-start(bf16[2,48,1024]{2,1,0:T(8,128)(2,1)S(1)} %get-tuple-element.60), channel_id=1, source_target_pairs={{0,4},{1,5},{2,6},{3,7},{4,0},{5,1},{6,2},{7,3},{8,12},{9,13},{10,... | collective-permute-start | bytes 589832 | tf_op jit(solution)/shard_map/ppermute | solution.py:50
  61.9 18.0 %collective-permute-start.19 = (bf16[2,48,1024]{2,1,0:T(8,128)(2,1)S(1)}, bf16[2,48,1024]{2,1,0:T(8,128)(2,1)S(1)}, u32[]{:S(2)}, u32[]{:S(2)}) collective-permute-start(bf16[2,48,1024]{2,1,0:T(8,128)(2,1)S(1)} %get-tuple-element.61), channel_id=1, source_target_pairs={{0,6},{1,7},{2,4},{3,5},{4,2},{5,3},{6,0},{7,1},{8,14},{9,15},{10,... | collective-permute-start | bytes 589832 | tf_op jit(solution)/shard_map/ppermute | solution.py:50
  70.9 37.5 %collective-permute-start.28 = (bf16[2,512,768]{2,1,0:T(8,128)(2,1)S(1)}, bf16[2,512,768]{2,1,0:T(8,128)(2,1)S(1)}, u32[]{:S(2)}, u32[]{:S(2)}) collective-permute-start(bf16[2,512,768]{2,1,0:T(8,128)(2,1)S(1)} %get-tuple-element.79), channel_id=1, source_target_pairs={{0,8},{1,17},{2,10},{3,19},{4,12},{5,21},{6,14},{7,23},{8,0},{9,25... | collective-permute-start | bytes 4718600 | tf_op jit(solution)/shard_map/ppermute | solution.py:41
  79.9 4.8 %collective-permute-start.23 = (bf16[2,48,1024]{2,1,0:T(8,128)(2,1)S(1)}, bf16[2,48,1024]{2,1,0:T(8,128)(2,1)S(1)}, u32[]{:S(2)}, u32[]{:S(2)}) collective-permute-start(bf16[2,48,1024]{2,1,0:T(8,128)(2,1)S(1)} %get-tuple-element.70), channel_id=1, source_target_pairs={{0,2},{1,3},{2,0},{3,1},{4,6},{5,7},{6,4},{7,5},{8,10},{9,11},{10,... | collective-permute-start | bytes 589832 | tf_op jit(solution)/shard_map/ppermute | solution.py:50
  79.9 8.0 %collective-permute-start.24 = (bf16[2,48,1024]{2,1,0:T(8,128)(2,1)S(1)}, bf16[2,48,1024]{2,1,0:T(8,128)(2,1)S(1)}, u32[]{:S(2)}, u32[]{:S(2)}) collective-permute-start(bf16[2,48,1024]{2,1,0:T(8,128)(2,1)S(1)} %get-tuple-element.72), channel_id=1, source_target_pairs={{0,4},{1,5},{2,6},{3,7},{4,0},{5,1},{6,2},{7,3},{8,12},{9,13},{10,... | collective-permute-start | bytes 589832 | tf_op jit(solution)/shard_map/ppermute | solution.py:50
  81.1 18.2 %collective-permute-start.25 = (bf16[2,48,1024]{2,1,0:T(8,128)(2,1)S(1)}, bf16[2,48,1024]{2,1,0:T(8,128)(2,1)S(1)}, u32[]{:S(2)}, u32[]{:S(2)}) collective-permute-start(bf16[2,48,1024]{2,1,0:T(8,128)(2,1)S(1)} %get-tuple-element.74), channel_id=1, source_target_pairs={{0,6},{1,7},{2,4},{3,5},{4,2},{5,3},{6,0},{7,1},{8,14},{9,15},{10,... | collective-permute-start | bytes 589832 | tf_op jit(solution)/shard_map/ppermute | solution.py:50
  84.8 14.7 %collective-permute-start.21 = (bf16[4,48,1024]{2,1,0:T(8,128)(2,1)S(1)}, bf16[4,48,1024]{2,1,0:T(8,128)(2,1)S(1)}, u32[]{:S(2)}, u32[]{:S(2)}) collective-permute-start(bf16[4,48,1024]{2,1,0:T(8,128)(2,1)S(1)} %get-tuple-element.68), channel_id=1, source_target_pairs={{0,16},{1,9},{2,18},{3,11},{4,20},{5,13},{6,22},{7,15},{8,24},{9,1... | collective-permute-start | bytes 1179656 | tf_op jit(solution)/shard_map/ppermute | solution.py:45
  99.6 3.8 %collective-permute-start.22 = (bf16[2,96,1024]{2,1,0:T(8,128)(2,1)S(1)}, bf16[2,96,1024]{2,1,0:T(8,128)(2,1)S(1)}, u32[]{:S(2)}, u32[]{:S(2)}) collective-permute-start(bf16[2,96,1024]{2,1,0:T(8,128)(2,1)S(1)} %pad_maximum_fusion.4), channel_id=1, source_target_pairs={{0,1},{1,0},{2,3},{3,2},{4,5},{5,4},{6,7},{7,6},{8,9},{9,8},{10,11... | collective-permute-start | bytes 1179656 | tf_op jit(solution)/shard_map/ppermute | solution.py:50
  101.4 6.9 %collective-permute-start.27 = (bf16[4,48,1024]{2,1,0:T(8,128)(2,1)S(1)}, bf16[4,48,1024]{2,1,0:T(8,128)(2,1)S(1)}, u32[]{:S(2)}, u32[]{:S(2)}) collective-permute-start(bf16[4,48,1024]{2,1,0:T(8,128)(2,1)S(1)} %pad_maximum_fusion.6), channel_id=1, source_target_pairs={{0,16},{1,9},{2,18},{3,11},{4,20},{5,13},{6,22},{7,15},{8,24},{9,1... | collective-permute-start | bytes 1179656 | tf_op jit(solution)/shard_map/ppermute | solution.py:45
  101.8 1.5 %copy-start.3 = (bf16[128,192]{1,0:T(8,128)(2,1)S(1)}, bf16[128,192]{1,0:T(8,128)(2,1)}, u32[]{:S(2)}) copy-start(bf16[128,192]{1,0:T(8,128)(2,1)} %get-tuple-element.43.pick) | copy-start | bytes 147460
  101.8 1.5 %copy-start.4 = (f32[128,128]{1,0:T(8,128)S(1)}, f32[128,128]{1,0:T(8,128)}, u32[]{:S(2)}) copy-start(f32[128,128]{1,0:T(8,128)} %get-tuple-element.44.weight) | copy-start | bytes 196612
  111.4 2.3 %collective-permute-start.29 = (bf16[2,96,1024]{2,1,0:T(8,128)(2,1)S(1)}, bf16[2,96,1024]{2,1,0:T(8,128)(2,1)S(1)}, u32[]{:S(2)}, u32[]{:S(2)}) collective-permute-start(bf16[2,96,1024]{2,1,0:T(8,128)(2,1)S(1)} %pad_maximum_fusion.7), channel_id=1, source_target_pairs={{0,1},{1,0},{2,3},{3,2},{4,5},{5,4},{6,7},{7,6},{8,9},{9,8},{10,11... | collective-permute-start | bytes 1179656 | tf_op jit(solution)/shard_map/ppermute | solution.py:50

commit v4 on v3

--- a/solution.py
+++ b/solution.py
@@ -410,7 +410,7 @@
         functools.partial(unslot_kernel, weighted),
         out_shape=jax.ShapeDtypeStruct((count, 2 * half), BF16),
         compiler_params=params(),
-        cost_estimate=cost(0.01),
+        cost_estimate=cost(4),
         name="unslot",
     )(pick, weight, near, far, other)
 
@@ -436,6 +436,8 @@
     near_parts, far_parts = by_chip(slots[0], other[0]), by_chip(far[0], far[1])
     if apart:
         near_parts = swap_chips(near_parts, chips, *before_near)
+        for k in range(1, chips):
+            far_parts[k] = after(far_parts[k], near_parts[k])
         return far, near_parts + swap_chips(far_parts, chips, *before_far)
     parts = [jnp.concatenate(pair, axis=0) for pair in zip(near_parts, far_parts)]
     return far, swap_chips(parts, chips, *before_near)
@@ -521,7 +523,11 @@
         tile,
         paired,
     )
-    grad_out_parts = swap_chips(cut(slot_grad), chips, *sent)
+    grad_out_parts = cut(slot_grad)
+    for k in range(len(grad_out_parts)):
+        if k % chips:
+            value = after(grad_out_parts[k], out_parts[k % chips])
+            grad_out_parts[k] = swap_expert(value, 2 * (k % chips))
     got_far = swap_weight(after(far_grads, *sent[:1]))
 
     grad_w_gate = contract_first(rows[:, :block], grads[0]) + got_far[0].astype(F32)
@@ -533,7 +539,7 @@
 
     back = return_slots(out_parts, chips, capacity, (slot_grad[0],), ())
     mixed = unslot(pick, weight, *back, True)
-    grad_back = return_slots(grad_out_parts, chips, capacity, (got_down,), (mixed, grad_w_gate, grad_w_up, grad_w_down))
+    grad_back = return_slots(grad_out_parts, chips, capacity, (), (mixed,))
     grad_tokens = unslot(pick, weight, *grad_back, False)
     return (
         mixed,

time: 115 us -> 114 us (level); the launches traced: 115 us -> 113 us
  waiting for transfers between devices: 63 us -> 49.4 us
  starting transfers between devices: 25.5 us -> 36.7 us
    ppermute x19, waiting for transfers between devices: 43.3 us -> 30.1 us  [swap_expert(): lax.ppermute(value, 'expert', [(i, i ^ mask) for i in range(experts)])]
    ppermute x19, starting transfers between devices: 15.9 us -> 26.2 us  [swap_expert(): lax.ppermute(value, 'expert', [(i, i ^ mask) for i in range(experts)])]
    ppermute x5, waiting for transfers between devices: 7.55 us -> 4.8 us  [swap_weight(): return lax.ppermute(value, BOTH, pair_list(lax.axis_size('expert'), (1, 2)))]
    ppermute x6, waiting for transfers between devices: 12.1 us -> 14.4 us  [swap_rows(): return lax.ppermute(value, BOTH, pair_list(lax.axis_size('expert'), (2, 1)))]
  transfers between devices with their start and end apart: 30 -> 30, of which waited for: 14 -> 12; matrix products, arithmetic and copies ran while one was open for 4% -> 4% of each run, Pallas kernels for 12% -> 14%
where the time goes in v4:
time: 114 us; the launch traced here: 113 us
  waiting for transfers between devices  49.4 us (43%)
  starting transfers between devices  36.7 us (32%)
  Pallas kernels  18 us (16%)
  matrix products  4.44 us (4%)
  local copies, waits for them, and re-layouts  2.46 us (2%)
    ppermute x19, waiting for transfers between devices, swap_expert(): lax.ppermute(value, 'expert', [(i, i ^ mask) for i in range(experts)])  30.1 us
    ppermute x19, starting transfers between devices, swap_expert(): lax.ppermute(value, 'expert', [(i, i ^ mask) for i in range(experts)])  26.2 us
    ppermute x6, waiting for transfers between devices, swap_rows(): return lax.ppermute(value, BOTH, pair_list(lax.axis_size('expert'), (2, 1)))  14.4 us
    ppermute x6, starting transfers between devices, swap_rows(): return lax.ppermute(value, BOTH, pair_list(lax.axis_size('expert'), (2, 1)))  5.69 us
    ppermute x5, waiting for transfers between devices, swap_weight(): return lax.ppermute(value, BOTH, pair_list(lax.axis_size('expert'), (1, 2)))  4.8 us
    ppermute x5, starting transfers between devices, swap_weight(): return lax.ppermute(value, BOTH, pair_list(lax.axis_size('expert'), (1, 2)))  4.76 us
    pallas_call x1, Pallas kernels, slot_grad_parts(): pl.pallas_call(functools.partial(slot_grad_kernel, places), grid=(hidden...  4.63 us
    dot_general x3, matrix products, contract_first(): lax.dot_general(left_side, right_side, (((0,), (0,)), ((), ())), preferre...  4.44 us
  transfers between devices with their start and end apart: 30, of which 12 were waited for; matrix products, arithmetic and copies ran while one was open for 4% of the time, Pallas kernels for 14%

profile of v4, /device:TPU:19, one launch (start us, length us, event | category | flops | bytes accessed | tf_op | source)
XLA Modules:
  0.0 112.5 jit_solution(638185693529587703)
XLA Ops:
  0.6 2.4 %make_grads.1 = (bf16[2,96,1024]{2,1,0:T(8,128)(2,1)}, bf16[2,96,1024]{2,1,0:T(8,128)(2,1)}, bf16[128,192]{1,0:T(8,128)(2,1)}, f32[128,128]{1,0:T(8,128)}) custom-call(bf16[128,2048]{1,0:T(8,128)(2,1)} %cot.1, s32[1,128]{1,0:T(1,128)} %bitcast.129, s32[1,128]{1,0:T(1,128)} %bitcast.131), custom_call_target="tpu_custom_call" | custom-call | flops 10000000 | bytes 30000 | tf_op jit(solution)/shard_map/make_grads/pallas_call | solution.py:141
  3.0 0.7 collective-permute-start.12
  3.7 1.2 %collective-permute-start.9 = (bf16[1,512,768]{2,1,0:T(8,128)(2,1)}, bf16[1,512,768]{2,1,0:T(8,128)(2,1)S(1)}, u32[]{:S(2)}, u32[]{:S(2)}) collective-permute-start(bf16[1,512,768]{2,1,0:T(8,128)(2,1)} %up.1), channel_id=1, source_target_pairs={{0,8},{1,17},{2,10},{3,19},{4,12},{5,21},{6,14},{7,23},{8,0},{9,25... | collective-permute-start | bytes 2359304 | tf_op jit(solution)/shard_map/ppermute | solution.py:41
  4.9 2.3 %make_slots.1 = (bf16[2,96,1024]{2,1,0:T(8,128)(2,1)}, bf16[2,96,1024]{2,1,0:T(8,128)(2,1)}) custom-call(bf16[128,2048]{1,0:T(8,128)(2,1)} %tok.1, s32[1,128]{1,0:T(1,128)} %bitcast.130, s32[1,128]{1,0:T(1,128)} %bitcast.132), custom_call_target="tpu_custom_call" | custom-call | flops 10000000 | bytes 30000 | tf_op jit(solution)/shard_map/make_slots/pallas_call | solution.py:129
  7.3 0.5 collective-permute-start.8
  7.8 1.0 fusion.29
  8.9 1.1 fusion.32
  10.0 1.3 %collective-permute-start.4 = (bf16[2,96,1024]{2,1,0:T(8,128)(2,1)S(1)}, bf16[2,96,1024]{2,1,0:T(8,128)(2,1)S(1)}, u32[]{:S(2)}, u32[]{:S(2)}) collective-permute-start(bf16[2,96,1024]{2,1,0:T(8,128)(2,1)S(1)} %pad_maximum_fusion), channel_id=1, source_target_pairs={{0,16},{1,9},{2,18},{3,11},{4,20},{5,13},{6,22},{7,15},{8,24},{9,1... | collective-permute-start | bytes 1179656 | tf_op jit(solution)/shard_map/ppermute | solution.py:45
  11.5 3.2 %collective-permute-start.2 = (bf16[1,48,1024]{2,1,0:T(8,128)(2,1)S(1)}, bf16[1,48,1024]{2,1,0:T(8,128)(2,1)S(1)}, u32[]{:S(2)}, u32[]{:S(2)}) collective-permute-start(bf16[1,48,1024]{2,1,0:T(8,128)(2,1)S(1)} %bitcast.124), channel_id=1, source_target_pairs={{0,4},{1,5},{2,6},{3,7},{4,0},{5,1},{6,2},{7,3},{8,12},{9,13},{10,... | collective-permute-start | bytes 294920 | tf_op jit(solution)/shard_map/ppermute | solution.py:50
  14.9 1.4 %collective-permute-done.9.refs_11_.far_up = bf16[1,512,768]{2,1,0:T(8,128)(2,1)S(1)} collective-permute-done((bf16[1,512,768]{2,1,0:T(8,128)(2,1)}, bf16[1,512,768]{2,1,0:T(8,128)(2,1)S(1)}, u32[]{:S(2)}, u32[]{:S(2)}) %collective-permute-start.9) | collective-permute-done | bytes 786464 | tf_op jit(solution)/shard_map/ppermute | solution.py:41
  16.2 1.3 %collective-permute-start.1 = (bf16[1,48,1024]{2,1,0:T(8,128)(2,1)S(1)}, bf16[1,48,1024]{2,1,0:T(8,128)(2,1)S(1)}, u32[]{:S(2)}, u32[]{:S(2)}) collective-permute-start(bf16[1,48,1024]{2,1,0:T(8,128)(2,1)S(1)} %bitcast.123), channel_id=1, source_target_pairs={{0,2},{1,3},{2,0},{3,1},{4,6},{5,7},{6,4},{7,5},{8,10},{9,11},{10,... | collective-permute-start | bytes 294920 | tf_op jit(solution)/shard_map/ppermute | solution.py:50
  17.6 3.7 %collective-permute-done.4 = bf16[2,96,1024]{2,1,0:T(8,128)(2,1)S(1)} collective-permute-done((bf16[2,96,1024]{2,1,0:T(8,128)(2,1)S(1)}, bf16[2,96,1024]{2,1,0:T(8,128)(2,1)S(1)}, u32[]{:S(2)}, u32[]{:S(2)}) %collective-permute-start.4) | collective-permute-done | bytes 393248 | tf_op jit(solution)/shard_map/ppermute | solution.py:45
  21.3 1.2 %collective-permute-start.13 = (bf16[2,96,1024]{2,1,0:T(8,128)(2,1)S(1)}, bf16[2,96,1024]{2,1,0:T(8,128)(2,1)S(1)}, u32[]{:S(2)}, u32[]{:S(2)}) collective-permute-start(bf16[2,96,1024]{2,1,0:T(8,128)(2,1)S(1)} %pad_maximum_fusion.1), channel_id=1, source_target_pairs={{0,16},{1,9},{2,18},{3,11},{4,20},{5,13},{6,22},{7,15},{8,24},{9,1... | collective-permute-start | bytes 1179656 | tf_op jit(solution)/shard_map/ppermute | solution.py:45
  22.8 3.2 %collective-permute-start.6 = (bf16[1,48,1024]{2,1,0:T(8,128)(2,1)S(1)}, bf16[1,48,1024]{2,1,0:T(8,128)(2,1)S(1)}, u32[]{:S(2)}, u32[]{:S(2)}) collective-permute-start(bf16[1,48,1024]{2,1,0:T(8,128)(2,1)S(1)} %bitcast.127), channel_id=1, source_target_pairs={{0,4},{1,5},{2,6},{3,7},{4,0},{5,1},{6,2},{7,3},{8,12},{9,13},{10,... | collective-permute-start | bytes 294920 | tf_op jit(solution)/shard_map/ppermute | solution.py:50
  26.0 3.4 %collective-permute-done.8.refs_10_.far_gate = bf16[1,512,768]{2,1,0:T(8,128)(2,1)S(1)} collective-permute-done((bf16[1,512,768]{2,1,0:T(8,128)(2,1)}, bf16[1,512,768]{2,1,0:T(8,128)(2,1)S(1)}, u32[]{:S(2)}, u32[]{:S(2)}) %collective-permute-start.8) | collective-permute-done | bytes 786464 | tf_op jit(solution)/shard_map/ppermute | solution.py:41
  29.5 1.5 %collective-permute-start.11 = (bf16[1,768,512]{2,1,0:T(8,128)(2,1)S(1)}, bf16[1,768,512]{2,1,0:T(8,128)(2,1)S(1)}, u32[]{:S(2)}, u32[]{:S(2)}) collective-permute-start(bf16[1,768,512]{2,1,0:T(8,128)(2,1)S(1)} %copy-done.2), channel_id=1, source_target_pairs={{0,8},{1,17},{2,10},{3,19},{4,12},{5,21},{6,14},{7,23},{8,0},{9,25... | collective-permute-start | bytes 2359304 | tf_op jit(solution)/shard_map/ppermute | solution.py:41
  31.0 2.4 %gate_up_parts.1 = (bf16[384,1024]{1,0:T(8,128)(2,1)S(1)}, f32[2,384,768]{2,1,0:T(8,128)S(1)}, bf16[2,384,768]{2,1,0:T(8,128)(2,1)S(1)}) custom-call(bf16[1,48,1024]{2,1,0:T(8,128)(2,1)S(1)} %bitcast.93, bf16[1,48,1024]{2,1,0:T(8,128)(2,1)S(1)} %collective-permute-done.1.refs_1_, bf16[1,48,1024]{2,1,0:T(8,128)(2,1)S(1)} %collective-permute-done.2.refs_2_, ...), custom_call_target="tpu_custom_call" | custom-call | flops 10000000 | bytes 30000 | tf_op jit(solution)/shard_map/gate_up_parts/pallas_call | solution.py:203
  33.6 1.0 collective-permute-start.16
  34.6 2.5 %collective-permute-start.15 = (bf16[2,48,1024]{2,1,0:T(8,128)(2,1)S(1)}, bf16[2,48,1024]{2,1,0:T(8,128)(2,1)S(1)}, u32[]{:S(2)}, u32[]{:S(2)}) collective-permute-start(bf16[2,48,1024]{2,1,0:T(8,128)(2,1)S(1)} %pad_maximum_fusion.10), channel_id=1, source_target_pairs={{0,4},{1,5},{2,6},{3,7},{4,0},{5,1},{6,2},{7,3},{8,12},{9,13},{10,... | collective-permute-start | bytes 589832 | tf_op jit(solution)/shard_map/ppermute | solution.py:50
  37.1 1.0 collective-permute-start.14
  38.2 4.9 %collective-permute-done.16.refs_3_ = bf16[2,48,1024]{2,1,0:T(8,128)(2,1)S(1)} collective-permute-done((bf16[2,48,1024]{2,1,0:T(8,128)(2,1)S(1)}, bf16[2,48,1024]{2,1,0:T(8,128)(2,1)S(1)}, u32[]{:S(2)}, u32[]{:S(2)}) %collective-permute-start.16) | collective-permute-done | bytes 196640 | tf_op jit(solution)/shard_map/ppermute | solution.py:50
  43.1 6.5 %collective-permute-done.15.refs_2_ = bf16[2,48,1024]{2,1,0:T(8,128)(2,1)S(1)} collective-permute-done((bf16[2,48,1024]{2,1,0:T(8,128)(2,1)S(1)}, bf16[2,48,1024]{2,1,0:T(8,128)(2,1)S(1)}, u32[]{:S(2)}, u32[]{:S(2)}) %collective-permute-start.15) | collective-permute-done | bytes 196640 | tf_op jit(solution)/shard_map/ppermute | solution.py:50
  49.9 1.4 %grad_hidden_parts.1 = (bf16[384,1024]{1,0:T(8,128)(2,1)S(1)}, f32[384,768]{1,0:T(8,128)S(1)}, bf16[384,768]{1,0:T(8,128)(2,1)S(1)}) custom-call(bf16[2,48,1024]{2,1,0:T(8,128)(2,1)S(1)} %pad_maximum_fusion.8.refs_0_, bf16[2,48,1024]{2,1,0:T(8,128)(2,1)S(1)} %collective-permute-done.14.refs_1_, bf16[2,48,1024]{2,1,0:T(8,128)(2,1)S(1)} %collective-permute-done.15.refs_2_, ...), custom_call_target="tpu_custom_call" | custom-call | flops 1000000000 | bytes 3000000 | tf_op jit(solution)/shard_map/grad_hidden_parts/pallas_call | solution.py:244
  51.3 1.4 %collective-permute-start.20 = (bf16[384,768]{1,0:T(8,128)(2,1)S(1)}, bf16[384,768]{1,0:T(8,128)(2,1)S(1)}, u32[]{:S(2)}, u32[]{:S(2)}) collective-permute-start(bf16[384,768]{1,0:T(8,128)(2,1)S(1)} %get-tuple-element.68), channel_id=1, source_target_pairs={{0,16},{1,9},{2,18},{3,11},{4,20},{5,13},{6,22},{7,15},{8,24},{9,1... | collective-permute-start | bytes 1769480 | tf_op jit(solution)/shard_map/ppermute | solution.py:45
  52.7 3.8 %collective-permute-done.10.got = bf16[2,384,768]{2,1,0:T(8,128)(2,1)S(1)} collective-permute-done((bf16[2,384,768]{2,1,0:T(8,128)(2,1)S(1)}, bf16[2,384,768]{2,1,0:T(8,128)(2,1)S(1)}, u32[]{:S(2)}, u32[]{:S(2)}) %collective-permute-start.10) | collective-permute-done | bytes 1179680 | tf_op jit(solution)/shard_map/ppermute | solution.py:45
  56.5 2.4 %slot_out.1 = (bf16[384,768]{1,0:T(8,128)(2,1)S(1)}, bf16[768,512]{1,0:T(8,128)(2,1)S(1)}, bf16[2,48,1024]{2,1,0:T(8,128)(2,1)S(1)}, bf16[2,48,1024]{2,1,0:T(8,1...) custom-call(f32[2,384,768]{2,1,0:T(8,128)S(1)} %get-tuple-element.52.own, ...), custom_call_target="tpu_custom_call" | custom-call | flops 10000000 | bytes 30000 | tf_op jit(solution)/shard_map/slot_out/pallas_call | solution.py:292
  58.9 0.5 collective-permute-start.29
  59.4 1.3 %collective-permute-start.17 = (bf16[2,48,1024]{2,1,0:T(8,128)(2,1)S(1)}, bf16[2,48,1024]{2,1,0:T(8,128)(2,1)S(1)}, u32[]{:S(2)}, u32[]{:S(2)}) collective-permute-start(bf16[2,48,1024]{2,1,0:T(8,128)(2,1)S(1)} %get-tuple-element.64), channel_id=1, source_target_pairs={{0,2},{1,3},{2,0},{3,1},{4,6},{5,7},{6,4},{7,5},{8,10},{9,11},{10,... | collective-permute-start | bytes 589832 | tf_op jit(solution)/shard_map/ppermute | solution.py:50
  60.7 0.8 collective-permute-start.18
  61.5 0.5 collective-permute-start.19
  62.1 2.4 %collective-permute-done.20.got_grad = bf16[384,768]{1,0:T(8,128)(2,1)S(1)} collective-permute-done((bf16[384,768]{1,0:T(8,128)(2,1)S(1)}, bf16[384,768]{1,0:T(8,128)(2,1)S(1)}, u32[]{:S(2)}, u32[]{:S(2)}) %collective-permute-start.20) | collective-permute-done | bytes 589856 | tf_op jit(solution)/shard_map/ppermute | solution.py:45
  64.5 4.6 %slot_grad.1 = (bf16[2,384,768]{2,1,0:T(8,128)(2,1)S(1)}, bf16[2,512,768]{2,1,0:T(8,128)(2,1)S(1)}, bf16[2,48,1024]{2,1,0:T(8,128)(2,1)S(1)}, bf16[2,48,1024]{2,...) custom-call(f32[2,384,768]{2,1,0:T(8,128)S(1)} %get-tuple-element.52.own, ...), custom_call_target="tpu_custom_call" | custom-call | tf_op jit(solution)/shard_map/slot_grad/pallas_call | solution.py:360
  69.2 1.0 collective-permute-start.28
  70.2 0.8 collective-permute-start.23
  71.0 6.2 %collective-permute-start.24 = (bf16[2,48,1024]{2,1,0:T(8,128)(2,1)S(1)}, bf16[2,48,1024]{2,1,0:T(8,128)(2,1)S(1)}, u32[]{:S(2)}, u32[]{:S(2)}) collective-permute-start(bf16[2,48,1024]{2,1,0:T(8,128)(2,1)S(1)} %get-tuple-element.77), channel_id=1, source_target_pairs={{0,4},{1,5},{2,6},{3,7},{4,0},{5,1},{6,2},{7,3},{8,12},{9,13},{10,... | collective-permute-start | bytes 589832 | tf_op jit(solution)/shard_map/ppermute | solution.py:50
  77.2 6.8 %collective-permute-done.19 = bf16[2,48,1024]{2,1,0:T(8,128)(2,1)S(1)} collective-permute-done((bf16[2,48,1024]{2,1,0:T(8,128)(2,1)S(1)}, bf16[2,48,1024]{2,1,0:T(8,128)(2,1)S(1)}, u32[]{:S(2)}, u32[]{:S(2)}) %collective-permute-start.19) | collective-permute-done | bytes 196640 | tf_op jit(solution)/shard_map/ppermute | solution.py:50
  84.3 0.8 collective-permute-start.21
  85.1 5.9 %collective-permute-done.24 = bf16[2,48,1024]{2,1,0:T(8,128)(2,1)S(1)} collective-permute-done((bf16[2,48,1024]{2,1,0:T(8,128)(2,1)S(1)}, bf16[2,48,1024]{2,1,0:T(8,128)(2,1)S(1)}, u32[]{:S(2)}, u32[]{:S(2)}) %collective-permute-start.24) | collective-permute-done | bytes 196640 | tf_op jit(solution)/shard_map/ppermute | solution.py:50
  91.0 5.7 %collective-permute-done.25 = bf16[2,48,1024]{2,1,0:T(8,128)(2,1)S(1)} collective-permute-done((bf16[2,48,1024]{2,1,0:T(8,128)(2,1)S(1)}, bf16[2,48,1024]{2,1,0:T(8,128)(2,1)S(1)}, u32[]{:S(2)}, u32[]{:S(2)}) %collective-permute-start.25) | collective-permute-done | bytes 196640 | tf_op jit(solution)/shard_map/ppermute | solution.py:50
  96.8 0.8 collective-permute-start.26
  97.7 1.5 %collective-permute-start.22 = (bf16[2,96,1024]{2,1,0:T(8,128)(2,1)S(1)}, bf16[2,96,1024]{2,1,0:T(8,128)(2,1)S(1)}, u32[]{:S(2)}, u32[]{:S(2)}) collective-permute-start(bf16[2,96,1024]{2,1,0:T(8,128)(2,1)S(1)} %pad_maximum_fusion.4), channel_id=1, source_target_pairs={{0,1},{1,0},{2,3},{3,2},{4,5},{5,4},{6,7},{7,6},{8,9},{9,8},{10,11... | collective-permute-start | bytes 1179656 | tf_op jit(solution)/shard_map/ppermute | solution.py:50
  99.2 4.5 %collective-permute-done.26 = bf16[4,48,1024]{2,1,0:T(8,128)(2,1)S(1)} collective-permute-done((bf16[4,48,1024]{2,1,0:T(8,128)(2,1)S(1)}, bf16[4,48,1024]{2,1,0:T(8,128)(2,1)S(1)}, u32[]{:S(2)}, u32[]{:S(2)}) %collective-permute-start.26) | collective-permute-done | bytes 393248 | tf_op jit(solution)/shard_map/ppermute | solution.py:45
  103.8 1.3 %unslot.2 = bf16[128,2048]{1,0:T(8,128)(2,1)} custom-call(bf16[128,192]{1,0:T(8,128)(2,1)S(1)} %copy-done.3, f32[128,128]{1,0:T(8,128)S(1)} %copy-done.4, bf16[96,1024]{1,0:T(8,128)(2,1)S(1)} %bitcast.95, bf16[96,1024]{1,0:T(8,128)(2,1)S(1)} %bitcast.98, bf16[2,96,1024]{2,1,0:T(8,128)(2,1)S(1)} %collective-permute-done.22.other), custom_call_target="tpu_custom_call" | custom-call | flops 4000000000 | bytes 12000000 | tf_op jit(solution)/shard_map/unslot/pallas_call | solution.py:409
  105.1 1.7 %collective-permute-start.27 = (bf16[2,96,1024]{2,1,0:T(8,128)(2,1)S(1)}, bf16[2,96,1024]{2,1,0:T(8,128)(2,1)S(1)}, u32[]{:S(2)}, u32[]{:S(2)}) collective-permute-start(bf16[2,96,1024]{2,1,0:T(8,128)(2,1)S(1)} %pad_maximum_fusion.7), channel_id=1, source_target_pairs={{0,1},{1,0},{2,3},{3,2},{4,5},{5,4},{6,7},{7,6},{8,9},{9,8},{10,11... | collective-permute-start | bytes 1179656 | tf_op jit(solution)/shard_map/ppermute | solution.py:50
  106.8 1.5 %fusion.2 = bf16[1,768,512]{2,1,0:T(8,128)(2,1)} fusion(bf16[768,512]{1,0:T(8,128)(2,1)S(1)} %collective-permute-done.29, bf16[384,768]{1,0:T(8,128)(2,1)S(1)} %get-tuple-element.69, bf16[384,1024]{1,0:T(8,128)(2,1)S(1)} %get-tuple-element.62.grad_rows), kind=kOutput, calls=%fused_computation.5 | convolution fusion | flops 303169536 | bytes 2555904 | tf_op jit(solution)/shard_map/dot_general | solution.py:23
  108.3 1.3 %unslot.3 = bf16[128,2048]{1,0:T(8,128)(2,1)} custom-call(bf16[128,192]{1,0:T(8,128)(2,1)S(1)} %copy-done.3, f32[128,128]{1,0:T(8,128)S(1)} %copy-done.4, bf16[96,1024]{1,0:T(8,128)(2,1)S(1)} %bitcast.96, bf16[96,1024]{1,0:T(8,128)(2,1)S(1)} %bitcast.97, bf16[2,96,1024]{2,1,0:T(8,128)(2,1)S(1)} %collective-permute-done.27.other), custom_call_target="tpu_custom_call" | custom-call | flops 4000000000 | bytes 12000000 | tf_op jit(solution)/shard_map/unslot/pallas_call | solution.py:409
  109.6 1.5 %fusion.4 = bf16[1,512,768]{2,1,0:T(8,128)(2,1)} fusion(bf16[2,512,768]{2,1,0:T(8,128)(2,1)S(1)} %collective-permute-done.28, bf16[2,384,768]{2,1,0:T(8,128)(2,1)S(1)} %get-tuple-element.81, bf16[384,1024]{1,0:T(8,128)(2,1)S(1)} %get-tuple-element.71.rows), kind=kOutput, calls=%fused_computation.7 | convolution fusion | flops 303169536 | bytes 2555904 | tf_op jit(solution)/shard_map/dot_general | solution.py:23
  111.0 1.5 %fusion.3 = bf16[1,512,768]{2,1,0:T(8,128)(2,1)} fusion(bf16[2,512,768]{2,1,0:T(8,128)(2,1)S(1)} %collective-permute-done.28, bf16[2,384,768]{2,1,0:T(8,128)(2,1)S(1)} %get-tuple-element.81, bf16[384,1024]{1,0:T(8,128)(2,1)S(1)} %get-tuple-element.71.rows), kind=kOutput, calls=%fused_computation.6 | convolution fusion | flops 303169536 | bytes 2555904 | tf_op jit(solution)/shard_map/dot_general | solution.py:23
  (66 shorter events, 1.9 us)
Async XLA Ops:
  3.0 8.5 %collective-permute-start.12 = (bf16[2,96,1024]{2,1,0:T(8,128)(2,1)}, bf16[2,96,1024]{2,1,0:T(8,128)(2,1)S(1)}, u32[]{:S(2)}, u32[]{:S(2)}) collective-permute-start(bf16[2,96,1024]{2,1,0:T(8,128)(2,1)} %get-tuple-element.56), channel_id=1, source_target_pairs={{0,1},{1,0},{2,3},{3,2},{4,5},{5,4},{6,7},{7,6},{8,9},{9,8},{10,11... | collective-permute-start | bytes 1179656 | tf_op jit(solution)/shard_map/ppermute | solution.py:50
  3.7 12.6 %collective-permute-start.9 = (bf16[1,512,768]{2,1,0:T(8,128)(2,1)}, bf16[1,512,768]{2,1,0:T(8,128)(2,1)S(1)}, u32[]{:S(2)}, u32[]{:S(2)}) collective-permute-start(bf16[1,512,768]{2,1,0:T(8,128)(2,1)} %up.1), channel_id=1, source_target_pairs={{0,8},{1,17},{2,10},{3,19},{4,12},{5,21},{6,14},{7,23},{8,0},{9,25... | collective-permute-start | bytes 2359304 | tf_op jit(solution)/shard_map/ppermute | solution.py:41
  7.3 2.6 %collective-permute-start = (bf16[2,96,1024]{2,1,0:T(8,128)(2,1)}, bf16[2,96,1024]{2,1,0:T(8,128)(2,1)S(1)}, u32[]{:S(2)}, u32[]{:S(2)}) collective-permute-start(bf16[2,96,1024]{2,1,0:T(8,128)(2,1)} %get-tuple-element.48), channel_id=1, source_target_pairs={{0,1},{1,0},{2,3},{3,2},{4,5},{5,4},{6,7},{7,6},{8,9},{9,8},{10,11... | collective-permute-start | bytes 1179656 | tf_op jit(solution)/shard_map/ppermute | solution.py:50
  7.3 22.2 %collective-permute-start.8 = (bf16[1,512,768]{2,1,0:T(8,128)(2,1)}, bf16[1,512,768]{2,1,0:T(8,128)(2,1)S(1)}, u32[]{:S(2)}, u32[]{:S(2)}) collective-permute-start(bf16[1,512,768]{2,1,0:T(8,128)(2,1)} %gate.1), channel_id=1, source_target_pairs={{0,8},{1,17},{2,10},{3,19},{4,12},{5,21},{6,14},{7,23},{8,0},{9,25... | collective-permute-start | bytes 2359304 | tf_op jit(solution)/shard_map/ppermute | solution.py:41
  10.0 11.3 %collective-permute-start.4 = (bf16[2,96,1024]{2,1,0:T(8,128)(2,1)S(1)}, bf16[2,96,1024]{2,1,0:T(8,128)(2,1)S(1)}, u32[]{:S(2)}, u32[]{:S(2)}) collective-permute-start(bf16[2,96,1024]{2,1,0:T(8,128)(2,1)S(1)} %pad_maximum_fusion), channel_id=1, source_target_pairs={{0,16},{1,9},{2,18},{3,11},{4,20},{5,13},{6,22},{7,15},{8,24},{9,1... | collective-permute-start | bytes 1179656 | tf_op jit(solution)/shard_map/ppermute | solution.py:45
  11.3 11.2 %collective-permute-start.3 = (bf16[1,48,1024]{2,1,0:T(8,128)(2,1)S(1)}, bf16[1,48,1024]{2,1,0:T(8,128)(2,1)S(1)}, u32[]{:S(2)}, u32[]{:S(2)}) collective-permute-start(bf16[1,48,1024]{2,1,0:T(8,128)(2,1)S(1)} %bitcast.125), channel_id=1, source_target_pairs={{0,6},{1,7},{2,4},{3,5},{4,2},{5,3},{6,0},{7,1},{8,14},{9,15},{10,... | collective-permute-start | bytes 294920 | tf_op jit(solution)/shard_map/ppermute | solution.py:50
  11.5 11.2 %collective-permute-start.2 = (bf16[1,48,1024]{2,1,0:T(8,128)(2,1)S(1)}, bf16[1,48,1024]{2,1,0:T(8,128)(2,1)S(1)}, u32[]{:S(2)}, u32[]{:S(2)}) collective-permute-start(bf16[1,48,1024]{2,1,0:T(8,128)(2,1)S(1)} %bitcast.124), channel_id=1, source_target_pairs={{0,4},{1,5},{2,6},{3,7},{4,0},{5,1},{6,2},{7,3},{8,12},{9,13},{10,... | collective-permute-start | bytes 294920 | tf_op jit(solution)/shard_map/ppermute | solution.py:50
  14.8 14.7 %copy-start.2 = (bf16[1,768,512]{2,1,0:T(8,128)(2,1)S(1)}, bf16[1,768,512]{2,1,0:T(8,128)(2,1)}, u32[]{:S(2)}) copy-start(bf16[1,768,512]{2,1,0:T(8,128)(2,1)} %down.1) | copy-start | bytes 2359300
  14.8 16.2 %copy-start = (bf16[1,512,768]{2,1,0:T(8,128)(2,1)S(1)}, bf16[1,512,768]{2,1,0:T(8,128)(2,1)}, u32[]{:S(2)}) copy-start(bf16[1,512,768]{2,1,0:T(8,128)(2,1)} %gate.1) | copy-start | bytes 2359300
  14.8 16.2 %copy-start.1 = (bf16[1,512,768]{2,1,0:T(8,128)(2,1)S(1)}, bf16[1,512,768]{2,1,0:T(8,128)(2,1)}, u32[]{:S(2)}) copy-start(bf16[1,512,768]{2,1,0:T(8,128)(2,1)} %up.1) | copy-start | bytes 2359300
  16.2 9.8 %collective-permute-start.1 = (bf16[1,48,1024]{2,1,0:T(8,128)(2,1)S(1)}, bf16[1,48,1024]{2,1,0:T(8,128)(2,1)S(1)}, u32[]{:S(2)}, u32[]{:S(2)}) collective-permute-start(bf16[1,48,1024]{2,1,0:T(8,128)(2,1)S(1)} %bitcast.123), channel_id=1, source_target_pairs={{0,2},{1,3},{2,0},{3,1},{4,6},{5,7},{6,4},{7,5},{8,10},{9,11},{10,... | collective-permute-start | bytes 294920 | tf_op jit(solution)/shard_map/ppermute | solution.py:50
  21.3 12.3 %collective-permute-start.13 = (bf16[2,96,1024]{2,1,0:T(8,128)(2,1)S(1)}, bf16[2,96,1024]{2,1,0:T(8,128)(2,1)S(1)}, u32[]{:S(2)}, u32[]{:S(2)}) collective-permute-start(bf16[2,96,1024]{2,1,0:T(8,128)(2,1)S(1)} %pad_maximum_fusion.1), channel_id=1, source_target_pairs={{0,16},{1,9},{2,18},{3,11},{4,20},{5,13},{6,22},{7,15},{8,24},{9,1... | collective-permute-start | bytes 1179656 | tf_op jit(solution)/shard_map/ppermute | solution.py:45
  22.6 8.4 %collective-permute-start.7 = (bf16[1,48,1024]{2,1,0:T(8,128)(2,1)S(1)}, bf16[1,48,1024]{2,1,0:T(8,128)(2,1)S(1)}, u32[]{:S(2)}, u32[]{:S(2)}) collective-permute-start(bf16[1,48,1024]{2,1,0:T(8,128)(2,1)S(1)} %bitcast.128), channel_id=1, source_target_pairs={{0,6},{1,7},{2,4},{3,5},{4,2},{5,3},{6,0},{7,1},{8,14},{9,15},{10,... | collective-permute-start | bytes 294920 | tf_op jit(solution)/shard_map/ppermute | solution.py:50
  22.8 8.2 %collective-permute-start.6 = (bf16[1,48,1024]{2,1,0:T(8,128)(2,1)S(1)}, bf16[1,48,1024]{2,1,0:T(8,128)(2,1)S(1)}, u32[]{:S(2)}, u32[]{:S(2)}) collective-permute-start(bf16[1,48,1024]{2,1,0:T(8,128)(2,1)S(1)} %bitcast.127), channel_id=1, source_target_pairs={{0,4},{1,5},{2,6},{3,7},{4,0},{5,1},{6,2},{7,3},{8,12},{9,13},{10,... | collective-permute-start | bytes 294920 | tf_op jit(solution)/shard_map/ppermute | solution.py:50
  26.0 5.0 %collective-permute-start.5 = (bf16[1,48,1024]{2,1,0:T(8,128)(2,1)S(1)}, bf16[1,48,1024]{2,1,0:T(8,128)(2,1)S(1)}, u32[]{:S(2)}, u32[]{:S(2)}) collective-permute-start(bf16[1,48,1024]{2,1,0:T(8,128)(2,1)S(1)} %bitcast.126), channel_id=1, source_target_pairs={{0,2},{1,3},{2,0},{3,1},{4,6},{5,7},{6,4},{7,5},{8,10},{9,11},{10,... | collective-permute-start | bytes 294920 | tf_op jit(solution)/shard_map/ppermute | solution.py:50
  29.5 20.4 %collective-permute-start.11 = (bf16[1,768,512]{2,1,0:T(8,128)(2,1)S(1)}, bf16[1,768,512]{2,1,0:T(8,128)(2,1)S(1)}, u32[]{:S(2)}, u32[]{:S(2)}) collective-permute-start(bf16[1,768,512]{2,1,0:T(8,128)(2,1)S(1)} %copy-done.2), channel_id=1, source_target_pairs={{0,8},{1,17},{2,10},{3,19},{4,12},{5,21},{6,14},{7,23},{8,0},{9,25... | collective-permute-start | bytes 2359304 | tf_op jit(solution)/shard_map/ppermute | solution.py:41
  33.4 23.2 %collective-permute-start.10 = (bf16[2,384,768]{2,1,0:T(8,128)(2,1)S(1)}, bf16[2,384,768]{2,1,0:T(8,128)(2,1)S(1)}, u32[]{:S(2)}, u32[]{:S(2)}) collective-permute-start(bf16[2,384,768]{2,1,0:T(8,128)(2,1)S(1)} %get-tuple-element.53), channel_id=1, source_target_pairs={{0,16},{1,9},{2,18},{3,11},{4,20},{5,13},{6,22},{7,15},{8,24},{9,1... | collective-permute-start | bytes 3538952 | tf_op jit(solution)/shard_map/ppermute | solution.py:45
  33.6 9.5 %collective-permute-start.16 = (bf16[2,48,1024]{2,1,0:T(8,128)(2,1)S(1)}, bf16[2,48,1024]{2,1,0:T(8,128)(2,1)S(1)}, u32[]{:S(2)}, u32[]{:S(2)}) collective-permute-start(bf16[2,48,1024]{2,1,0:T(8,128)(2,1)S(1)} %pad_maximum_fusion.11), channel_id=1, source_target_pairs={{0,6},{1,7},{2,4},{3,5},{4,2},{5,3},{6,0},{7,1},{8,14},{9,15},{10,... | collective-permute-start | bytes 589832 | tf_op jit(solution)/shard_map/ppermute | solution.py:50
  34.6 15.0 %collective-permute-start.15 = (bf16[2,48,1024]{2,1,0:T(8,128)(2,1)S(1)}, bf16[2,48,1024]{2,1,0:T(8,128)(2,1)S(1)}, u32[]{:S(2)}, u32[]{:S(2)}) collective-permute-start(bf16[2,48,1024]{2,1,0:T(8,128)(2,1)S(1)} %pad_maximum_fusion.10), channel_id=1, source_target_pairs={{0,4},{1,5},{2,6},{3,7},{4,0},{5,1},{6,2},{7,3},{8,12},{9,13},{10,... | collective-permute-start | bytes 589832 | tf_op jit(solution)/shard_map/ppermute | solution.py:50
  37.1 12.8 %collective-permute-start.14 = (bf16[2,48,1024]{2,1,0:T(8,128)(2,1)S(1)}, bf16[2,48,1024]{2,1,0:T(8,128)(2,1)S(1)}, u32[]{:S(2)}, u32[]{:S(2)}) collective-permute-start(bf16[2,48,1024]{2,1,0:T(8,128)(2,1)S(1)} %pad_maximum_fusion.9), channel_id=1, source_target_pairs={{0,2},{1,3},{2,0},{3,1},{4,6},{5,7},{6,4},{7,5},{8,10},{9,11},{10,... | collective-permute-start | bytes 589832 | tf_op jit(solution)/shard_map/ppermute | solution.py:50
  51.3 13.2 %collective-permute-start.20 = (bf16[384,768]{1,0:T(8,128)(2,1)S(1)}, bf16[384,768]{1,0:T(8,128)(2,1)S(1)}, u32[]{:S(2)}, u32[]{:S(2)}) collective-permute-start(bf16[384,768]{1,0:T(8,128)(2,1)S(1)} %get-tuple-element.68), channel_id=1, source_target_pairs={{0,16},{1,9},{2,18},{3,11},{4,20},{5,13},{6,22},{7,15},{8,24},{9,1... | collective-permute-start | bytes 1769480 | tf_op jit(solution)/shard_map/ppermute | solution.py:45
  58.9 47.9 %collective-permute-start.29 = (bf16[768,512]{1,0:T(8,128)(2,1)S(1)}, bf16[768,512]{1,0:T(8,128)(2,1)S(1)}, u32[]{:S(2)}, u32[]{:S(2)}) collective-permute-start(bf16[768,512]{1,0:T(8,128)(2,1)S(1)} %get-tuple-element.84), channel_id=1, source_target_pairs={{0,8},{1,17},{2,10},{3,19},{4,12},{5,21},{6,14},{7,23},{8,0},{9,25... | collective-permute-start | bytes 2359304 | tf_op jit(solution)/shard_map/ppermute | solution.py:41
  59.4 9.8 %collective-permute-start.17 = (bf16[2,48,1024]{2,1,0:T(8,128)(2,1)S(1)}, bf16[2,48,1024]{2,1,0:T(8,128)(2,1)S(1)}, u32[]{:S(2)}, u32[]{:S(2)}) collective-permute-start(bf16[2,48,1024]{2,1,0:T(8,128)(2,1)S(1)} %get-tuple-element.64), channel_id=1, source_target_pairs={{0,2},{1,3},{2,0},{3,1},{4,6},{5,7},{6,4},{7,5},{8,10},{9,11},{10,... | collective-permute-start | bytes 589832 | tf_op jit(solution)/shard_map/ppermute | solution.py:50
  60.7 10.3 %collective-permute-start.18 = (bf16[2,48,1024]{2,1,0:T(8,128)(2,1)S(1)}, bf16[2,48,1024]{2,1,0:T(8,128)(2,1)S(1)}, u32[]{:S(2)}, u32[]{:S(2)}) collective-permute-start(bf16[2,48,1024]{2,1,0:T(8,128)(2,1)S(1)} %get-tuple-element.65), channel_id=1, source_target_pairs={{0,4},{1,5},{2,6},{3,7},{4,0},{5,1},{6,2},{7,3},{8,12},{9,13},{10,... | collective-permute-start | bytes 589832 | tf_op jit(solution)/shard_map/ppermute | solution.py:50
  61.5 22.5 %collective-permute-start.19 = (bf16[2,48,1024]{2,1,0:T(8,128)(2,1)S(1)}, bf16[2,48,1024]{2,1,0:T(8,128)(2,1)S(1)}, u32[]{:S(2)}, u32[]{:S(2)}) collective-permute-start(bf16[2,48,1024]{2,1,0:T(8,128)(2,1)S(1)} %get-tuple-element.66), channel_id=1, source_target_pairs={{0,6},{1,7},{2,4},{3,5},{4,2},{5,3},{6,0},{7,1},{8,14},{9,15},{10,... | collective-permute-start | bytes 589832 | tf_op jit(solution)/shard_map/ppermute | solution.py:50
  69.2 40.4 %collective-permute-start.28 = (bf16[2,512,768]{2,1,0:T(8,128)(2,1)S(1)}, bf16[2,512,768]{2,1,0:T(8,128)(2,1)S(1)}, u32[]{:S(2)}, u32[]{:S(2)}) collective-permute-start(bf16[2,512,768]{2,1,0:T(8,128)(2,1)S(1)} %get-tuple-element.83), channel_id=1, source_target_pairs={{0,8},{1,17},{2,10},{3,19},{4,12},{5,21},{6,14},{7,23},{8,0},{9,25... | collective-permute-start | bytes 4718600 | tf_op jit(solution)/shard_map/ppermute | solution.py:41
  70.2 14.1 %collective-permute-start.23 = (bf16[2,48,1024]{2,1,0:T(8,128)(2,1)S(1)}, bf16[2,48,1024]{2,1,0:T(8,128)(2,1)S(1)}, u32[]{:S(2)}, u32[]{:S(2)}) collective-permute-start(bf16[2,48,1024]{2,1,0:T(8,128)(2,1)S(1)} %get-tuple-element.75), channel_id=1, source_target_pairs={{0,2},{1,3},{2,0},{3,1},{4,6},{5,7},{6,4},{7,5},{8,10},{9,11},{10,... | collective-permute-start | bytes 589832 | tf_op jit(solution)/shard_map/ppermute | solution.py:50
  71.0 20.0 %collective-permute-start.24 = (bf16[2,48,1024]{2,1,0:T(8,128)(2,1)S(1)}, bf16[2,48,1024]{2,1,0:T(8,128)(2,1)S(1)}, u32[]{:S(2)}, u32[]{:S(2)}) collective-permute-start(bf16[2,48,1024]{2,1,0:T(8,128)(2,1)S(1)} %get-tuple-element.77), channel_id=1, source_target_pairs={{0,4},{1,5},{2,6},{3,7},{4,0},{5,1},{6,2},{7,3},{8,12},{9,13},{10,... | collective-permute-start | bytes 589832 | tf_op jit(solution)/shard_map/ppermute | solution.py:50
  84.0 12.6 %collective-permute-start.25 = (bf16[2,48,1024]{2,1,0:T(8,128)(2,1)S(1)}, bf16[2,48,1024]{2,1,0:T(8,128)(2,1)S(1)}, u32[]{:S(2)}, u32[]{:S(2)}) collective-permute-start(bf16[2,48,1024]{2,1,0:T(8,128)(2,1)S(1)} %get-tuple-element.79), channel_id=1, source_target_pairs={{0,6},{1,7},{2,4},{3,5},{4,2},{5,3},{6,0},{7,1},{8,14},{9,15},{10,... | collective-permute-start | bytes 589832 | tf_op jit(solution)/shard_map/ppermute | solution.py:50
  84.3 13.4 %collective-permute-start.21 = (bf16[4,48,1024]{2,1,0:T(8,128)(2,1)S(1)}, bf16[4,48,1024]{2,1,0:T(8,128)(2,1)S(1)}, u32[]{:S(2)}, u32[]{:S(2)}) collective-permute-start(bf16[4,48,1024]{2,1,0:T(8,128)(2,1)S(1)} %get-tuple-element.73), channel_id=1, source_target_pairs={{0,16},{1,9},{2,18},{3,11},{4,20},{5,13},{6,22},{7,15},{8,24},{9,1... | collective-permute-start | bytes 1179656 | tf_op jit(solution)/shard_map/ppermute | solution.py:45
  96.8 7.0 %collective-permute-start.26 = (bf16[4,48,1024]{2,1,0:T(8,128)(2,1)S(1)}, bf16[4,48,1024]{2,1,0:T(8,128)(2,1)S(1)}, u32[]{:S(2)}, u32[]{:S(2)}) collective-permute-start(bf16[4,48,1024]{2,1,0:T(8,128)(2,1)S(1)} %pad_maximum_fusion.6), channel_id=1, source_target_pairs={{0,16},{1,9},{2,18},{3,11},{4,20},{5,13},{6,22},{7,15},{8,24},{9,1... | collective-permute-start | bytes 1179656 | tf_op jit(solution)/shard_map/ppermute | solution.py:45
  97.7 6.2 %copy-start.3 = (bf16[128,192]{1,0:T(8,128)(2,1)S(1)}, bf16[128,192]{1,0:T(8,128)(2,1)}, u32[]{:S(2)}) copy-start(bf16[128,192]{1,0:T(8,128)(2,1)} %get-tuple-element.45.pick) | copy-start | bytes 147460
  97.7 6.2 %copy-start.4 = (f32[128,128]{1,0:T(8,128)S(1)}, f32[128,128]{1,0:T(8,128)}, u32[]{:S(2)}) copy-start(f32[128,128]{1,0:T(8,128)} %get-tuple-element.46.weight) | copy-start | bytes 196612
  97.7 6.1 %collective-permute-start.22 = (bf16[2,96,1024]{2,1,0:T(8,128)(2,1)S(1)}, bf16[2,96,1024]{2,1,0:T(8,128)(2,1)S(1)}, u32[]{:S(2)}, u32[]{:S(2)}) collective-permute-start(bf16[2,96,1024]{2,1,0:T(8,128)(2,1)S(1)} %pad_maximum_fusion.4), channel_id=1, source_target_pairs={{0,1},{1,0},{2,3},{3,2},{4,5},{5,4},{6,7},{7,6},{8,9},{9,8},{10,11... | collective-permute-start | bytes 1179656 | tf_op jit(solution)/shard_map/ppermute | solution.py:50
  105.1 3.2 %collective-permute-start.27 = (bf16[2,96,1024]{2,1,0:T(8,128)(2,1)S(1)}, bf16[2,96,1024]{2,1,0:T(8,128)(2,1)S(1)}, u32[]{:S(2)}, u32[]{:S(2)}) collective-permute-start(bf16[2,96,1024]{2,1,0:T(8,128)(2,1)S(1)} %pad_maximum_fusion.7), channel_id=1, source_target_pairs={{0,1},{1,0},{2,3},{3,2},{4,5},{5,4},{6,7},{7,6},{8,9},{9,8},{10,11... | collective-permute-start | bytes 1179656 | tf_op jit(solution)/shard_map/ppermute | solution.py:50

commit v5 on v4

--- a/solution.py
+++ b/solution.py
@@ -509,7 +509,7 @@
     )
     out_parts = swap_chips(cut(slot_out), chips)
     sent = [part for k, part in enumerate(out_parts) if k % chips]
-    got_down = swap_weight(far_grad_down)
+    got_down = swap_weight(after(far_grad_down, *(got_grad,)))
     grads, far_grads, *slot_grad = slot_grad_parts(
         own,
         got,
@@ -528,7 +528,7 @@
         if k % chips:
             value = after(grad_out_parts[k], out_parts[k % chips])
             grad_out_parts[k] = swap_expert(value, 2 * (k % chips))
-    got_far = swap_weight(after(far_grads, *sent[:1]))
+    got_far = swap_weight(after(far_grads, *sent[1:2]))
 
     grad_w_gate = contract_first(rows[:, :block], grads[0]) + got_far[0].astype(F32)
     grad_w_up = contract_first(rows[:, :block], grads[1]) + got_far[1].astype(F32)

time: 114 us -> 112 us (0.982); the launches traced: 113 us -> 112 us
  starting transfers between devices: 36.7 us -> 31.6 us
  waiting for transfers between devices: 49.4 us -> 53.7 us
    ppermute x19, starting transfers between devices: 26.2 us -> 21.5 us  [swap_expert(): lax.ppermute(value, 'expert', [(i, i ^ mask) for i in range(experts)])]
    ppermute x19, waiting for transfers between devices: 30.1 us -> 34.3 us  [swap_expert(): lax.ppermute(value, 'expert', [(i, i ^ mask) for i in range(experts)])]
  transfers between devices with their start and end apart: 30 -> 30, of which waited for: 12 -> 13; matrix products, arithmetic and copies ran while one was open for 4% -> 4% of each run, Pallas kernels for 14% -> 14%
where the time goes in v5:
time: 112 us
  waiting for transfers between devices  53.7 us (48%)
  starting transfers between devices  31.6 us (28%)
  Pallas kernels  18 us (16%)
  matrix products  4.44 us (4%)
  local copies, waits for them, and re-layouts  2.46 us (2%)
    ppermute x19, waiting for transfers between devices, swap_expert(): lax.ppermute(value, 'expert', [(i, i ^ mask) for i in range(experts)])  34.3 us
    ppermute x19, starting transfers between devices, swap_expert(): lax.ppermute(value, 'expert', [(i, i ^ mask) for i in range(experts)])  21.5 us
    ppermute x6, waiting for transfers between devices, swap_rows(): return lax.ppermute(value, BOTH, pair_list(lax.axis_size('expert'), (2, 1)))  14.6 us
    ppermute x6, starting transfers between devices, swap_rows(): return lax.ppermute(value, BOTH, pair_list(lax.axis_size('expert'), (2, 1)))  5.08 us
    ppermute x5, starting transfers between devices, swap_weight(): return lax.ppermute(value, BOTH, pair_list(lax.axis_size('expert'), (1, 2)))  4.99 us
    ppermute x5, waiting for transfers between devices, swap_weight(): return lax.ppermute(value, BOTH, pair_list(lax.axis_size('expert'), (1, 2)))  4.8 us
    pallas_call x1, Pallas kernels, slot_grad_parts(): pl.pallas_call(functools.partial(slot_grad_kernel, places), grid=(hidden...  4.63 us
    dot_general x3, matrix products, contract_first(): lax.dot_general(left_side, right_side, (((0,), (0,)), ((), ())), preferre...  4.44 us
  transfers between devices with their start and end apart: 30, of which 13 were waited for; matrix products, arithmetic and copies ran while one was open for 4% of the time, Pallas kernels for 14%

profile of v5, /device:TPU:19, one launch (start us, length us, event | category | flops | bytes accessed | tf_op | source)
XLA Modules:
  0.0 111.7 jit_solution(645547771358432563)
XLA Ops:
  0.6 2.4 %make_grads.1 = (bf16[2,96,1024]{2,1,0:T(8,128)(2,1)}, bf16[2,96,1024]{2,1,0:T(8,128)(2,1)}, bf16[128,192]{1,0:T(8,128)(2,1)}, f32[128,128]{1,0:T(8,128)}) custom-call(bf16[128,2048]{1,0:T(8,128)(2,1)} %cot.1, s32[1,128]{1,0:T(1,128)} %bitcast.129, s32[1,128]{1,0:T(1,128)} %bitcast.131), custom_call_target="tpu_custom_call" | custom-call | flops 10000000 | bytes 30000 | tf_op jit(solution)/shard_map/make_grads/pallas_call | solution.py:141
  3.0 0.7 collective-permute-start.12
  3.7 1.2 %collective-permute-start.9 = (bf16[1,512,768]{2,1,0:T(8,128)(2,1)}, bf16[1,512,768]{2,1,0:T(8,128)(2,1)S(1)}, u32[]{:S(2)}, u32[]{:S(2)}) collective-permute-start(bf16[1,512,768]{2,1,0:T(8,128)(2,1)} %up.1), channel_id=1, source_target_pairs={{0,8},{1,17},{2,10},{3,19},{4,12},{5,21},{6,14},{7,23},{8,0},{9,25... | collective-permute-start | bytes 2359304 | tf_op jit(solution)/shard_map/ppermute | solution.py:41
  4.9 2.3 %make_slots.1 = (bf16[2,96,1024]{2,1,0:T(8,128)(2,1)}, bf16[2,96,1024]{2,1,0:T(8,128)(2,1)}) custom-call(bf16[128,2048]{1,0:T(8,128)(2,1)} %tok.1, s32[1,128]{1,0:T(1,128)} %bitcast.130, s32[1,128]{1,0:T(1,128)} %bitcast.132), custom_call_target="tpu_custom_call" | custom-call | flops 10000000 | bytes 30000 | tf_op jit(solution)/shard_map/make_slots/pallas_call | solution.py:129
  7.3 0.5 collective-permute-start.8
  7.8 1.0 fusion.29
  8.9 1.1 fusion.32
  10.0 1.3 %collective-permute-start.4 = (bf16[2,96,1024]{2,1,0:T(8,128)(2,1)S(1)}, bf16[2,96,1024]{2,1,0:T(8,128)(2,1)S(1)}, u32[]{:S(2)}, u32[]{:S(2)}) collective-permute-start(bf16[2,96,1024]{2,1,0:T(8,128)(2,1)S(1)} %pad_maximum_fusion), channel_id=1, source_target_pairs={{0,16},{1,9},{2,18},{3,11},{4,20},{5,13},{6,22},{7,15},{8,24},{9,1... | collective-permute-start | bytes 1179656 | tf_op jit(solution)/shard_map/ppermute | solution.py:45
  11.5 3.2 %collective-permute-start.2 = (bf16[1,48,1024]{2,1,0:T(8,128)(2,1)S(1)}, bf16[1,48,1024]{2,1,0:T(8,128)(2,1)S(1)}, u32[]{:S(2)}, u32[]{:S(2)}) collective-permute-start(bf16[1,48,1024]{2,1,0:T(8,128)(2,1)S(1)} %bitcast.124), channel_id=1, source_target_pairs={{0,4},{1,5},{2,6},{3,7},{4,0},{5,1},{6,2},{7,3},{8,12},{9,13},{10,... | collective-permute-start | bytes 294920 | tf_op jit(solution)/shard_map/ppermute | solution.py:50
  14.9 1.4 %collective-permute-done.9.refs_11_.far_up = bf16[1,512,768]{2,1,0:T(8,128)(2,1)S(1)} collective-permute-done((bf16[1,512,768]{2,1,0:T(8,128)(2,1)}, bf16[1,512,768]{2,1,0:T(8,128)(2,1)S(1)}, u32[]{:S(2)}, u32[]{:S(2)}) %collective-permute-start.9) | collective-permute-done | bytes 786464 | tf_op jit(solution)/shard_map/ppermute | solution.py:41
  16.2 1.3 %collective-permute-start.1 = (bf16[1,48,1024]{2,1,0:T(8,128)(2,1)S(1)}, bf16[1,48,1024]{2,1,0:T(8,128)(2,1)S(1)}, u32[]{:S(2)}, u32[]{:S(2)}) collective-permute-start(bf16[1,48,1024]{2,1,0:T(8,128)(2,1)S(1)} %bitcast.123), channel_id=1, source_target_pairs={{0,2},{1,3},{2,0},{3,1},{4,6},{5,7},{6,4},{7,5},{8,10},{9,11},{10,... | collective-permute-start | bytes 294920 | tf_op jit(solution)/shard_map/ppermute | solution.py:50
  17.6 3.7 %collective-permute-done.4 = bf16[2,96,1024]{2,1,0:T(8,128)(2,1)S(1)} collective-permute-done((bf16[2,96,1024]{2,1,0:T(8,128)(2,1)S(1)}, bf16[2,96,1024]{2,1,0:T(8,128)(2,1)S(1)}, u32[]{:S(2)}, u32[]{:S(2)}) %collective-permute-start.4) | collective-permute-done | bytes 393248 | tf_op jit(solution)/shard_map/ppermute | solution.py:45
  21.3 1.2 %collective-permute-start.13 = (bf16[2,96,1024]{2,1,0:T(8,128)(2,1)S(1)}, bf16[2,96,1024]{2,1,0:T(8,128)(2,1)S(1)}, u32[]{:S(2)}, u32[]{:S(2)}) collective-permute-start(bf16[2,96,1024]{2,1,0:T(8,128)(2,1)S(1)} %pad_maximum_fusion.1), channel_id=1, source_target_pairs={{0,16},{1,9},{2,18},{3,11},{4,20},{5,13},{6,22},{7,15},{8,24},{9,1... | collective-permute-start | bytes 1179656 | tf_op jit(solution)/shard_map/ppermute | solution.py:45
  22.8 3.2 %collective-permute-start.6 = (bf16[1,48,1024]{2,1,0:T(8,128)(2,1)S(1)}, bf16[1,48,1024]{2,1,0:T(8,128)(2,1)S(1)}, u32[]{:S(2)}, u32[]{:S(2)}) collective-permute-start(bf16[1,48,1024]{2,1,0:T(8,128)(2,1)S(1)} %bitcast.127), channel_id=1, source_target_pairs={{0,4},{1,5},{2,6},{3,7},{4,0},{5,1},{6,2},{7,3},{8,12},{9,13},{10,... | collective-permute-start | bytes 294920 | tf_op jit(solution)/shard_map/ppermute | solution.py:50
  26.0 3.4 %collective-permute-done.8.refs_10_.far_gate = bf16[1,512,768]{2,1,0:T(8,128)(2,1)S(1)} collective-permute-done((bf16[1,512,768]{2,1,0:T(8,128)(2,1)}, bf16[1,512,768]{2,1,0:T(8,128)(2,1)S(1)}, u32[]{:S(2)}, u32[]{:S(2)}) %collective-permute-start.8) | collective-permute-done | bytes 786464 | tf_op jit(solution)/shard_map/ppermute | solution.py:41
  29.5 1.5 %collective-permute-start.11 = (bf16[1,768,512]{2,1,0:T(8,128)(2,1)S(1)}, bf16[1,768,512]{2,1,0:T(8,128)(2,1)S(1)}, u32[]{:S(2)}, u32[]{:S(2)}) collective-permute-start(bf16[1,768,512]{2,1,0:T(8,128)(2,1)S(1)} %copy-done.2), channel_id=1, source_target_pairs={{0,8},{1,17},{2,10},{3,19},{4,12},{5,21},{6,14},{7,23},{8,0},{9,25... | collective-permute-start | bytes 2359304 | tf_op jit(solution)/shard_map/ppermute | solution.py:41
  31.0 2.4 %gate_up_parts.1 = (bf16[384,1024]{1,0:T(8,128)(2,1)S(1)}, f32[2,384,768]{2,1,0:T(8,128)S(1)}, bf16[2,384,768]{2,1,0:T(8,128)(2,1)S(1)}) custom-call(bf16[1,48,1024]{2,1,0:T(8,128)(2,1)S(1)} %bitcast.93, bf16[1,48,1024]{2,1,0:T(8,128)(2,1)S(1)} %collective-permute-done.1.refs_1_, bf16[1,48,1024]{2,1,0:T(8,128)(2,1)S(1)} %collective-permute-done.2.refs_2_, ...), custom_call_target="tpu_custom_call" | custom-call | flops 10000000 | bytes 30000 | tf_op jit(solution)/shard_map/gate_up_parts/pallas_call | solution.py:203
  33.6 1.0 collective-permute-start.16
  34.6 2.5 %collective-permute-start.15 = (bf16[2,48,1024]{2,1,0:T(8,128)(2,1)S(1)}, bf16[2,48,1024]{2,1,0:T(8,128)(2,1)S(1)}, u32[]{:S(2)}, u32[]{:S(2)}) collective-permute-start(bf16[2,48,1024]{2,1,0:T(8,128)(2,1)S(1)} %pad_maximum_fusion.10), channel_id=1, source_target_pairs={{0,4},{1,5},{2,6},{3,7},{4,0},{5,1},{6,2},{7,3},{8,12},{9,13},{10,... | collective-permute-start | bytes 589832 | tf_op jit(solution)/shard_map/ppermute | solution.py:50
  37.1 1.0 collective-permute-start.14
  38.2 4.9 %collective-permute-done.16.refs_3_ = bf16[2,48,1024]{2,1,0:T(8,128)(2,1)S(1)} collective-permute-done((bf16[2,48,1024]{2,1,0:T(8,128)(2,1)S(1)}, bf16[2,48,1024]{2,1,0:T(8,128)(2,1)S(1)}, u32[]{:S(2)}, u32[]{:S(2)}) %collective-permute-start.16) | collective-permute-done | bytes 196640 | tf_op jit(solution)/shard_map/ppermute | solution.py:50
  43.1 6.5 %collective-permute-done.15.refs_2_ = bf16[2,48,1024]{2,1,0:T(8,128)(2,1)S(1)} collective-permute-done((bf16[2,48,1024]{2,1,0:T(8,128)(2,1)S(1)}, bf16[2,48,1024]{2,1,0:T(8,128)(2,1)S(1)}, u32[]{:S(2)}, u32[]{:S(2)}) %collective-permute-start.15) | collective-permute-done | bytes 196640 | tf_op jit(solution)/shard_map/ppermute | solution.py:50
  49.6 0.3 collective-permute-done.14.refs_1_
  49.9 1.4 %grad_hidden_parts.1 = (bf16[384,1024]{1,0:T(8,128)(2,1)S(1)}, f32[384,768]{1,0:T(8,128)S(1)}, bf16[384,768]{1,0:T(8,128)(2,1)S(1)}) custom-call(bf16[2,48,1024]{2,1,0:T(8,128)(2,1)S(1)} %pad_maximum_fusion.8.refs_0_, bf16[2,48,1024]{2,1,0:T(8,128)(2,1)S(1)} %collective-permute-done.14.refs_1_, bf16[2,48,1024]{2,1,0:T(8,128)(2,1)S(1)} %collective-permute-done.15.refs_2_, ...), custom_call_target="tpu_custom_call" | custom-call | flops 1000000000 | bytes 3000000 | tf_op jit(solution)/shard_map/grad_hidden_parts/pallas_call | solution.py:244
  51.3 1.4 %collective-permute-start.20 = (bf16[384,768]{1,0:T(8,128)(2,1)S(1)}, bf16[384,768]{1,0:T(8,128)(2,1)S(1)}, u32[]{:S(2)}, u32[]{:S(2)}) collective-permute-start(bf16[384,768]{1,0:T(8,128)(2,1)S(1)} %get-tuple-element.69), channel_id=1, source_target_pairs={{0,16},{1,9},{2,18},{3,11},{4,20},{5,13},{6,22},{7,15},{8,24},{9,1... | collective-permute-start | bytes 1769480 | tf_op jit(solution)/shard_map/ppermute | solution.py:45
  52.7 3.8 %collective-permute-done.10.got = bf16[2,384,768]{2,1,0:T(8,128)(2,1)S(1)} collective-permute-done((bf16[2,384,768]{2,1,0:T(8,128)(2,1)S(1)}, bf16[2,384,768]{2,1,0:T(8,128)(2,1)S(1)}, u32[]{:S(2)}, u32[]{:S(2)}) %collective-permute-start.10) | collective-permute-done | bytes 1179680 | tf_op jit(solution)/shard_map/ppermute | solution.py:45
  56.5 2.4 %slot_out.1 = (bf16[384,768]{1,0:T(8,128)(2,1)S(1)}, bf16[768,512]{1,0:T(8,128)(2,1)S(1)}, bf16[2,48,1024]{2,1,0:T(8,128)(2,1)S(1)}, bf16[2,48,1024]{2,1,0:T(8,1...) custom-call(f32[2,384,768]{2,1,0:T(8,128)S(1)} %get-tuple-element.53.own, ...), custom_call_target="tpu_custom_call" | custom-call | flops 10000000 | bytes 30000 | tf_op jit(solution)/shard_map/slot_out/pallas_call | solution.py:292
  59.1 1.4 %collective-permute-start.17 = (bf16[2,48,1024]{2,1,0:T(8,128)(2,1)S(1)}, bf16[2,48,1024]{2,1,0:T(8,128)(2,1)S(1)}, u32[]{:S(2)}, u32[]{:S(2)}) collective-permute-start(bf16[2,48,1024]{2,1,0:T(8,128)(2,1)S(1)} %get-tuple-element.65), channel_id=1, source_target_pairs={{0,2},{1,3},{2,0},{3,1},{4,6},{5,7},{6,4},{7,5},{8,10},{9,11},{10,... | collective-permute-start | bytes 589832 | tf_op jit(solution)/shard_map/ppermute | solution.py:50
  60.4 1.2 %collective-permute-start.19 = (bf16[2,48,1024]{2,1,0:T(8,128)(2,1)S(1)}, bf16[2,48,1024]{2,1,0:T(8,128)(2,1)S(1)}, u32[]{:S(2)}, u32[]{:S(2)}) collective-permute-start(bf16[2,48,1024]{2,1,0:T(8,128)(2,1)S(1)} %get-tuple-element.67), channel_id=1, source_target_pairs={{0,6},{1,7},{2,4},{3,5},{4,2},{5,3},{6,0},{7,1},{8,14},{9,15},{10,... | collective-permute-start | bytes 589832 | tf_op jit(solution)/shard_map/ppermute | solution.py:50
  61.7 1.5 %collective-permute-done.20.got_grad = bf16[384,768]{1,0:T(8,128)(2,1)S(1)} collective-permute-done((bf16[384,768]{1,0:T(8,128)(2,1)S(1)}, bf16[384,768]{1,0:T(8,128)(2,1)S(1)}, u32[]{:S(2)}, u32[]{:S(2)}) %collective-permute-start.20) | collective-permute-done | bytes 589856 | tf_op jit(solution)/shard_map/ppermute | solution.py:45
  63.2 0.4 collective-permute-start.29
  63.6 4.6 %slot_grad.1 = (bf16[2,384,768]{2,1,0:T(8,128)(2,1)S(1)}, bf16[2,512,768]{2,1,0:T(8,128)(2,1)S(1)}, bf16[2,48,1024]{2,1,0:T(8,128)(2,1)S(1)}, bf16[2,48,1024]{2,...) custom-call(f32[2,384,768]{2,1,0:T(8,128)S(1)} %get-tuple-element.53.own, ...), custom_call_target="tpu_custom_call" | custom-call | tf_op jit(solution)/shard_map/slot_grad/pallas_call | solution.py:360
  68.2 1.3 %collective-permute-start.28 = (bf16[2,512,768]{2,1,0:T(8,128)(2,1)S(1)}, bf16[2,512,768]{2,1,0:T(8,128)(2,1)S(1)}, u32[]{:S(2)}, u32[]{:S(2)}) collective-permute-start(bf16[2,512,768]{2,1,0:T(8,128)(2,1)S(1)} %get-tuple-element.84), channel_id=1, source_target_pairs={{0,8},{1,17},{2,10},{3,19},{4,12},{5,21},{6,14},{7,23},{8,0},{9,25... | collective-permute-start | bytes 4718600 | tf_op jit(solution)/shard_map/ppermute | solution.py:41
  69.5 0.6 collective-permute-done.17
  70.1 2.5 %collective-permute-start.23 = (bf16[2,48,1024]{2,1,0:T(8,128)(2,1)S(1)}, bf16[2,48,1024]{2,1,0:T(8,128)(2,1)S(1)}, u32[]{:S(2)}, u32[]{:S(2)}) collective-permute-start(bf16[2,48,1024]{2,1,0:T(8,128)(2,1)S(1)} %get-tuple-element.76), channel_id=1, source_target_pairs={{0,2},{1,3},{2,0},{3,1},{4,6},{5,7},{6,4},{7,5},{8,10},{9,11},{10,... | collective-permute-start | bytes 589832 | tf_op jit(solution)/shard_map/ppermute | solution.py:50
  72.6 0.5 collective-permute-start.24
  73.1 9.3 %collective-permute-done.19 = bf16[2,48,1024]{2,1,0:T(8,128)(2,1)S(1)} collective-permute-done((bf16[2,48,1024]{2,1,0:T(8,128)(2,1)S(1)}, bf16[2,48,1024]{2,1,0:T(8,128)(2,1)S(1)}, u32[]{:S(2)}, u32[]{:S(2)}) %collective-permute-start.19) | collective-permute-done | bytes 196640 | tf_op jit(solution)/shard_map/ppermute | solution.py:50
  82.7 0.9 collective-permute-start.21
  83.6 4.3 %collective-permute-done.24 = bf16[2,48,1024]{2,1,0:T(8,128)(2,1)S(1)} collective-permute-done((bf16[2,48,1024]{2,1,0:T(8,128)(2,1)S(1)}, bf16[2,48,1024]{2,1,0:T(8,128)(2,1)S(1)}, u32[]{:S(2)}, u32[]{:S(2)}) %collective-permute-start.24) | collective-permute-done | bytes 196640 | tf_op jit(solution)/shard_map/ppermute | solution.py:50
  87.9 8.4 %collective-permute-done.25 = bf16[2,48,1024]{2,1,0:T(8,128)(2,1)S(1)} collective-permute-done((bf16[2,48,1024]{2,1,0:T(8,128)(2,1)S(1)}, bf16[2,48,1024]{2,1,0:T(8,128)(2,1)S(1)}, u32[]{:S(2)}, u32[]{:S(2)}) %collective-permute-start.25) | collective-permute-done | bytes 196640 | tf_op jit(solution)/shard_map/ppermute | solution.py:50
  96.6 1.1 %collective-permute-start.22 = (bf16[2,96,1024]{2,1,0:T(8,128)(2,1)S(1)}, bf16[2,96,1024]{2,1,0:T(8,128)(2,1)S(1)}, u32[]{:S(2)}, u32[]{:S(2)}) collective-permute-start(bf16[2,96,1024]{2,1,0:T(8,128)(2,1)S(1)} %pad_maximum_fusion.4), channel_id=1, source_target_pairs={{0,1},{1,0},{2,3},{3,2},{4,5},{5,4},{6,7},{7,6},{8,9},{9,8},{10,11... | collective-permute-start | bytes 1179656 | tf_op jit(solution)/shard_map/ppermute | solution.py:50
  97.8 5.6 %collective-permute-done.26 = bf16[4,48,1024]{2,1,0:T(8,128)(2,1)S(1)} collective-permute-done((bf16[4,48,1024]{2,1,0:T(8,128)(2,1)S(1)}, bf16[4,48,1024]{2,1,0:T(8,128)(2,1)S(1)}, u32[]{:S(2)}, u32[]{:S(2)}) %collective-permute-start.26) | collective-permute-done | bytes 393248 | tf_op jit(solution)/shard_map/ppermute | solution.py:45
  103.5 1.3 %unslot.2 = bf16[128,2048]{1,0:T(8,128)(2,1)} custom-call(bf16[128,192]{1,0:T(8,128)(2,1)S(1)} %copy-done.3, f32[128,128]{1,0:T(8,128)S(1)} %copy-done.4, bf16[96,1024]{1,0:T(8,128)(2,1)S(1)} %bitcast.95, bf16[96,1024]{1,0:T(8,128)(2,1)S(1)} %bitcast.98, bf16[2,96,1024]{2,1,0:T(8,128)(2,1)S(1)} %collective-permute-done.22.other), custom_call_target="tpu_custom_call" | custom-call | flops 4000000000 | bytes 12000000 | tf_op jit(solution)/shard_map/unslot/pallas_call | solution.py:409
  104.8 1.3 %collective-permute-start.27 = (bf16[2,96,1024]{2,1,0:T(8,128)(2,1)S(1)}, bf16[2,96,1024]{2,1,0:T(8,128)(2,1)S(1)}, u32[]{:S(2)}, u32[]{:S(2)}) collective-permute-start(bf16[2,96,1024]{2,1,0:T(8,128)(2,1)S(1)} %pad_maximum_fusion.7), channel_id=1, source_target_pairs={{0,1},{1,0},{2,3},{3,2},{4,5},{5,4},{6,7},{7,6},{8,9},{9,8},{10,11... | collective-permute-start | bytes 1179656 | tf_op jit(solution)/shard_map/ppermute | solution.py:50
  106.0 1.5 %fusion.2 = bf16[1,768,512]{2,1,0:T(8,128)(2,1)} fusion(bf16[768,512]{1,0:T(8,128)(2,1)S(1)} %collective-permute-done.29, bf16[384,768]{1,0:T(8,128)(2,1)S(1)} %get-tuple-element.70, bf16[384,1024]{1,0:T(8,128)(2,1)S(1)} %get-tuple-element.63.grad_rows), kind=kOutput, calls=%fused_computation.5 | convolution fusion | flops 303169536 | bytes 2555904 | tf_op jit(solution)/shard_map/dot_general | solution.py:23
  107.5 1.3 %unslot.3 = bf16[128,2048]{1,0:T(8,128)(2,1)} custom-call(bf16[128,192]{1,0:T(8,128)(2,1)S(1)} %copy-done.3, f32[128,128]{1,0:T(8,128)S(1)} %copy-done.4, bf16[96,1024]{1,0:T(8,128)(2,1)S(1)} %bitcast.96, bf16[96,1024]{1,0:T(8,128)(2,1)S(1)} %bitcast.97, bf16[2,96,1024]{2,1,0:T(8,128)(2,1)S(1)} %collective-permute-done.27.other), custom_call_target="tpu_custom_call" | custom-call | flops 4000000000 | bytes 12000000 | tf_op jit(solution)/shard_map/unslot/pallas_call | solution.py:409
  108.8 1.5 %fusion.4 = bf16[1,512,768]{2,1,0:T(8,128)(2,1)} fusion(bf16[2,512,768]{2,1,0:T(8,128)(2,1)S(1)} %collective-permute-done.28, bf16[2,384,768]{2,1,0:T(8,128)(2,1)S(1)} %get-tuple-element.82, bf16[384,1024]{1,0:T(8,128)(2,1)S(1)} %get-tuple-element.72.rows), kind=kOutput, calls=%fused_computation.7 | convolution fusion | flops 303169536 | bytes 2555904 | tf_op jit(solution)/shard_map/dot_general | solution.py:23
  110.3 1.5 %fusion.3 = bf16[1,512,768]{2,1,0:T(8,128)(2,1)} fusion(bf16[2,512,768]{2,1,0:T(8,128)(2,1)S(1)} %collective-permute-done.28, bf16[2,384,768]{2,1,0:T(8,128)(2,1)S(1)} %get-tuple-element.82, bf16[384,1024]{1,0:T(8,128)(2,1)S(1)} %get-tuple-element.72.rows), kind=kOutput, calls=%fused_computation.6 | convolution fusion | flops 303169536 | bytes 2555904 | tf_op jit(solution)/shard_map/dot_general | solution.py:23
  (66 shorter events, 1.8 us)
Async XLA Ops:
  3.0 8.5 %collective-permute-start.12 = (bf16[2,96,1024]{2,1,0:T(8,128)(2,1)}, bf16[2,96,1024]{2,1,0:T(8,128)(2,1)S(1)}, u32[]{:S(2)}, u32[]{:S(2)}) collective-permute-start(bf16[2,96,1024]{2,1,0:T(8,128)(2,1)} %get-tuple-element.57), channel_id=1, source_target_pairs={{0,1},{1,0},{2,3},{3,2},{4,5},{5,4},{6,7},{7,6},{8,9},{9,8},{10,11... | collective-permute-start | bytes 1179656 | tf_op jit(solution)/shard_map/ppermute | solution.py:50
  3.7 12.6 %collective-permute-start.9 = (bf16[1,512,768]{2,1,0:T(8,128)(2,1)}, bf16[1,512,768]{2,1,0:T(8,128)(2,1)S(1)}, u32[]{:S(2)}, u32[]{:S(2)}) collective-permute-start(bf16[1,512,768]{2,1,0:T(8,128)(2,1)} %up.1), channel_id=1, source_target_pairs={{0,8},{1,17},{2,10},{3,19},{4,12},{5,21},{6,14},{7,23},{8,0},{9,25... | collective-permute-start | bytes 2359304 | tf_op jit(solution)/shard_map/ppermute | solution.py:41
  7.3 2.6 %collective-permute-start = (bf16[2,96,1024]{2,1,0:T(8,128)(2,1)}, bf16[2,96,1024]{2,1,0:T(8,128)(2,1)S(1)}, u32[]{:S(2)}, u32[]{:S(2)}) collective-permute-start(bf16[2,96,1024]{2,1,0:T(8,128)(2,1)} %get-tuple-element.49), channel_id=1, source_target_pairs={{0,1},{1,0},{2,3},{3,2},{4,5},{5,4},{6,7},{7,6},{8,9},{9,8},{10,11... | collective-permute-start | bytes 1179656 | tf_op jit(solution)/shard_map/ppermute | solution.py:50
  7.3 22.2 %collective-permute-start.8 = (bf16[1,512,768]{2,1,0:T(8,128)(2,1)}, bf16[1,512,768]{2,1,0:T(8,128)(2,1)S(1)}, u32[]{:S(2)}, u32[]{:S(2)}) collective-permute-start(bf16[1,512,768]{2,1,0:T(8,128)(2,1)} %gate.1), channel_id=1, source_target_pairs={{0,8},{1,17},{2,10},{3,19},{4,12},{5,21},{6,14},{7,23},{8,0},{9,25... | collective-permute-start | bytes 2359304 | tf_op jit(solution)/shard_map/ppermute | solution.py:41
  10.0 11.3 %collective-permute-start.4 = (bf16[2,96,1024]{2,1,0:T(8,128)(2,1)S(1)}, bf16[2,96,1024]{2,1,0:T(8,128)(2,1)S(1)}, u32[]{:S(2)}, u32[]{:S(2)}) collective-permute-start(bf16[2,96,1024]{2,1,0:T(8,128)(2,1)S(1)} %pad_maximum_fusion), channel_id=1, source_target_pairs={{0,16},{1,9},{2,18},{3,11},{4,20},{5,13},{6,22},{7,15},{8,24},{9,1... | collective-permute-start | bytes 1179656 | tf_op jit(solution)/shard_map/ppermute | solution.py:45
  11.3 11.2 %collective-permute-start.3 = (bf16[1,48,1024]{2,1,0:T(8,128)(2,1)S(1)}, bf16[1,48,1024]{2,1,0:T(8,128)(2,1)S(1)}, u32[]{:S(2)}, u32[]{:S(2)}) collective-permute-start(bf16[1,48,1024]{2,1,0:T(8,128)(2,1)S(1)} %bitcast.125), channel_id=1, source_target_pairs={{0,6},{1,7},{2,4},{3,5},{4,2},{5,3},{6,0},{7,1},{8,14},{9,15},{10,... | collective-permute-start | bytes 294920 | tf_op jit(solution)/shard_map/ppermute | solution.py:50
  11.5 11.2 %collective-permute-start.2 = (bf16[1,48,1024]{2,1,0:T(8,128)(2,1)S(1)}, bf16[1,48,1024]{2,1,0:T(8,128)(2,1)S(1)}, u32[]{:S(2)}, u32[]{:S(2)}) collective-permute-start(bf16[1,48,1024]{2,1,0:T(8,128)(2,1)S(1)} %bitcast.124), channel_id=1, source_target_pairs={{0,4},{1,5},{2,6},{3,7},{4,0},{5,1},{6,2},{7,3},{8,12},{9,13},{10,... | collective-permute-start | bytes 294920 | tf_op jit(solution)/shard_map/ppermute | solution.py:50
  14.8 14.7 %copy-start.2 = (bf16[1,768,512]{2,1,0:T(8,128)(2,1)S(1)}, bf16[1,768,512]{2,1,0:T(8,128)(2,1)}, u32[]{:S(2)}) copy-start(bf16[1,768,512]{2,1,0:T(8,128)(2,1)} %down.1) | copy-start | bytes 2359300
  14.8 16.2 %copy-start = (bf16[1,512,768]{2,1,0:T(8,128)(2,1)S(1)}, bf16[1,512,768]{2,1,0:T(8,128)(2,1)}, u32[]{:S(2)}) copy-start(bf16[1,512,768]{2,1,0:T(8,128)(2,1)} %gate.1) | copy-start | bytes 2359300
  14.8 16.2 %copy-start.1 = (bf16[1,512,768]{2,1,0:T(8,128)(2,1)S(1)}, bf16[1,512,768]{2,1,0:T(8,128)(2,1)}, u32[]{:S(2)}) copy-start(bf16[1,512,768]{2,1,0:T(8,128)(2,1)} %up.1) | copy-start | bytes 2359300
  16.2 9.8 %collective-permute-start.1 = (bf16[1,48,1024]{2,1,0:T(8,128)(2,1)S(1)}, bf16[1,48,1024]{2,1,0:T(8,128)(2,1)S(1)}, u32[]{:S(2)}, u32[]{:S(2)}) collective-permute-start(bf16[1,48,1024]{2,1,0:T(8,128)(2,1)S(1)} %bitcast.123), channel_id=1, source_target_pairs={{0,2},{1,3},{2,0},{3,1},{4,6},{5,7},{6,4},{7,5},{8,10},{9,11},{10,... | collective-permute-start | bytes 294920 | tf_op jit(solution)/shard_map/ppermute | solution.py:50
  21.3 12.3 %collective-permute-start.13 = (bf16[2,96,1024]{2,1,0:T(8,128)(2,1)S(1)}, bf16[2,96,1024]{2,1,0:T(8,128)(2,1)S(1)}, u32[]{:S(2)}, u32[]{:S(2)}) collective-permute-start(bf16[2,96,1024]{2,1,0:T(8,128)(2,1)S(1)} %pad_maximum_fusion.1), channel_id=1, source_target_pairs={{0,16},{1,9},{2,18},{3,11},{4,20},{5,13},{6,22},{7,15},{8,24},{9,1... | collective-permute-start | bytes 1179656 | tf_op jit(solution)/shard_map/ppermute | solution.py:45
  22.6 8.4 %collective-permute-start.7 = (bf16[1,48,1024]{2,1,0:T(8,128)(2,1)S(1)}, bf16[1,48,1024]{2,1,0:T(8,128)(2,1)S(1)}, u32[]{:S(2)}, u32[]{:S(2)}) collective-permute-start(bf16[1,48,1024]{2,1,0:T(8,128)(2,1)S(1)} %bitcast.128), channel_id=1, source_target_pairs={{0,6},{1,7},{2,4},{3,5},{4,2},{5,3},{6,0},{7,1},{8,14},{9,15},{10,... | collective-permute-start | bytes 294920 | tf_op jit(solution)/shard_map/ppermute | solution.py:50
  22.8 8.2 %collective-permute-start.6 = (bf16[1,48,1024]{2,1,0:T(8,128)(2,1)S(1)}, bf16[1,48,1024]{2,1,0:T(8,128)(2,1)S(1)}, u32[]{:S(2)}, u32[]{:S(2)}) collective-permute-start(bf16[1,48,1024]{2,1,0:T(8,128)(2,1)S(1)} %bitcast.127), channel_id=1, source_target_pairs={{0,4},{1,5},{2,6},{3,7},{4,0},{5,1},{6,2},{7,3},{8,12},{9,13},{10,... | collective-permute-start | bytes 294920 | tf_op jit(solution)/shard_map/ppermute | solution.py:50
  26.0 5.0 %collective-permute-start.5 = (bf16[1,48,1024]{2,1,0:T(8,128)(2,1)S(1)}, bf16[1,48,1024]{2,1,0:T(8,128)(2,1)S(1)}, u32[]{:S(2)}, u32[]{:S(2)}) collective-permute-start(bf16[1,48,1024]{2,1,0:T(8,128)(2,1)S(1)} %bitcast.126), channel_id=1, source_target_pairs={{0,2},{1,3},{2,0},{3,1},{4,6},{5,7},{6,4},{7,5},{8,10},{9,11},{10,... | collective-permute-start | bytes 294920 | tf_op jit(solution)/shard_map/ppermute | solution.py:50
  29.5 20.4 %collective-permute-start.11 = (bf16[1,768,512]{2,1,0:T(8,128)(2,1)S(1)}, bf16[1,768,512]{2,1,0:T(8,128)(2,1)S(1)}, u32[]{:S(2)}, u32[]{:S(2)}) collective-permute-start(bf16[1,768,512]{2,1,0:T(8,128)(2,1)S(1)} %copy-done.2), channel_id=1, source_target_pairs={{0,8},{1,17},{2,10},{3,19},{4,12},{5,21},{6,14},{7,23},{8,0},{9,25... | collective-permute-start | bytes 2359304 | tf_op jit(solution)/shard_map/ppermute | solution.py:41
  33.4 23.2 %collective-permute-start.10 = (bf16[2,384,768]{2,1,0:T(8,128)(2,1)S(1)}, bf16[2,384,768]{2,1,0:T(8,128)(2,1)S(1)}, u32[]{:S(2)}, u32[]{:S(2)}) collective-permute-start(bf16[2,384,768]{2,1,0:T(8,128)(2,1)S(1)} %get-tuple-element.54), channel_id=1, source_target_pairs={{0,16},{1,9},{2,18},{3,11},{4,20},{5,13},{6,22},{7,15},{8,24},{9,1... | collective-permute-start | bytes 3538952 | tf_op jit(solution)/shard_map/ppermute | solution.py:45
  33.6 9.5 %collective-permute-start.16 = (bf16[2,48,1024]{2,1,0:T(8,128)(2,1)S(1)}, bf16[2,48,1024]{2,1,0:T(8,128)(2,1)S(1)}, u32[]{:S(2)}, u32[]{:S(2)}) collective-permute-start(bf16[2,48,1024]{2,1,0:T(8,128)(2,1)S(1)} %pad_maximum_fusion.11), channel_id=1, source_target_pairs={{0,6},{1,7},{2,4},{3,5},{4,2},{5,3},{6,0},{7,1},{8,14},{9,15},{10,... | collective-permute-start | bytes 589832 | tf_op jit(solution)/shard_map/ppermute | solution.py:50
  34.6 15.0 %collective-permute-start.15 = (bf16[2,48,1024]{2,1,0:T(8,128)(2,1)S(1)}, bf16[2,48,1024]{2,1,0:T(8,128)(2,1)S(1)}, u32[]{:S(2)}, u32[]{:S(2)}) collective-permute-start(bf16[2,48,1024]{2,1,0:T(8,128)(2,1)S(1)} %pad_maximum_fusion.10), channel_id=1, source_target_pairs={{0,4},{1,5},{2,6},{3,7},{4,0},{5,1},{6,2},{7,3},{8,12},{9,13},{10,... | collective-permute-start | bytes 589832 | tf_op jit(solution)/shard_map/ppermute | solution.py:50
  37.1 12.8 %collective-permute-start.14 = (bf16[2,48,1024]{2,1,0:T(8,128)(2,1)S(1)}, bf16[2,48,1024]{2,1,0:T(8,128)(2,1)S(1)}, u32[]{:S(2)}, u32[]{:S(2)}) collective-permute-start(bf16[2,48,1024]{2,1,0:T(8,128)(2,1)S(1)} %pad_maximum_fusion.9), channel_id=1, source_target_pairs={{0,2},{1,3},{2,0},{3,1},{4,6},{5,7},{6,4},{7,5},{8,10},{9,11},{10,... | collective-permute-start | bytes 589832 | tf_op jit(solution)/shard_map/ppermute | solution.py:50
  51.3 11.9 %collective-permute-start.20 = (bf16[384,768]{1,0:T(8,128)(2,1)S(1)}, bf16[384,768]{1,0:T(8,128)(2,1)S(1)}, u32[]{:S(2)}, u32[]{:S(2)}) collective-permute-start(bf16[384,768]{1,0:T(8,128)(2,1)S(1)} %get-tuple-element.69), channel_id=1, source_target_pairs={{0,16},{1,9},{2,18},{3,11},{4,20},{5,13},{6,22},{7,15},{8,24},{9,1... | collective-permute-start | bytes 1769480 | tf_op jit(solution)/shard_map/ppermute | solution.py:45
  58.9 9.3 %collective-permute-start.18 = (bf16[2,48,1024]{2,1,0:T(8,128)(2,1)S(1)}, bf16[2,48,1024]{2,1,0:T(8,128)(2,1)S(1)}, u32[]{:S(2)}, u32[]{:S(2)}) collective-permute-start(bf16[2,48,1024]{2,1,0:T(8,128)(2,1)S(1)} %get-tuple-element.66), channel_id=1, source_target_pairs={{0,4},{1,5},{2,6},{3,7},{4,0},{5,1},{6,2},{7,3},{8,12},{9,13},{10,... | collective-permute-start | bytes 589832 | tf_op jit(solution)/shard_map/ppermute | solution.py:50
  59.1 11.0 %collective-permute-start.17 = (bf16[2,48,1024]{2,1,0:T(8,128)(2,1)S(1)}, bf16[2,48,1024]{2,1,0:T(8,128)(2,1)S(1)}, u32[]{:S(2)}, u32[]{:S(2)}) collective-permute-start(bf16[2,48,1024]{2,1,0:T(8,128)(2,1)S(1)} %get-tuple-element.65), channel_id=1, source_target_pairs={{0,2},{1,3},{2,0},{3,1},{4,6},{5,7},{6,4},{7,5},{8,10},{9,11},{10,... | collective-permute-start | bytes 589832 | tf_op jit(solution)/shard_map/ppermute | solution.py:50
  60.4 22.0 %collective-permute-start.19 = (bf16[2,48,1024]{2,1,0:T(8,128)(2,1)S(1)}, bf16[2,48,1024]{2,1,0:T(8,128)(2,1)S(1)}, u32[]{:S(2)}, u32[]{:S(2)}) collective-permute-start(bf16[2,48,1024]{2,1,0:T(8,128)(2,1)S(1)} %get-tuple-element.67), channel_id=1, source_target_pairs={{0,6},{1,7},{2,4},{3,5},{4,2},{5,3},{6,0},{7,1},{8,14},{9,15},{10,... | collective-permute-start | bytes 589832 | tf_op jit(solution)/shard_map/ppermute | solution.py:50
  63.2 42.9 %collective-permute-start.29 = (bf16[768,512]{1,0:T(8,128)(2,1)S(1)}, bf16[768,512]{1,0:T(8,128)(2,1)S(1)}, u32[]{:S(2)}, u32[]{:S(2)}) collective-permute-start(bf16[768,512]{1,0:T(8,128)(2,1)S(1)} %get-tuple-element.86), channel_id=1, source_target_pairs={{0,8},{1,17},{2,10},{3,19},{4,12},{5,21},{6,14},{7,23},{8,0},{9,25... | collective-permute-start | bytes 2359304 | tf_op jit(solution)/shard_map/ppermute | solution.py:41
  68.2 40.5 %collective-permute-start.28 = (bf16[2,512,768]{2,1,0:T(8,128)(2,1)S(1)}, bf16[2,512,768]{2,1,0:T(8,128)(2,1)S(1)}, u32[]{:S(2)}, u32[]{:S(2)}) collective-permute-start(bf16[2,512,768]{2,1,0:T(8,128)(2,1)S(1)} %get-tuple-element.84), channel_id=1, source_target_pairs={{0,8},{1,17},{2,10},{3,19},{4,12},{5,21},{6,14},{7,23},{8,0},{9,25... | collective-permute-start | bytes 4718600 | tf_op jit(solution)/shard_map/ppermute | solution.py:41
  70.1 12.6 %collective-permute-start.23 = (bf16[2,48,1024]{2,1,0:T(8,128)(2,1)S(1)}, bf16[2,48,1024]{2,1,0:T(8,128)(2,1)S(1)}, u32[]{:S(2)}, u32[]{:S(2)}) collective-permute-start(bf16[2,48,1024]{2,1,0:T(8,128)(2,1)S(1)} %get-tuple-element.76), channel_id=1, source_target_pairs={{0,2},{1,3},{2,0},{3,1},{4,6},{5,7},{6,4},{7,5},{8,10},{9,11},{10,... | collective-permute-start | bytes 589832 | tf_op jit(solution)/shard_map/ppermute | solution.py:50
  72.6 15.3 %collective-permute-start.24 = (bf16[2,48,1024]{2,1,0:T(8,128)(2,1)S(1)}, bf16[2,48,1024]{2,1,0:T(8,128)(2,1)S(1)}, u32[]{:S(2)}, u32[]{:S(2)}) collective-permute-start(bf16[2,48,1024]{2,1,0:T(8,128)(2,1)S(1)} %get-tuple-element.78), channel_id=1, source_target_pairs={{0,4},{1,5},{2,6},{3,7},{4,0},{5,1},{6,2},{7,3},{8,12},{9,13},{10,... | collective-permute-start | bytes 589832 | tf_op jit(solution)/shard_map/ppermute | solution.py:50
  82.5 13.9 %collective-permute-start.25 = (bf16[2,48,1024]{2,1,0:T(8,128)(2,1)S(1)}, bf16[2,48,1024]{2,1,0:T(8,128)(2,1)S(1)}, u32[]{:S(2)}, u32[]{:S(2)}) collective-permute-start(bf16[2,48,1024]{2,1,0:T(8,128)(2,1)S(1)} %get-tuple-element.80), channel_id=1, source_target_pairs={{0,6},{1,7},{2,4},{3,5},{4,2},{5,3},{6,0},{7,1},{8,14},{9,15},{10,... | collective-permute-start | bytes 589832 | tf_op jit(solution)/shard_map/ppermute | solution.py:50
  82.7 13.9 %collective-permute-start.21 = (bf16[4,48,1024]{2,1,0:T(8,128)(2,1)S(1)}, bf16[4,48,1024]{2,1,0:T(8,128)(2,1)S(1)}, u32[]{:S(2)}, u32[]{:S(2)}) collective-permute-start(bf16[4,48,1024]{2,1,0:T(8,128)(2,1)S(1)} %get-tuple-element.74), channel_id=1, source_target_pairs={{0,16},{1,9},{2,18},{3,11},{4,20},{5,13},{6,22},{7,15},{8,24},{9,1... | collective-permute-start | bytes 1179656 | tf_op jit(solution)/shard_map/ppermute | solution.py:45
  96.4 7.0 %collective-permute-start.26 = (bf16[4,48,1024]{2,1,0:T(8,128)(2,1)S(1)}, bf16[4,48,1024]{2,1,0:T(8,128)(2,1)S(1)}, u32[]{:S(2)}, u32[]{:S(2)}) collective-permute-start(bf16[4,48,1024]{2,1,0:T(8,128)(2,1)S(1)} %pad_maximum_fusion.6), channel_id=1, source_target_pairs={{0,16},{1,9},{2,18},{3,11},{4,20},{5,13},{6,22},{7,15},{8,24},{9,1... | collective-permute-start | bytes 1179656 | tf_op jit(solution)/shard_map/ppermute | solution.py:45
  96.6 6.9 %copy-start.3 = (bf16[128,192]{1,0:T(8,128)(2,1)S(1)}, bf16[128,192]{1,0:T(8,128)(2,1)}, u32[]{:S(2)}) copy-start(bf16[128,192]{1,0:T(8,128)(2,1)} %get-tuple-element.46.pick) | copy-start | bytes 147460
  96.6 6.9 %copy-start.4 = (f32[128,128]{1,0:T(8,128)S(1)}, f32[128,128]{1,0:T(8,128)}, u32[]{:S(2)}) copy-start(f32[128,128]{1,0:T(8,128)} %get-tuple-element.47.weight) | copy-start | bytes 196612
  96.6 6.8 %collective-permute-start.22 = (bf16[2,96,1024]{2,1,0:T(8,128)(2,1)S(1)}, bf16[2,96,1024]{2,1,0:T(8,128)(2,1)S(1)}, u32[]{:S(2)}, u32[]{:S(2)}) collective-permute-start(bf16[2,96,1024]{2,1,0:T(8,128)(2,1)S(1)} %pad_maximum_fusion.4), channel_id=1, source_target_pairs={{0,1},{1,0},{2,3},{3,2},{4,5},{5,4},{6,7},{7,6},{8,9},{9,8},{10,11... | collective-permute-start | bytes 1179656 | tf_op jit(solution)/shard_map/ppermute | solution.py:50
  104.8 2.7 %collective-permute-start.27 = (bf16[2,96,1024]{2,1,0:T(8,128)(2,1)S(1)}, bf16[2,96,1024]{2,1,0:T(8,128)(2,1)S(1)}, u32[]{:S(2)}, u32[]{:S(2)}) collective-permute-start(bf16[2,96,1024]{2,1,0:T(8,128)(2,1)S(1)} %pad_maximum_fusion.7), channel_id=1, source_target_pairs={{0,1},{1,0},{2,3},{3,2},{4,5},{5,4},{6,7},{7,6},{8,9},{9,8},{10,11... | collective-permute-start | bytes 1179656 | tf_op jit(solution)/shard_map/ppermute | solution.py:50

commit v6 on v5

--- a/solution.py
+++ b/solution.py
@@ -473,7 +473,7 @@
         slots, others, chips, capacity, True, (), (), ()
     )
     far_up = swap_weight(w_up)
-    far_down = swap_weight(after(w_down, *(far,)))
+    far_down = swap_weight(after(w_down, *(far_up,)))
     grad_far, got_grad_parts = send_slots(
         grad_slots, grad_others, chips, capacity, False, (far_up,), got_parts, got_parts
     )

time: 112 us -> 112 us (level)
  no operation moved by 1% of the time
where the time goes in v6:
time: 112 us
  waiting for transfers between devices  53.7 us (48%)
  starting transfers between devices  31.6 us (28%)
  Pallas kernels  18 us (16%)
  matrix products  4.44 us (4%)
  local copies, waits for them, and re-layouts  2.46 us (2%)
    ppermute x19, waiting for transfers between devices, swap_expert(): lax.ppermute(value, 'expert', [(i, i ^ mask) for i in range(experts)])  34.3 us
    ppermute x19, starting transfers between devices, swap_expert(): lax.ppermute(value, 'expert', [(i, i ^ mask) for i in range(experts)])  21.5 us
    ppermute x6, waiting for transfers between devices, swap_rows(): return lax.ppermute(value, BOTH, pair_list(lax.axis_size('expert'), (2, 1)))  14.6 us
    ppermute x6, starting transfers between devices, swap_rows(): return lax.ppermute(value, BOTH, pair_list(lax.axis_size('expert'), (2, 1)))  5.08 us
    ppermute x5, starting transfers between devices, swap_weight(): return lax.ppermute(value, BOTH, pair_list(lax.axis_size('expert'), (1, 2)))  4.99 us
    ppermute x5, waiting for transfers between devices, swap_weight(): return lax.ppermute(value, BOTH, pair_list(lax.axis_size('expert'), (1, 2)))  4.8 us
    pallas_call x1, Pallas kernels, slot_grad_parts(): pl.pallas_call(functools.partial(slot_grad_kernel, places), grid=(hidden...  4.63 us
    dot_general x3, matrix products, contract_first(): lax.dot_general(left_side, right_side, (((0,), (0,)), ((), ())), preferre...  4.44 us
  transfers between devices with their start and end apart: 30, of which 13 were waited for; matrix products, arithmetic and copies ran while one was open for 4% of the time, Pallas kernels for 14%

profile of v6, /device:TPU:19, one launch (start us, length us, event | category | flops | bytes accessed | tf_op | source)
XLA Modules:
  0.0 111.7 jit_solution(645547771358432563)
XLA Ops:
  0.6 2.4 %make_grads.1 = (bf16[2,96,1024]{2,1,0:T(8,128)(2,1)}, bf16[2,96,1024]{2,1,0:T(8,128)(2,1)}, bf16[128,192]{1,0:T(8,128)(2,1)}, f32[128,128]{1,0:T(8,128)}) custom-call(bf16[128,2048]{1,0:T(8,128)(2,1)} %cot.1, s32[1,128]{1,0:T(1,128)} %bitcast.129, s32[1,128]{1,0:T(1,128)} %bitcast.131), custom_call_target="tpu_custom_call" | custom-call | flops 10000000 | bytes 30000 | tf_op jit(solution)/shard_map/make_grads/pallas_call | solution.py:141
  3.0 0.7 collective-permute-start.12
  3.7 1.2 %collective-permute-start.9 = (bf16[1,512,768]{2,1,0:T(8,128)(2,1)}, bf16[1,512,768]{2,1,0:T(8,128)(2,1)S(1)}, u32[]{:S(2)}, u32[]{:S(2)}) collective-permute-start(bf16[1,512,768]{2,1,0:T(8,128)(2,1)} %up.1), channel_id=1, source_target_pairs={{0,8},{1,17},{2,10},{3,19},{4,12},{5,21},{6,14},{7,23},{8,0},{9,25... | collective-permute-start | bytes 2359304 | tf_op jit(solution)/shard_map/ppermute | solution.py:41
  4.9 2.3 %make_slots.1 = (bf16[2,96,1024]{2,1,0:T(8,128)(2,1)}, bf16[2,96,1024]{2,1,0:T(8,128)(2,1)}) custom-call(bf16[128,2048]{1,0:T(8,128)(2,1)} %tok.1, s32[1,128]{1,0:T(1,128)} %bitcast.130, s32[1,128]{1,0:T(1,128)} %bitcast.132), custom_call_target="tpu_custom_call" | custom-call | flops 10000000 | bytes 30000 | tf_op jit(solution)/shard_map/make_slots/pallas_call | solution.py:129
  7.3 0.5 collective-permute-start.8
  7.8 1.0 fusion.29
  8.9 1.1 fusion.32
  10.0 1.3 %collective-permute-start.4 = (bf16[2,96,1024]{2,1,0:T(8,128)(2,1)S(1)}, bf16[2,96,1024]{2,1,0:T(8,128)(2,1)S(1)}, u32[]{:S(2)}, u32[]{:S(2)}) collective-permute-start(bf16[2,96,1024]{2,1,0:T(8,128)(2,1)S(1)} %pad_maximum_fusion), channel_id=1, source_target_pairs={{0,16},{1,9},{2,18},{3,11},{4,20},{5,13},{6,22},{7,15},{8,24},{9,1... | collective-permute-start | bytes 1179656 | tf_op jit(solution)/shard_map/ppermute | solution.py:45
  11.5 3.2 %collective-permute-start.2 = (bf16[1,48,1024]{2,1,0:T(8,128)(2,1)S(1)}, bf16[1,48,1024]{2,1,0:T(8,128)(2,1)S(1)}, u32[]{:S(2)}, u32[]{:S(2)}) collective-permute-start(bf16[1,48,1024]{2,1,0:T(8,128)(2,1)S(1)} %bitcast.124), channel_id=1, source_target_pairs={{0,4},{1,5},{2,6},{3,7},{4,0},{5,1},{6,2},{7,3},{8,12},{9,13},{10,... | collective-permute-start | bytes 294920 | tf_op jit(solution)/shard_map/ppermute | solution.py:50
  14.9 1.4 %collective-permute-done.9.refs_11_.far_up = bf16[1,512,768]{2,1,0:T(8,128)(2,1)S(1)} collective-permute-done((bf16[1,512,768]{2,1,0:T(8,128)(2,1)}, bf16[1,512,768]{2,1,0:T(8,128)(2,1)S(1)}, u32[]{:S(2)}, u32[]{:S(2)}) %collective-permute-start.9) | collective-permute-done | bytes 786464 | tf_op jit(solution)/shard_map/ppermute | solution.py:41
  16.2 1.3 %collective-permute-start.1 = (bf16[1,48,1024]{2,1,0:T(8,128)(2,1)S(1)}, bf16[1,48,1024]{2,1,0:T(8,128)(2,1)S(1)}, u32[]{:S(2)}, u32[]{:S(2)}) collective-permute-start(bf16[1,48,1024]{2,1,0:T(8,128)(2,1)S(1)} %bitcast.123), channel_id=1, source_target_pairs={{0,2},{1,3},{2,0},{3,1},{4,6},{5,7},{6,4},{7,5},{8,10},{9,11},{10,... | collective-permute-start | bytes 294920 | tf_op jit(solution)/shard_map/ppermute | solution.py:50
  17.6 3.7 %collective-permute-done.4 = bf16[2,96,1024]{2,1,0:T(8,128)(2,1)S(1)} collective-permute-done((bf16[2,96,1024]{2,1,0:T(8,128)(2,1)S(1)}, bf16[2,96,1024]{2,1,0:T(8,128)(2,1)S(1)}, u32[]{:S(2)}, u32[]{:S(2)}) %collective-permute-start.4) | collective-permute-done | bytes 393248 | tf_op jit(solution)/shard_map/ppermute | solution.py:45
  21.3 1.2 %collective-permute-start.13 = (bf16[2,96,1024]{2,1,0:T(8,128)(2,1)S(1)}, bf16[2,96,1024]{2,1,0:T(8,128)(2,1)S(1)}, u32[]{:S(2)}, u32[]{:S(2)}) collective-permute-start(bf16[2,96,1024]{2,1,0:T(8,128)(2,1)S(1)} %pad_maximum_fusion.1), channel_id=1, source_target_pairs={{0,16},{1,9},{2,18},{3,11},{4,20},{5,13},{6,22},{7,15},{8,24},{9,1... | collective-permute-start | bytes 1179656 | tf_op jit(solution)/shard_map/ppermute | solution.py:45
  22.8 3.2 %collective-permute-start.6 = (bf16[1,48,1024]{2,1,0:T(8,128)(2,1)S(1)}, bf16[1,48,1024]{2,1,0:T(8,128)(2,1)S(1)}, u32[]{:S(2)}, u32[]{:S(2)}) collective-permute-start(bf16[1,48,1024]{2,1,0:T(8,128)(2,1)S(1)} %bitcast.127), channel_id=1, source_target_pairs={{0,4},{1,5},{2,6},{3,7},{4,0},{5,1},{6,2},{7,3},{8,12},{9,13},{10,... | collective-permute-start | bytes 294920 | tf_op jit(solution)/shard_map/ppermute | solution.py:50
  26.0 3.4 %collective-permute-done.8.refs_10_.far_gate = bf16[1,512,768]{2,1,0:T(8,128)(2,1)S(1)} collective-permute-done((bf16[1,512,768]{2,1,0:T(8,128)(2,1)}, bf16[1,512,768]{2,1,0:T(8,128)(2,1)S(1)}, u32[]{:S(2)}, u32[]{:S(2)}) %collective-permute-start.8) | collective-permute-done | bytes 786464 | tf_op jit(solution)/shard_map/ppermute | solution.py:41
  29.5 1.5 %collective-permute-start.11 = (bf16[1,768,512]{2,1,0:T(8,128)(2,1)S(1)}, bf16[1,768,512]{2,1,0:T(8,128)(2,1)S(1)}, u32[]{:S(2)}, u32[]{:S(2)}) collective-permute-start(bf16[1,768,512]{2,1,0:T(8,128)(2,1)S(1)} %copy-done.2), channel_id=1, source_target_pairs={{0,8},{1,17},{2,10},{3,19},{4,12},{5,21},{6,14},{7,23},{8,0},{9,25... | collective-permute-start | bytes 2359304 | tf_op jit(solution)/shard_map/ppermute | solution.py:41
  31.0 2.4 %gate_up_parts.1 = (bf16[384,1024]{1,0:T(8,128)(2,1)S(1)}, f32[2,384,768]{2,1,0:T(8,128)S(1)}, bf16[2,384,768]{2,1,0:T(8,128)(2,1)S(1)}) custom-call(bf16[1,48,1024]{2,1,0:T(8,128)(2,1)S(1)} %bitcast.93, bf16[1,48,1024]{2,1,0:T(8,128)(2,1)S(1)} %collective-permute-done.1.refs_1_, bf16[1,48,1024]{2,1,0:T(8,128)(2,1)S(1)} %collective-permute-done.2.refs_2_, ...), custom_call_target="tpu_custom_call" | custom-call | flops 10000000 | bytes 30000 | tf_op jit(solution)/shard_map/gate_up_parts/pallas_call | solution.py:203
  33.6 1.0 collective-permute-start.16
  34.6 2.5 %collective-permute-start.15 = (bf16[2,48,1024]{2,1,0:T(8,128)(2,1)S(1)}, bf16[2,48,1024]{2,1,0:T(8,128)(2,1)S(1)}, u32[]{:S(2)}, u32[]{:S(2)}) collective-permute-start(bf16[2,48,1024]{2,1,0:T(8,128)(2,1)S(1)} %pad_maximum_fusion.10), channel_id=1, source_target_pairs={{0,4},{1,5},{2,6},{3,7},{4,0},{5,1},{6,2},{7,3},{8,12},{9,13},{10,... | collective-permute-start | bytes 589832 | tf_op jit(solution)/shard_map/ppermute | solution.py:50
  37.1 1.0 collective-permute-start.14
  38.2 4.9 %collective-permute-done.16.refs_3_ = bf16[2,48,1024]{2,1,0:T(8,128)(2,1)S(1)} collective-permute-done((bf16[2,48,1024]{2,1,0:T(8,128)(2,1)S(1)}, bf16[2,48,1024]{2,1,0:T(8,128)(2,1)S(1)}, u32[]{:S(2)}, u32[]{:S(2)}) %collective-permute-start.16) | collective-permute-done | bytes 196640 | tf_op jit(solution)/shard_map/ppermute | solution.py:50
  43.1 6.5 %collective-permute-done.15.refs_2_ = bf16[2,48,1024]{2,1,0:T(8,128)(2,1)S(1)} collective-permute-done((bf16[2,48,1024]{2,1,0:T(8,128)(2,1)S(1)}, bf16[2,48,1024]{2,1,0:T(8,128)(2,1)S(1)}, u32[]{:S(2)}, u32[]{:S(2)}) %collective-permute-start.15) | collective-permute-done | bytes 196640 | tf_op jit(solution)/shard_map/ppermute | solution.py:50
  49.6 0.3 collective-permute-done.14.refs_1_
  49.9 1.4 %grad_hidden_parts.1 = (bf16[384,1024]{1,0:T(8,128)(2,1)S(1)}, f32[384,768]{1,0:T(8,128)S(1)}, bf16[384,768]{1,0:T(8,128)(2,1)S(1)}) custom-call(bf16[2,48,1024]{2,1,0:T(8,128)(2,1)S(1)} %pad_maximum_fusion.8.refs_0_, bf16[2,48,1024]{2,1,0:T(8,128)(2,1)S(1)} %collective-permute-done.14.refs_1_, bf16[2,48,1024]{2,1,0:T(8,128)(2,1)S(1)} %collective-permute-done.15.refs_2_, ...), custom_call_target="tpu_custom_call" | custom-call | flops 1000000000 | bytes 3000000 | tf_op jit(solution)/shard_map/grad_hidden_parts/pallas_call | solution.py:244
  51.3 1.4 %collective-permute-start.20 = (bf16[384,768]{1,0:T(8,128)(2,1)S(1)}, bf16[384,768]{1,0:T(8,128)(2,1)S(1)}, u32[]{:S(2)}, u32[]{:S(2)}) collective-permute-start(bf16[384,768]{1,0:T(8,128)(2,1)S(1)} %get-tuple-element.69), channel_id=1, source_target_pairs={{0,16},{1,9},{2,18},{3,11},{4,20},{5,13},{6,22},{7,15},{8,24},{9,1... | collective-permute-start | bytes 1769480 | tf_op jit(solution)/shard_map/ppermute | solution.py:45
  52.7 3.8 %collective-permute-done.10.got = bf16[2,384,768]{2,1,0:T(8,128)(2,1)S(1)} collective-permute-done((bf16[2,384,768]{2,1,0:T(8,128)(2,1)S(1)}, bf16[2,384,768]{2,1,0:T(8,128)(2,1)S(1)}, u32[]{:S(2)}, u32[]{:S(2)}) %collective-permute-start.10) | collective-permute-done | bytes 1179680 | tf_op jit(solution)/shard_map/ppermute | solution.py:45
  56.5 2.4 %slot_out.1 = (bf16[384,768]{1,0:T(8,128)(2,1)S(1)}, bf16[768,512]{1,0:T(8,128)(2,1)S(1)}, bf16[2,48,1024]{2,1,0:T(8,128)(2,1)S(1)}, bf16[2,48,1024]{2,1,0:T(8,1...) custom-call(f32[2,384,768]{2,1,0:T(8,128)S(1)} %get-tuple-element.53.own, ...), custom_call_target="tpu_custom_call" | custom-call | flops 10000000 | bytes 30000 | tf_op jit(solution)/shard_map/slot_out/pallas_call | solution.py:292
  59.1 1.4 %collective-permute-start.17 = (bf16[2,48,1024]{2,1,0:T(8,128)(2,1)S(1)}, bf16[2,48,1024]{2,1,0:T(8,128)(2,1)S(1)}, u32[]{:S(2)}, u32[]{:S(2)}) collective-permute-start(bf16[2,48,1024]{2,1,0:T(8,128)(2,1)S(1)} %get-tuple-element.65), channel_id=1, source_target_pairs={{0,2},{1,3},{2,0},{3,1},{4,6},{5,7},{6,4},{7,5},{8,10},{9,11},{10,... | collective-permute-start | bytes 589832 | tf_op jit(solution)/shard_map/ppermute | solution.py:50
  60.4 1.2 %collective-permute-start.19 = (bf16[2,48,1024]{2,1,0:T(8,128)(2,1)S(1)}, bf16[2,48,1024]{2,1,0:T(8,128)(2,1)S(1)}, u32[]{:S(2)}, u32[]{:S(2)}) collective-permute-start(bf16[2,48,1024]{2,1,0:T(8,128)(2,1)S(1)} %get-tuple-element.67), channel_id=1, source_target_pairs={{0,6},{1,7},{2,4},{3,5},{4,2},{5,3},{6,0},{7,1},{8,14},{9,15},{10,... | collective-permute-start | bytes 589832 | tf_op jit(solution)/shard_map/ppermute | solution.py:50
  61.7 1.5 %collective-permute-done.20.got_grad = bf16[384,768]{1,0:T(8,128)(2,1)S(1)} collective-permute-done((bf16[384,768]{1,0:T(8,128)(2,1)S(1)}, bf16[384,768]{1,0:T(8,128)(2,1)S(1)}, u32[]{:S(2)}, u32[]{:S(2)}) %collective-permute-start.20) | collective-permute-done | bytes 589856 | tf_op jit(solution)/shard_map/ppermute | solution.py:45
  63.2 0.4 collective-permute-start.29
  63.6 4.6 %slot_grad.1 = (bf16[2,384,768]{2,1,0:T(8,128)(2,1)S(1)}, bf16[2,512,768]{2,1,0:T(8,128)(2,1)S(1)}, bf16[2,48,1024]{2,1,0:T(8,128)(2,1)S(1)}, bf16[2,48,1024]{2,...) custom-call(f32[2,384,768]{2,1,0:T(8,128)S(1)} %get-tuple-element.53.own, ...), custom_call_target="tpu_custom_call" | custom-call | tf_op jit(solution)/shard_map/slot_grad/pallas_call | solution.py:360
  68.2 1.3 %collective-permute-start.28 = (bf16[2,512,768]{2,1,0:T(8,128)(2,1)S(1)}, bf16[2,512,768]{2,1,0:T(8,128)(2,1)S(1)}, u32[]{:S(2)}, u32[]{:S(2)}) collective-permute-start(bf16[2,512,768]{2,1,0:T(8,128)(2,1)S(1)} %get-tuple-element.84), channel_id=1, source_target_pairs={{0,8},{1,17},{2,10},{3,19},{4,12},{5,21},{6,14},{7,23},{8,0},{9,25... | collective-permute-start | bytes 4718600 | tf_op jit(solution)/shard_map/ppermute | solution.py:41
  69.5 0.6 collective-permute-done.17
  70.1 2.5 %collective-permute-start.23 = (bf16[2,48,1024]{2,1,0:T(8,128)(2,1)S(1)}, bf16[2,48,1024]{2,1,0:T(8,128)(2,1)S(1)}, u32[]{:S(2)}, u32[]{:S(2)}) collective-permute-start(bf16[2,48,1024]{2,1,0:T(8,128)(2,1)S(1)} %get-tuple-element.76), channel_id=1, source_target_pairs={{0,2},{1,3},{2,0},{3,1},{4,6},{5,7},{6,4},{7,5},{8,10},{9,11},{10,... | collective-permute-start | bytes 589832 | tf_op jit(solution)/shard_map/ppermute | solution.py:50
  72.6 0.5 collective-permute-start.24
  73.1 9.3 %collective-permute-done.19 = bf16[2,48,1024]{2,1,0:T(8,128)(2,1)S(1)} collective-permute-done((bf16[2,48,1024]{2,1,0:T(8,128)(2,1)S(1)}, bf16[2,48,1024]{2,1,0:T(8,128)(2,1)S(1)}, u32[]{:S(2)}, u32[]{:S(2)}) %collective-permute-start.19) | collective-permute-done | bytes 196640 | tf_op jit(solution)/shard_map/ppermute | solution.py:50
  82.7 0.9 collective-permute-start.21
  83.6 4.3 %collective-permute-done.24 = bf16[2,48,1024]{2,1,0:T(8,128)(2,1)S(1)} collective-permute-done((bf16[2,48,1024]{2,1,0:T(8,128)(2,1)S(1)}, bf16[2,48,1024]{2,1,0:T(8,128)(2,1)S(1)}, u32[]{:S(2)}, u32[]{:S(2)}) %collective-permute-start.24) | collective-permute-done | bytes 196640 | tf_op jit(solution)/shard_map/ppermute | solution.py:50
  87.9 8.4 %collective-permute-done.25 = bf16[2,48,1024]{2,1,0:T(8,128)(2,1)S(1)} collective-permute-done((bf16[2,48,1024]{2,1,0:T(8,128)(2,1)S(1)}, bf16[2,48,1024]{2,1,0:T(8,128)(2,1)S(1)}, u32[]{:S(2)}, u32[]{:S(2)}) %collective-permute-start.25) | collective-permute-done | bytes 196640 | tf_op jit(solution)/shard_map/ppermute | solution.py:50
  96.6 1.1 %collective-permute-start.22 = (bf16[2,96,1024]{2,1,0:T(8,128)(2,1)S(1)}, bf16[2,96,1024]{2,1,0:T(8,128)(2,1)S(1)}, u32[]{:S(2)}, u32[]{:S(2)}) collective-permute-start(bf16[2,96,1024]{2,1,0:T(8,128)(2,1)S(1)} %pad_maximum_fusion.4), channel_id=1, source_target_pairs={{0,1},{1,0},{2,3},{3,2},{4,5},{5,4},{6,7},{7,6},{8,9},{9,8},{10,11... | collective-permute-start | bytes 1179656 | tf_op jit(solution)/shard_map/ppermute | solution.py:50
  97.8 5.6 %collective-permute-done.26 = bf16[4,48,1024]{2,1,0:T(8,128)(2,1)S(1)} collective-permute-done((bf16[4,48,1024]{2,1,0:T(8,128)(2,1)S(1)}, bf16[4,48,1024]{2,1,0:T(8,128)(2,1)S(1)}, u32[]{:S(2)}, u32[]{:S(2)}) %collective-permute-start.26) | collective-permute-done | bytes 393248 | tf_op jit(solution)/shard_map/ppermute | solution.py:45
  103.5 1.3 %unslot.2 = bf16[128,2048]{1,0:T(8,128)(2,1)} custom-call(bf16[128,192]{1,0:T(8,128)(2,1)S(1)} %copy-done.3, f32[128,128]{1,0:T(8,128)S(1)} %copy-done.4, bf16[96,1024]{1,0:T(8,128)(2,1)S(1)} %bitcast.95, bf16[96,1024]{1,0:T(8,128)(2,1)S(1)} %bitcast.98, bf16[2,96,1024]{2,1,0:T(8,128)(2,1)S(1)} %collective-permute-done.22.other), custom_call_target="tpu_custom_call" | custom-call | flops 4000000000 | bytes 12000000 | tf_op jit(solution)/shard_map/unslot/pallas_call | solution.py:409
  104.8 1.3 %collective-permute-start.27 = (bf16[2,96,1024]{2,1,0:T(8,128)(2,1)S(1)}, bf16[2,96,1024]{2,1,0:T(8,128)(2,1)S(1)}, u32[]{:S(2)}, u32[]{:S(2)}) collective-permute-start(bf16[2,96,1024]{2,1,0:T(8,128)(2,1)S(1)} %pad_maximum_fusion.7), channel_id=1, source_target_pairs={{0,1},{1,0},{2,3},{3,2},{4,5},{5,4},{6,7},{7,6},{8,9},{9,8},{10,11... | collective-permute-start | bytes 1179656 | tf_op jit(solution)/shard_map/ppermute | solution.py:50
  106.0 1.5 %fusion.2 = bf16[1,768,512]{2,1,0:T(8,128)(2,1)} fusion(bf16[768,512]{1,0:T(8,128)(2,1)S(1)} %collective-permute-done.29, bf16[384,768]{1,0:T(8,128)(2,1)S(1)} %get-tuple-element.70, bf16[384,1024]{1,0:T(8,128)(2,1)S(1)} %get-tuple-element.63.grad_rows), kind=kOutput, calls=%fused_computation.5 | convolution fusion | flops 303169536 | bytes 2555904 | tf_op jit(solution)/shard_map/dot_general | solution.py:23
  107.5 1.3 %unslot.3 = bf16[128,2048]{1,0:T(8,128)(2,1)} custom-call(bf16[128,192]{1,0:T(8,128)(2,1)S(1)} %copy-done.3, f32[128,128]{1,0:T(8,128)S(1)} %copy-done.4, bf16[96,1024]{1,0:T(8,128)(2,1)S(1)} %bitcast.96, bf16[96,1024]{1,0:T(8,128)(2,1)S(1)} %bitcast.97, bf16[2,96,1024]{2,1,0:T(8,128)(2,1)S(1)} %collective-permute-done.27.other), custom_call_target="tpu_custom_call" | custom-call | flops 4000000000 | bytes 12000000 | tf_op jit(solution)/shard_map/unslot/pallas_call | solution.py:409
  108.8 1.5 %fusion.4 = bf16[1,512,768]{2,1,0:T(8,128)(2,1)} fusion(bf16[2,512,768]{2,1,0:T(8,128)(2,1)S(1)} %collective-permute-done.28, bf16[2,384,768]{2,1,0:T(8,128)(2,1)S(1)} %get-tuple-element.82, bf16[384,1024]{1,0:T(8,128)(2,1)S(1)} %get-tuple-element.72.rows), kind=kOutput, calls=%fused_computation.7 | convolution fusion | flops 303169536 | bytes 2555904 | tf_op jit(solution)/shard_map/dot_general | solution.py:23
  110.3 1.5 %fusion.3 = bf16[1,512,768]{2,1,0:T(8,128)(2,1)} fusion(bf16[2,512,768]{2,1,0:T(8,128)(2,1)S(1)} %collective-permute-done.28, bf16[2,384,768]{2,1,0:T(8,128)(2,1)S(1)} %get-tuple-element.82, bf16[384,1024]{1,0:T(8,128)(2,1)S(1)} %get-tuple-element.72.rows), kind=kOutput, calls=%fused_computation.6 | convolution fusion | flops 303169536 | bytes 2555904 | tf_op jit(solution)/shard_map/dot_general | solution.py:23
  (66 shorter events, 1.8 us)
Async XLA Ops:
  3.0 8.5 %collective-permute-start.12 = (bf16[2,96,1024]{2,1,0:T(8,128)(2,1)}, bf16[2,96,1024]{2,1,0:T(8,128)(2,1)S(1)}, u32[]{:S(2)}, u32[]{:S(2)}) collective-permute-start(bf16[2,96,1024]{2,1,0:T(8,128)(2,1)} %get-tuple-element.57), channel_id=1, source_target_pairs={{0,1},{1,0},{2,3},{3,2},{4,5},{5,4},{6,7},{7,6},{8,9},{9,8},{10,11... | collective-permute-start | bytes 1179656 | tf_op jit(solution)/shard_map/ppermute | solution.py:50
  3.7 12.6 %collective-permute-start.9 = (bf16[1,512,768]{2,1,0:T(8,128)(2,1)}, bf16[1,512,768]{2,1,0:T(8,128)(2,1)S(1)}, u32[]{:S(2)}, u32[]{:S(2)}) collective-permute-start(bf16[1,512,768]{2,1,0:T(8,128)(2,1)} %up.1), channel_id=1, source_target_pairs={{0,8},{1,17},{2,10},{3,19},{4,12},{5,21},{6,14},{7,23},{8,0},{9,25... | collective-permute-start | bytes 2359304 | tf_op jit(solution)/shard_map/ppermute | solution.py:41
  7.3 2.6 %collective-permute-start = (bf16[2,96,1024]{2,1,0:T(8,128)(2,1)}, bf16[2,96,1024]{2,1,0:T(8,128)(2,1)S(1)}, u32[]{:S(2)}, u32[]{:S(2)}) collective-permute-start(bf16[2,96,1024]{2,1,0:T(8,128)(2,1)} %get-tuple-element.49), channel_id=1, source_target_pairs={{0,1},{1,0},{2,3},{3,2},{4,5},{5,4},{6,7},{7,6},{8,9},{9,8},{10,11... | collective-permute-start | bytes 1179656 | tf_op jit(solution)/shard_map/ppermute | solution.py:50
  7.3 22.2 %collective-permute-start.8 = (bf16[1,512,768]{2,1,0:T(8,128)(2,1)}, bf16[1,512,768]{2,1,0:T(8,128)(2,1)S(1)}, u32[]{:S(2)}, u32[]{:S(2)}) collective-permute-start(bf16[1,512,768]{2,1,0:T(8,128)(2,1)} %gate.1), channel_id=1, source_target_pairs={{0,8},{1,17},{2,10},{3,19},{4,12},{5,21},{6,14},{7,23},{8,0},{9,25... | collective-permute-start | bytes 2359304 | tf_op jit(solution)/shard_map/ppermute | solution.py:41
  10.0 11.3 %collective-permute-start.4 = (bf16[2,96,1024]{2,1,0:T(8,128)(2,1)S(1)}, bf16[2,96,1024]{2,1,0:T(8,128)(2,1)S(1)}, u32[]{:S(2)}, u32[]{:S(2)}) collective-permute-start(bf16[2,96,1024]{2,1,0:T(8,128)(2,1)S(1)} %pad_maximum_fusion), channel_id=1, source_target_pairs={{0,16},{1,9},{2,18},{3,11},{4,20},{5,13},{6,22},{7,15},{8,24},{9,1... | collective-permute-start | bytes 1179656 | tf_op jit(solution)/shard_map/ppermute | solution.py:45
  11.3 11.2 %collective-permute-start.3 = (bf16[1,48,1024]{2,1,0:T(8,128)(2,1)S(1)}, bf16[1,48,1024]{2,1,0:T(8,128)(2,1)S(1)}, u32[]{:S(2)}, u32[]{:S(2)}) collective-permute-start(bf16[1,48,1024]{2,1,0:T(8,128)(2,1)S(1)} %bitcast.125), channel_id=1, source_target_pairs={{0,6},{1,7},{2,4},{3,5},{4,2},{5,3},{6,0},{7,1},{8,14},{9,15},{10,... | collective-permute-start | bytes 294920 | tf_op jit(solution)/shard_map/ppermute | solution.py:50
  11.5 11.2 %collective-permute-start.2 = (bf16[1,48,1024]{2,1,0:T(8,128)(2,1)S(1)}, bf16[1,48,1024]{2,1,0:T(8,128)(2,1)S(1)}, u32[]{:S(2)}, u32[]{:S(2)}) collective-permute-start(bf16[1,48,1024]{2,1,0:T(8,128)(2,1)S(1)} %bitcast.124), channel_id=1, source_target_pairs={{0,4},{1,5},{2,6},{3,7},{4,0},{5,1},{6,2},{7,3},{8,12},{9,13},{10,... | collective-permute-start | bytes 294920 | tf_op jit(solution)/shard_map/ppermute | solution.py:50
  14.8 14.7 %copy-start.2 = (bf16[1,768,512]{2,1,0:T(8,128)(2,1)S(1)}, bf16[1,768,512]{2,1,0:T(8,128)(2,1)}, u32[]{:S(2)}) copy-start(bf16[1,768,512]{2,1,0:T(8,128)(2,1)} %down.1) | copy-start | bytes 2359300
  14.8 16.2 %copy-start = (bf16[1,512,768]{2,1,0:T(8,128)(2,1)S(1)}, bf16[1,512,768]{2,1,0:T(8,128)(2,1)}, u32[]{:S(2)}) copy-start(bf16[1,512,768]{2,1,0:T(8,128)(2,1)} %gate.1) | copy-start | bytes 2359300
  14.8 16.2 %copy-start.1 = (bf16[1,512,768]{2,1,0:T(8,128)(2,1)S(1)}, bf16[1,512,768]{2,1,0:T(8,128)(2,1)}, u32[]{:S(2)}) copy-start(bf16[1,512,768]{2,1,0:T(8,128)(2,1)} %up.1) | copy-start | bytes 2359300
  16.2 9.8 %collective-permute-start.1 = (bf16[1,48,1024]{2,1,0:T(8,128)(2,1)S(1)}, bf16[1,48,1024]{2,1,0:T(8,128)(2,1)S(1)}, u32[]{:S(2)}, u32[]{:S(2)}) collective-permute-start(bf16[1,48,1024]{2,1,0:T(8,128)(2,1)S(1)} %bitcast.123), channel_id=1, source_target_pairs={{0,2},{1,3},{2,0},{3,1},{4,6},{5,7},{6,4},{7,5},{8,10},{9,11},{10,... | collective-permute-start | bytes 294920 | tf_op jit(solution)/shard_map/ppermute | solution.py:50
  21.3 12.3 %collective-permute-start.13 = (bf16[2,96,1024]{2,1,0:T(8,128)(2,1)S(1)}, bf16[2,96,1024]{2,1,0:T(8,128)(2,1)S(1)}, u32[]{:S(2)}, u32[]{:S(2)}) collective-permute-start(bf16[2,96,1024]{2,1,0:T(8,128)(2,1)S(1)} %pad_maximum_fusion.1), channel_id=1, source_target_pairs={{0,16},{1,9},{2,18},{3,11},{4,20},{5,13},{6,22},{7,15},{8,24},{9,1... | collective-permute-start | bytes 1179656 | tf_op jit(solution)/shard_map/ppermute | solution.py:45
  22.6 8.4 %collective-permute-start.7 = (bf16[1,48,1024]{2,1,0:T(8,128)(2,1)S(1)}, bf16[1,48,1024]{2,1,0:T(8,128)(2,1)S(1)}, u32[]{:S(2)}, u32[]{:S(2)}) collective-permute-start(bf16[1,48,1024]{2,1,0:T(8,128)(2,1)S(1)} %bitcast.128), channel_id=1, source_target_pairs={{0,6},{1,7},{2,4},{3,5},{4,2},{5,3},{6,0},{7,1},{8,14},{9,15},{10,... | collective-permute-start | bytes 294920 | tf_op jit(solution)/shard_map/ppermute | solution.py:50
  22.8 8.2 %collective-permute-start.6 = (bf16[1,48,1024]{2,1,0:T(8,128)(2,1)S(1)}, bf16[1,48,1024]{2,1,0:T(8,128)(2,1)S(1)}, u32[]{:S(2)}, u32[]{:S(2)}) collective-permute-start(bf16[1,48,1024]{2,1,0:T(8,128)(2,1)S(1)} %bitcast.127), channel_id=1, source_target_pairs={{0,4},{1,5},{2,6},{3,7},{4,0},{5,1},{6,2},{7,3},{8,12},{9,13},{10,... | collective-permute-start | bytes 294920 | tf_op jit(solution)/shard_map/ppermute | solution.py:50
  26.0 5.0 %collective-permute-start.5 = (bf16[1,48,1024]{2,1,0:T(8,128)(2,1)S(1)}, bf16[1,48,1024]{2,1,0:T(8,128)(2,1)S(1)}, u32[]{:S(2)}, u32[]{:S(2)}) collective-permute-start(bf16[1,48,1024]{2,1,0:T(8,128)(2,1)S(1)} %bitcast.126), channel_id=1, source_target_pairs={{0,2},{1,3},{2,0},{3,1},{4,6},{5,7},{6,4},{7,5},{8,10},{9,11},{10,... | collective-permute-start | bytes 294920 | tf_op jit(solution)/shard_map/ppermute | solution.py:50
  29.5 20.4 %collective-permute-start.11 = (bf16[1,768,512]{2,1,0:T(8,128)(2,1)S(1)}, bf16[1,768,512]{2,1,0:T(8,128)(2,1)S(1)}, u32[]{:S(2)}, u32[]{:S(2)}) collective-permute-start(bf16[1,768,512]{2,1,0:T(8,128)(2,1)S(1)} %copy-done.2), channel_id=1, source_target_pairs={{0,8},{1,17},{2,10},{3,19},{4,12},{5,21},{6,14},{7,23},{8,0},{9,25... | collective-permute-start | bytes 2359304 | tf_op jit(solution)/shard_map/ppermute | solution.py:41
  33.4 23.2 %collective-permute-start.10 = (bf16[2,384,768]{2,1,0:T(8,128)(2,1)S(1)}, bf16[2,384,768]{2,1,0:T(8,128)(2,1)S(1)}, u32[]{:S(2)}, u32[]{:S(2)}) collective-permute-start(bf16[2,384,768]{2,1,0:T(8,128)(2,1)S(1)} %get-tuple-element.54), channel_id=1, source_target_pairs={{0,16},{1,9},{2,18},{3,11},{4,20},{5,13},{6,22},{7,15},{8,24},{9,1... | collective-permute-start | bytes 3538952 | tf_op jit(solution)/shard_map/ppermute | solution.py:45
  33.6 9.5 %collective-permute-start.16 = (bf16[2,48,1024]{2,1,0:T(8,128)(2,1)S(1)}, bf16[2,48,1024]{2,1,0:T(8,128)(2,1)S(1)}, u32[]{:S(2)}, u32[]{:S(2)}) collective-permute-start(bf16[2,48,1024]{2,1,0:T(8,128)(2,1)S(1)} %pad_maximum_fusion.11), channel_id=1, source_target_pairs={{0,6},{1,7},{2,4},{3,5},{4,2},{5,3},{6,0},{7,1},{8,14},{9,15},{10,... | collective-permute-start | bytes 589832 | tf_op jit(solution)/shard_map/ppermute | solution.py:50
  34.6 15.0 %collective-permute-start.15 = (bf16[2,48,1024]{2,1,0:T(8,128)(2,1)S(1)}, bf16[2,48,1024]{2,1,0:T(8,128)(2,1)S(1)}, u32[]{:S(2)}, u32[]{:S(2)}) collective-permute-start(bf16[2,48,1024]{2,1,0:T(8,128)(2,1)S(1)} %pad_maximum_fusion.10), channel_id=1, source_target_pairs={{0,4},{1,5},{2,6},{3,7},{4,0},{5,1},{6,2},{7,3},{8,12},{9,13},{10,... | collective-permute-start | bytes 589832 | tf_op jit(solution)/shard_map/ppermute | solution.py:50
  37.1 12.8 %collective-permute-start.14 = (bf16[2,48,1024]{2,1,0:T(8,128)(2,1)S(1)}, bf16[2,48,1024]{2,1,0:T(8,128)(2,1)S(1)}, u32[]{:S(2)}, u32[]{:S(2)}) collective-permute-start(bf16[2,48,1024]{2,1,0:T(8,128)(2,1)S(1)} %pad_maximum_fusion.9), channel_id=1, source_target_pairs={{0,2},{1,3},{2,0},{3,1},{4,6},{5,7},{6,4},{7,5},{8,10},{9,11},{10,... | collective-permute-start | bytes 589832 | tf_op jit(solution)/shard_map/ppermute | solution.py:50
  51.3 11.9 %collective-permute-start.20 = (bf16[384,768]{1,0:T(8,128)(2,1)S(1)}, bf16[384,768]{1,0:T(8,128)(2,1)S(1)}, u32[]{:S(2)}, u32[]{:S(2)}) collective-permute-start(bf16[384,768]{1,0:T(8,128)(2,1)S(1)} %get-tuple-element.69), channel_id=1, source_target_pairs={{0,16},{1,9},{2,18},{3,11},{4,20},{5,13},{6,22},{7,15},{8,24},{9,1... | collective-permute-start | bytes 1769480 | tf_op jit(solution)/shard_map/ppermute | solution.py:45
  58.9 9.3 %collective-permute-start.18 = (bf16[2,48,1024]{2,1,0:T(8,128)(2,1)S(1)}, bf16[2,48,1024]{2,1,0:T(8,128)(2,1)S(1)}, u32[]{:S(2)}, u32[]{:S(2)}) collective-permute-start(bf16[2,48,1024]{2,1,0:T(8,128)(2,1)S(1)} %get-tuple-element.66), channel_id=1, source_target_pairs={{0,4},{1,5},{2,6},{3,7},{4,0},{5,1},{6,2},{7,3},{8,12},{9,13},{10,... | collective-permute-start | bytes 589832 | tf_op jit(solution)/shard_map/ppermute | solution.py:50
  59.1 11.0 %collective-permute-start.17 = (bf16[2,48,1024]{2,1,0:T(8,128)(2,1)S(1)}, bf16[2,48,1024]{2,1,0:T(8,128)(2,1)S(1)}, u32[]{:S(2)}, u32[]{:S(2)}) collective-permute-start(bf16[2,48,1024]{2,1,0:T(8,128)(2,1)S(1)} %get-tuple-element.65), channel_id=1, source_target_pairs={{0,2},{1,3},{2,0},{3,1},{4,6},{5,7},{6,4},{7,5},{8,10},{9,11},{10,... | collective-permute-start | bytes 589832 | tf_op jit(solution)/shard_map/ppermute | solution.py:50
  60.4 22.0 %collective-permute-start.19 = (bf16[2,48,1024]{2,1,0:T(8,128)(2,1)S(1)}, bf16[2,48,1024]{2,1,0:T(8,128)(2,1)S(1)}, u32[]{:S(2)}, u32[]{:S(2)}) collective-permute-start(bf16[2,48,1024]{2,1,0:T(8,128)(2,1)S(1)} %get-tuple-element.67), channel_id=1, source_target_pairs={{0,6},{1,7},{2,4},{3,5},{4,2},{5,3},{6,0},{7,1},{8,14},{9,15},{10,... | collective-permute-start | bytes 589832 | tf_op jit(solution)/shard_map/ppermute | solution.py:50
  63.2 42.9 %collective-permute-start.29 = (bf16[768,512]{1,0:T(8,128)(2,1)S(1)}, bf16[768,512]{1,0:T(8,128)(2,1)S(1)}, u32[]{:S(2)}, u32[]{:S(2)}) collective-permute-start(bf16[768,512]{1,0:T(8,128)(2,1)S(1)} %get-tuple-element.86), channel_id=1, source_target_pairs={{0,8},{1,17},{2,10},{3,19},{4,12},{5,21},{6,14},{7,23},{8,0},{9,25... | collective-permute-start | bytes 2359304 | tf_op jit(solution)/shard_map/ppermute | solution.py:41
  68.2 40.5 %collective-permute-start.28 = (bf16[2,512,768]{2,1,0:T(8,128)(2,1)S(1)}, bf16[2,512,768]{2,1,0:T(8,128)(2,1)S(1)}, u32[]{:S(2)}, u32[]{:S(2)}) collective-permute-start(bf16[2,512,768]{2,1,0:T(8,128)(2,1)S(1)} %get-tuple-element.84), channel_id=1, source_target_pairs={{0,8},{1,17},{2,10},{3,19},{4,12},{5,21},{6,14},{7,23},{8,0},{9,25... | collective-permute-start | bytes 4718600 | tf_op jit(solution)/shard_map/ppermute | solution.py:41
  70.1 12.6 %collective-permute-start.23 = (bf16[2,48,1024]{2,1,0:T(8,128)(2,1)S(1)}, bf16[2,48,1024]{2,1,0:T(8,128)(2,1)S(1)}, u32[]{:S(2)}, u32[]{:S(2)}) collective-permute-start(bf16[2,48,1024]{2,1,0:T(8,128)(2,1)S(1)} %get-tuple-element.76), channel_id=1, source_target_pairs={{0,2},{1,3},{2,0},{3,1},{4,6},{5,7},{6,4},{7,5},{8,10},{9,11},{10,... | collective-permute-start | bytes 589832 | tf_op jit(solution)/shard_map/ppermute | solution.py:50
  72.6 15.3 %collective-permute-start.24 = (bf16[2,48,1024]{2,1,0:T(8,128)(2,1)S(1)}, bf16[2,48,1024]{2,1,0:T(8,128)(2,1)S(1)}, u32[]{:S(2)}, u32[]{:S(2)}) collective-permute-start(bf16[2,48,1024]{2,1,0:T(8,128)(2,1)S(1)} %get-tuple-element.78), channel_id=1, source_target_pairs={{0,4},{1,5},{2,6},{3,7},{4,0},{5,1},{6,2},{7,3},{8,12},{9,13},{10,... | collective-permute-start | bytes 589832 | tf_op jit(solution)/shard_map/ppermute | solution.py:50
  82.5 13.9 %collective-permute-start.25 = (bf16[2,48,1024]{2,1,0:T(8,128)(2,1)S(1)}, bf16[2,48,1024]{2,1,0:T(8,128)(2,1)S(1)}, u32[]{:S(2)}, u32[]{:S(2)}) collective-permute-start(bf16[2,48,1024]{2,1,0:T(8,128)(2,1)S(1)} %get-tuple-element.80), channel_id=1, source_target_pairs={{0,6},{1,7},{2,4},{3,5},{4,2},{5,3},{6,0},{7,1},{8,14},{9,15},{10,... | collective-permute-start | bytes 589832 | tf_op jit(solution)/shard_map/ppermute | solution.py:50
  82.7 13.9 %collective-permute-start.21 = (bf16[4,48,1024]{2,1,0:T(8,128)(2,1)S(1)}, bf16[4,48,1024]{2,1,0:T(8,128)(2,1)S(1)}, u32[]{:S(2)}, u32[]{:S(2)}) collective-permute-start(bf16[4,48,1024]{2,1,0:T(8,128)(2,1)S(1)} %get-tuple-element.74), channel_id=1, source_target_pairs={{0,16},{1,9},{2,18},{3,11},{4,20},{5,13},{6,22},{7,15},{8,24},{9,1... | collective-permute-start | bytes 1179656 | tf_op jit(solution)/shard_map/ppermute | solution.py:45
  96.4 7.0 %collective-permute-start.26 = (bf16[4,48,1024]{2,1,0:T(8,128)(2,1)S(1)}, bf16[4,48,1024]{2,1,0:T(8,128)(2,1)S(1)}, u32[]{:S(2)}, u32[]{:S(2)}) collective-permute-start(bf16[4,48,1024]{2,1,0:T(8,128)(2,1)S(1)} %pad_maximum_fusion.6), channel_id=1, source_target_pairs={{0,16},{1,9},{2,18},{3,11},{4,20},{5,13},{6,22},{7,15},{8,24},{9,1... | collective-permute-start | bytes 1179656 | tf_op jit(solution)/shard_map/ppermute | solution.py:45
  96.6 6.9 %copy-start.3 = (bf16[128,192]{1,0:T(8,128)(2,1)S(1)}, bf16[128,192]{1,0:T(8,128)(2,1)}, u32[]{:S(2)}) copy-start(bf16[128,192]{1,0:T(8,128)(2,1)} %get-tuple-element.46.pick) | copy-start | bytes 147460
  96.6 6.9 %copy-start.4 = (f32[128,128]{1,0:T(8,128)S(1)}, f32[128,128]{1,0:T(8,128)}, u32[]{:S(2)}) copy-start(f32[128,128]{1,0:T(8,128)} %get-tuple-element.47.weight) | copy-start | bytes 196612
  96.6 6.8 %collective-permute-start.22 = (bf16[2,96,1024]{2,1,0:T(8,128)(2,1)S(1)}, bf16[2,96,1024]{2,1,0:T(8,128)(2,1)S(1)}, u32[]{:S(2)}, u32[]{:S(2)}) collective-permute-start(bf16[2,96,1024]{2,1,0:T(8,128)(2,1)S(1)} %pad_maximum_fusion.4), channel_id=1, source_target_pairs={{0,1},{1,0},{2,3},{3,2},{4,5},{5,4},{6,7},{7,6},{8,9},{9,8},{10,11... | collective-permute-start | bytes 1179656 | tf_op jit(solution)/shard_map/ppermute | solution.py:50
  104.8 2.7 %collective-permute-start.27 = (bf16[2,96,1024]{2,1,0:T(8,128)(2,1)S(1)}, bf16[2,96,1024]{2,1,0:T(8,128)(2,1)S(1)}, u32[]{:S(2)}, u32[]{:S(2)}) collective-permute-start(bf16[2,96,1024]{2,1,0:T(8,128)(2,1)S(1)} %pad_maximum_fusion.7), channel_id=1, source_target_pairs={{0,1},{1,0},{2,3},{3,2},{4,5},{5,4},{6,7},{7,6},{8,9},{9,8},{10,11... | collective-permute-start | bytes 1179656 | tf_op jit(solution)/shard_map/ppermute | solution.py:50
